TPU v7x, 32 devices: a whole 2x2x4 slice. The times are simulated.
32 devices in a mesh: gx: 8 (over y, x, core), gy: 4 (over z).
Axes of the slice: x: 2, y: 2, z: 4, core: 2. Of those that a mesh axis runs over, the one named last changes fastest.
Arguments:
- coords: float32 [3, 8, 4, 128], P(None, 'gx', 'gy'), may hold values from 0 to 5
- atom_types: int32 [8, 4, 128], P('gx', 'gy'), may hold values 0 or 1
- neighbours: int32 [8, 4, 128, 128], P('gx', 'gy'), may hold values from 0 to 383
- send_x: int32 [8, 4, 2, 64], P('gx', 'gy'), may hold values from 0 to 127
- send_y: int32 [8, 4, 2, 64], P('gx', 'gy'), may hold values from 0 to 255
- poly_table: float32 [2, 6, 64], replicated, may hold values from -4 to 4
- fit_in: float32 [512, 128], replicated, may hold values from -0.25 to 0.25
- fit_hidden: float32 [2, 128, 128], replicated, may hold values from -0.5 to 0.5
- fit_bias: float32 [3, 128], replicated, may hold values from -3 to 3
- fit_out: float32 [128], replicated, may hold values from -0.5 to 0.5
- spectrum: float32 [2], replicated, may hold values from -0.02 to 0.1, as said below
- cheb_prev: float32 [4, 3, 8, 4, 128], P(None, None, 'gx', 'gy'), may hold values from -540 to 540
- cheb_cur: float32 [4, 3, 8, 4, 128], P(None, None, 'gx', 'gy'), may hold values from -540 to 540
Outputs:
- forces: float32 [3, 8, 4, 128], P(None, 'gx', 'gy')
- cheb_next: float32 [4, 3, 8, 4, 128], P(None, None, 'gx', 'gy')
- moments: float32 [2, 4], replicated
Inputs may be any that keep to these rules, and one draw needn't show every extreme that they name: spectrum[0] lies in [-0.02, -0.01] and spectrum[1] in [0.05, 0.1].
All inputs are finite; a program needn't handle non-finite values. No bound on the sum of `atom_types` on one device may be relied on, other than what follows from the above.
Results may differ from a plain program's by a relative error of at most 0.00029.
Values sent between devices are 32-bit elements; how exact they have to be, the bound alone decides.
No kernel may reach another device: no remote copies, remote signals or barrier semaphores. Data moves between devices by JAX's collectives and lax.ppermute only.
A program may use at most 64 MiB of HBM per device.

v0:
```python
import jax
import jax.numpy as jnp
from jax import lax
from jax.sharding import PartitionSpec as P

M2 = 8
ATOM_BLOCK = 32


BRICK = 5.0
SOFTENING = 0.25
CUTOFF_SQ = 16.0
HIGHEST = lax.Precision.HIGHEST


def with_halo(x, sides, width):
    for axis, dim in sides:
        devices, length = (lax.axis_size(axis), x.shape[dim])
        up = [(i, (i + 1) % devices) for i in range(devices)]
        down = [(j, i) for i, j in up]
        last = lax.slice_in_dim(x, length - width, length, axis=dim)
        leading = lax.slice_in_dim(x, 0, width, axis=dim)
        before = lax.ppermute(last, axis, up)
        after = lax.ppermute(leading, axis, down)
        x = jnp.concatenate([before, x, after], axis=dim)
    return x


def site_energy(offsets, near_kind, poly_table, fit_in, fit_hidden, fit_bias, fit_out):
    radius_sq = jnp.sum(offsets * offsets, axis=0)
    soft_radius = jnp.sqrt(radius_sq + SOFTENING)
    switch = 1.0 / (1.0 + radius_sq / CUTOFF_SQ)
    environ = jnp.concatenate([switch[None], switch[None] * offsets / soft_radius[None]], axis=0)
    powers = jnp.stack([switch**degree for degree in range(poly_table.shape[1])], axis=0)
    silicon = jnp.einsum("kbs,km->mbs", powers, poly_table[0], precision=HIGHEST)
    hydrogen = jnp.einsum("kbs,km->mbs", powers, poly_table[1] - poly_table[0], precision=HIGHEST)
    embedded = silicon + near_kind[None] * hydrogen
    contracted = jnp.einsum("cbs,mbs->cmb", environ, embedded, precision=HIGHEST) / offsets.shape[2]
    descriptor = jnp.einsum("cmb,cnb->mnb", contracted, contracted[:, :M2], precision=HIGHEST)
    descriptor = descriptor.reshape(-1, offsets.shape[1])
    hidden_layer = jnp.tanh(jnp.dot(fit_in.T, descriptor, precision=HIGHEST) + fit_bias[0][:, None])
    hidden_layer = (
        jnp.tanh(jnp.dot(fit_hidden[0].T, hidden_layer, precision=HIGHEST) + fit_bias[1][:, None])
        + hidden_layer
    )
    hidden_layer = (
        jnp.tanh(jnp.dot(fit_hidden[1].T, hidden_layer, precision=HIGHEST) + fit_bias[2][:, None])
        + hidden_layer
    )
    return jnp.sum(jnp.dot(fit_out, hidden_layer, precision=HIGHEST))


def block_terms(ghosted, slot_rows, first_atom, params):
    block_atoms = slot_rows.shape[0]
    centre = lax.dynamic_slice_in_dim(ghosted, first_atom, block_atoms, 1)
    picked = jnp.take(ghosted, slot_rows.reshape(-1), axis=1).reshape(
        ghosted.shape[0], block_atoms, -1
    )
    offsets = picked[0:3] - centre[0:3, :, None]
    near_kind = picked[3]
    tangents = (picked[4:16] - centre[4:16, :, None]).reshape(4, 3, block_atoms, -1)

    def energy_of(moved):
        return site_energy(moved, near_kind, *params)

    gradient, linear = jax.vjp(jax.grad(energy_of), offsets)
    curvature = jax.vmap(lambda vector: linear(vector)[0])(tangents)
    return jnp.concatenate([gradient, curvature.reshape(12, block_atoms, -1)], axis=0)


def brick_sum(ghosted, near_lists, params):
    block_size = ATOM_BLOCK

    def advance(accumulated, number):
        first_atom = number * block_size
        slot_rows = lax.dynamic_slice_in_dim(near_lists, first_atom, block_size, 0)
        terms = block_terms(ghosted, slot_rows, first_atom, params)
        accumulated = accumulated.at[:, slot_rows.reshape(-1)].add(terms.reshape(15, -1))
        centre_sum = lax.dynamic_slice_in_dim(accumulated, first_atom, block_size, 1) - jnp.sum(
            terms, axis=2
        )
        accumulated = lax.dynamic_update_slice_in_dim(accumulated, centre_sum, first_atom, 1)
        return (accumulated, None)

    start_sum = jnp.zeros((15, ghosted.shape[1]), jnp.float32)
    blocks = jnp.arange(near_lists.shape[0] // block_size, dtype=jnp.int32)
    accumulated, unused = lax.scan(advance, start_sum, blocks)
    return accumulated


def outgoing(field, lists):
    return jnp.stack([field[:, lists[0]], field[:, lists[1]]], axis=0)


def returned(accumulated, lists, lower_terms, upper_terms):
    return accumulated.at[:, lists[0]].add(lower_terms).at[:, lists[1]].add(upper_terms)


def local(
    coords,
    atom_types,
    neighbours,
    send_x,
    send_y,
    poly_table,
    fit_in,
    fit_hidden,
    fit_bias,
    fit_out,
    spectrum,
    cheb_prev,
    cheb_cur,
):
    own_atoms = coords.shape[3]
    entries = 3.0 * own_atoms * lax.axis_size("gx") * lax.axis_size("gy")
    current = cheb_cur[:, :, 0, 0]
    kind = atom_types[0, 0].astype(jnp.float32)
    light = 1.008 ** (-0.5)
    heavy = 28.0855 ** (-0.5)
    scale = heavy + kind * (light - heavy)
    lent = (current * scale[None, None]).reshape(12, own_atoms)
    places = jnp.concatenate([coords[:, 0, 0], kind[None]], axis=0)
    lists_x = send_x[0, 0]
    lists_y = send_y[0, 0]
    field = jnp.concatenate([places, lent], axis=0)
    padded = with_halo(outgoing(field, lists_x), (("gx", 0),), 1)
    first = jnp.concatenate(
        [field, padded[0].at[0].add(-BRICK), padded[3].at[0].add(BRICK)], axis=1
    )
    padded = with_halo(outgoing(first, lists_y), (("gy", 0),), 1)
    ghosted = jnp.concatenate(
        [first, padded[0].at[1].add(-BRICK), padded[3].at[1].add(BRICK)], axis=1
    )
    params = (poly_table, fit_in, fit_hidden, fit_bias, fit_out)
    accumulated = brick_sum(ghosted, neighbours[0, 0], params)
    ghost_x = lists_x.shape[1]
    ghost_y = lists_y.shape[1]
    split = own_atoms + 2 * ghost_x
    stacked_rows = jnp.stack(
        [accumulated[:, split : split + ghost_y], accumulated[:, split + ghost_y :]], axis=0
    )
    padded = with_halo(stacked_rows, (("gy", 0),), 1)
    returned_y = returned(accumulated[:, :split], lists_y, padded[0], padded[3])
    stacked_rows = jnp.stack(
        [returned_y[:, own_atoms : own_atoms + ghost_x], returned_y[:, own_atoms + ghost_x :]],
        axis=0,
    )
    padded = with_halo(stacked_rows, (("gx", 0),), 1)
    own = returned(returned_y[:, :own_atoms], lists_x, padded[0], padded[3])
    forces = -own[0:3]
    curvature = own[3:15].reshape(4, 3, own_atoms)
    center = (spectrum[0] + spectrum[1]) / 2.0
    half_width = (spectrum[1] - spectrum[0]) / 2.0
    following = (
        2.0 * (scale[None, None] * curvature - center * current) / half_width
        - cheb_prev[:, :, 0, 0]
    )
    cross_part = jnp.sum(following * current, axis=(1, 2)) / entries
    norm_part = jnp.sum(current * current, axis=(1, 2)) / entries
    moments = lax.psum(jnp.stack([norm_part, cross_part], axis=0), ("gx", "gy"))
    return (forces[:, None, None], following[:, :, None, None], moments)


def solution(mesh):
    return jax.shard_map(
        local,
        mesh=mesh,
        in_specs=(
            P(None, "gx", "gy", None),
            P("gx", "gy", None),
            P("gx", "gy", None, None),
            P("gx", "gy", None, None),
            P("gx", "gy", None, None),
            P(),
            P(),
            P(),
            P(),
            P(),
            P(),
            P(None, None, "gx", "gy", None),
            P(None, None, "gx", "gy", None),
        ),
        out_specs=(P(None, "gx", "gy", None), P(None, None, "gx", "gy", None), P()),
        check_vma=False,
    )
```

profile of v0, /device:TPU:0, one launch (start us, length us, event | category | flops | bytes accessed | tf_op | source)
XLA Modules:
  0.0 603.3 jit_solution(16101563904620397851)
XLA Ops:
  6.0 2.9 collective-permute-start.1
  21.4 523.4 %while.17 = (s32[]{:T(128)}, f32[15,384]{0,1:T(8,128)S(1)}, s32[4]{0:T(128)}, s32[128,128]{1,0:T(8,128)}, f32[16,384]{0,1:T(8,128)S(1)}, /*index=5*/f32[128]{0:T...) while((s32[]{:T(128)}, f32[15,384]{0,1:T(8,128)S(1)}, ...), condition=%wide.region_12.13_spmd, body=%wide.region_0.12_spmd.sunk | while | flops 1125830656 | bytes 133411096 | solution.py:87
  24.4 10.8 %gather_fusion = f32[4096,16]{1,0:T(8,128)S(1)} fusion(f32[16,384]{0,1:T(8,128)S(1)} %get-tuple-element.642, s32[4096]{0:T(1024)S(1)} %broadcast_clamp_fusion.2), kind=kCustom, calls=%fused_computation.clone.1 | custom fusion | bytes 540672 | tf_op jit(solution)/shard_map/while/body/eval_jaxpr/jit(_take)/gather | solution.py:56
  60.2 4.2 fusion.440
  64.4 4.5 add_bitcast_fusion.3
  70.9 9.8 %fusion.441 = f32[32,4,64,4]{2,3,1,0:T(4,128)S(1)} fusion(f32[4,32,64,128]{3,2,1,0:T(8,128)S(1)} %add_bitcast_fusion.3, f32[4,32,128,1]{2,1,0,3:T(8,128)S(1)} %get-tuple-element.572), kind=kOutput, calls=%fused_computation.16.clone.1 | convolution fusion | flops 50331648 | bytes 4390912 | tf_op jit(solution)/shard_map/while/body/eval_jaxpr/vmap(transpose(jvp(transpose(jvp(cbs,mbs->cmb)))))/dot_general | solution.py:38
  97.9 7.0 %fusion.447 = f32[4,4,8,32]{2,1,0,3:T(4,128)S(1)} fusion(f32[4,4,8,32]{2,1,0,3:T(4,128)S(1)} %convolution_bitcast_fusion.32, f32[4,32,8,64]{3,2,0,1:T(8,128)S(1)} %copy.531, f32[32,64,4]{1,2,0:T(4,128)S(1)} %convolution_multiply_fusion.4), kind=kOutput, calls=%fused_computation.28.clone.1 | convolution fusion | flops 3149824 | bytes 327680 | tf_op jit(solution)/shard_map/while/body/eval_jaxpr/vmap(transpose(jvp(jvp(cmb,cnb->mnb))))/dot_general | solution.py:39
  106.7 2.5 fusion.450
  109.4 3.5 fusion.451
  112.9 6.8 %broadcast_multiply_fusion.20 = (f32[4,64,32,128]{3,1,0,2:T(8,128)S(1)}, f32[4,64,32,128]{3,1,0,2:T(8,128)S(1)}) fusion(f32[32,128]{1,0:T(8,128)S(1)} %bitcast.866, f32[4,32,64,4]{2,3,0,1:T(4,128)S(1)} %fusion.448, f32[4,32,128,1]{2,1,0,3:T(8,128)S(1)} %copy-done.24, f32[32,4,128,64]{2,3,1,0:T(8,128)S(1)} %fusion.451), kind=kOutput, calls=%fused_computation.20.clone.1 | convolution fusion | flops 52428800 | bytes 12795904 | tf_op jit(solution)/shard_map/while/body/eval_jaxpr/vmap(transpose(jvp(jvp(cbs,mbs->cmb))))/dot_general | solution.py:38
  119.7 3.4 fusion.452
  123.4 3.1 fusion.453
  129.1 22.5 %scatter_fusion = f32[15,384]{0,1:T(8,128)S(1)} fusion(f32[15,384]{0,1:T(8,128)S(1)} %get-tuple-element.621, s32[4096]{0:T(1024)S(1)} %bitcast.873, f32[4096,15]{1,0:T(8,128)S(1)} %copy.535), kind=kCustom, calls=%fused_computation.5.clone.1 | custom fusion | flops 61440 | bytes 753664 | tf_op jit(solution)/shard_map/while/body/eval_jaxpr/scatter-add | solution.py:78
  154.6 10.8 %gather_fusion = f32[4096,16]{1,0:T(8,128)S(1)} fusion(f32[16,384]{0,1:T(8,128)S(1)} %get-tuple-element.642, s32[4096]{0:T(1024)S(1)} %broadcast_clamp_fusion.2), kind=kCustom, calls=%fused_computation.clone.1 | custom fusion | bytes 540672 | tf_op jit(solution)/shard_map/while/body/eval_jaxpr/jit(_take)/gather | solution.py:56
  190.3 4.2 fusion.440
  194.5 4.5 add_bitcast_fusion.3
  201.0 9.8 %fusion.441 = f32[32,4,64,4]{2,3,1,0:T(4,128)S(1)} fusion(f32[4,32,64,128]{3,2,1,0:T(8,128)S(1)} %add_bitcast_fusion.3, f32[4,32,128,1]{2,1,0,3:T(8,128)S(1)} %get-tuple-element.572), kind=kOutput, calls=%fused_computation.16.clone.1 | convolution fusion | flops 50331648 | bytes 4390912 | tf_op jit(solution)/shard_map/while/body/eval_jaxpr/vmap(transpose(jvp(transpose(jvp(cbs,mbs->cmb)))))/dot_general | solution.py:38
  228.0 7.0 %fusion.447 = f32[4,4,8,32]{2,1,0,3:T(4,128)S(1)} fusion(f32[4,4,8,32]{2,1,0,3:T(4,128)S(1)} %convolution_bitcast_fusion.32, f32[4,32,8,64]{3,2,0,1:T(8,128)S(1)} %copy.531, f32[32,64,4]{1,2,0:T(4,128)S(1)} %convolution_multiply_fusion.4), kind=kOutput, calls=%fused_computation.28.clone.1 | convolution fusion | flops 3149824 | bytes 327680 | tf_op jit(solution)/shard_map/while/body/eval_jaxpr/vmap(transpose(jvp(jvp(cmb,cnb->mnb))))/dot_general | solution.py:39
  236.8 2.5 fusion.450
  239.5 3.5 fusion.451
  243.0 6.8 %broadcast_multiply_fusion.20 = (f32[4,64,32,128]{3,1,0,2:T(8,128)S(1)}, f32[4,64,32,128]{3,1,0,2:T(8,128)S(1)}) fusion(f32[32,128]{1,0:T(8,128)S(1)} %bitcast.866, f32[4,32,64,4]{2,3,0,1:T(4,128)S(1)} %fusion.448, f32[4,32,128,1]{2,1,0,3:T(8,128)S(1)} %copy-done.24, f32[32,4,128,64]{2,3,1,0:T(8,128)S(1)} %fusion.451), kind=kOutput, calls=%fused_computation.20.clone.1 | convolution fusion | flops 52428800 | bytes 12795904 | tf_op jit(solution)/shard_map/while/body/eval_jaxpr/vmap(transpose(jvp(jvp(cbs,mbs->cmb))))/dot_general | solution.py:38
  249.8 3.4 fusion.452
  253.5 3.1 fusion.453
  259.2 22.5 %scatter_fusion = f32[15,384]{0,1:T(8,128)S(1)} fusion(f32[15,384]{0,1:T(8,128)S(1)} %get-tuple-element.621, s32[4096]{0:T(1024)S(1)} %bitcast.873, f32[4096,15]{1,0:T(8,128)S(1)} %copy.535), kind=kCustom, calls=%fused_computation.5.clone.1 | custom fusion | flops 61440 | bytes 753664 | tf_op jit(solution)/shard_map/while/body/eval_jaxpr/scatter-add | solution.py:78
  284.7 10.8 %gather_fusion = f32[4096,16]{1,0:T(8,128)S(1)} fusion(f32[16,384]{0,1:T(8,128)S(1)} %get-tuple-element.642, s32[4096]{0:T(1024)S(1)} %broadcast_clamp_fusion.2), kind=kCustom, calls=%fused_computation.clone.1 | custom fusion | bytes 540672 | tf_op jit(solution)/shard_map/while/body/eval_jaxpr/jit(_take)/gather | solution.py:56
  320.4 4.2 fusion.440
  324.6 4.4 add_bitcast_fusion.3
  331.0 9.8 %fusion.441 = f32[32,4,64,4]{2,3,1,0:T(4,128)S(1)} fusion(f32[4,32,64,128]{3,2,1,0:T(8,128)S(1)} %add_bitcast_fusion.3, f32[4,32,128,1]{2,1,0,3:T(8,128)S(1)} %get-tuple-element.572), kind=kOutput, calls=%fused_computation.16.clone.1 | convolution fusion | flops 50331648 | bytes 4390912 | tf_op jit(solution)/shard_map/while/body/eval_jaxpr/vmap(transpose(jvp(transpose(jvp(cbs,mbs->cmb)))))/dot_general | solution.py:38
  358.1 7.0 %fusion.447 = f32[4,4,8,32]{2,1,0,3:T(4,128)S(1)} fusion(f32[4,4,8,32]{2,1,0,3:T(4,128)S(1)} %convolution_bitcast_fusion.32, f32[4,32,8,64]{3,2,0,1:T(8,128)S(1)} %copy.531, f32[32,64,4]{1,2,0:T(4,128)S(1)} %convolution_multiply_fusion.4), kind=kOutput, calls=%fused_computation.28.clone.1 | convolution fusion | flops 3149824 | bytes 327680 | tf_op jit(solution)/shard_map/while/body/eval_jaxpr/vmap(transpose(jvp(jvp(cmb,cnb->mnb))))/dot_general | solution.py:39
  366.9 2.5 fusion.450
  369.6 3.5 fusion.451
  373.1 6.8 %broadcast_multiply_fusion.20 = (f32[4,64,32,128]{3,1,0,2:T(8,128)S(1)}, f32[4,64,32,128]{3,1,0,2:T(8,128)S(1)}) fusion(f32[32,128]{1,0:T(8,128)S(1)} %bitcast.866, f32[4,32,64,4]{2,3,0,1:T(4,128)S(1)} %fusion.448, f32[4,32,128,1]{2,1,0,3:T(8,128)S(1)} %copy-done.24, f32[32,4,128,64]{2,3,1,0:T(8,128)S(1)} %fusion.451), kind=kOutput, calls=%fused_computation.20.clone.1 | convolution fusion | flops 52428800 | bytes 12795904 | tf_op jit(solution)/shard_map/while/body/eval_jaxpr/vmap(transpose(jvp(jvp(cbs,mbs->cmb))))/dot_general | solution.py:38
  379.9 3.4 fusion.452
  383.5 3.1 fusion.453
  389.2 22.5 %scatter_fusion = f32[15,384]{0,1:T(8,128)S(1)} fusion(f32[15,384]{0,1:T(8,128)S(1)} %get-tuple-element.621, s32[4096]{0:T(1024)S(1)} %bitcast.873, f32[4096,15]{1,0:T(8,128)S(1)} %copy.535), kind=kCustom, calls=%fused_computation.5.clone.1 | custom fusion | flops 61440 | bytes 753664 | tf_op jit(solution)/shard_map/while/body/eval_jaxpr/scatter-add | solution.py:78
  414.8 10.8 %gather_fusion = f32[4096,16]{1,0:T(8,128)S(1)} fusion(f32[16,384]{0,1:T(8,128)S(1)} %get-tuple-element.642, s32[4096]{0:T(1024)S(1)} %broadcast_clamp_fusion.2), kind=kCustom, calls=%fused_computation.clone.1 | custom fusion | bytes 540672 | tf_op jit(solution)/shard_map/while/body/eval_jaxpr/jit(_take)/gather | solution.py:56
  450.5 4.2 fusion.440
  454.7 4.5 add_bitcast_fusion.3
  461.1 9.8 %fusion.441 = f32[32,4,64,4]{2,3,1,0:T(4,128)S(1)} fusion(f32[4,32,64,128]{3,2,1,0:T(8,128)S(1)} %add_bitcast_fusion.3, f32[4,32,128,1]{2,1,0,3:T(8,128)S(1)} %get-tuple-element.572), kind=kOutput, calls=%fused_computation.16.clone.1 | convolution fusion | flops 50331648 | bytes 4390912 | tf_op jit(solution)/shard_map/while/body/eval_jaxpr/vmap(transpose(jvp(transpose(jvp(cbs,mbs->cmb)))))/dot_general | solution.py:38
  488.2 7.0 %fusion.447 = f32[4,4,8,32]{2,1,0,3:T(4,128)S(1)} fusion(f32[4,4,8,32]{2,1,0,3:T(4,128)S(1)} %convolution_bitcast_fusion.32, f32[4,32,8,64]{3,2,0,1:T(8,128)S(1)} %copy.531, f32[32,64,4]{1,2,0:T(4,128)S(1)} %convolution_multiply_fusion.4), kind=kOutput, calls=%fused_computation.28.clone.1 | convolution fusion | flops 3149824 | bytes 327680 | tf_op jit(solution)/shard_map/while/body/eval_jaxpr/vmap(transpose(jvp(jvp(cmb,cnb->mnb))))/dot_general | solution.py:39
  497.0 2.5 fusion.450
  499.6 3.5 fusion.451
  503.2 6.8 %broadcast_multiply_fusion.20 = (f32[4,64,32,128]{3,1,0,2:T(8,128)S(1)}, f32[4,64,32,128]{3,1,0,2:T(8,128)S(1)}) fusion(f32[32,128]{1,0:T(8,128)S(1)} %bitcast.866, f32[4,32,64,4]{2,3,0,1:T(4,128)S(1)} %fusion.448, f32[4,32,128,1]{2,1,0,3:T(8,128)S(1)} %copy-done.24, f32[32,4,128,64]{2,3,1,0:T(8,128)S(1)} %fusion.451), kind=kOutput, calls=%fused_computation.20.clone.1 | convolution fusion | flops 52428800 | bytes 12795904 | tf_op jit(solution)/shard_map/while/body/eval_jaxpr/vmap(transpose(jvp(jvp(cbs,mbs->cmb))))/dot_general | solution.py:38
  510.0 3.4 fusion.452
  513.6 3.1 fusion.453
  519.3 22.5 %scatter_fusion = f32[15,384]{0,1:T(8,128)S(1)} fusion(f32[15,384]{0,1:T(8,128)S(1)} %get-tuple-element.621, s32[4096]{0:T(1024)S(1)} %bitcast.873, f32[4096,15]{1,0:T(8,128)S(1)} %copy.535), kind=kCustom, calls=%fused_computation.5.clone.1 | custom fusion | flops 61440 | bytes 753664 | tf_op jit(solution)/shard_map/while/body/eval_jaxpr/scatter-add | solution.py:78
  553.0 2.6 collective-permute-start.7
  564.9 38.2 %psum.7 = f32[2,4]{1,0:T(2,128)} all-reduce(f32[2,4]{1,0:T(2,128)S(1)} %pad_maximum_fusion.3), channel_id=1, replica_groups=mesh['gx'=8,'gy'=4] {'gx','gy'}, use_global_device_ids=true, to_apply=%region_19.20 | all-reduce | flops 8 | bytes 64 | tf_op jit(solution)/shard_map/psum | solution.py:160
  (1020 shorter events, 232.1 us)
Async XLA Ops:
  4.9 6.1 %collective-permute-start = (f32[1,16,64]{1,2,0:T(8,128)S(1)}, f32[1,16,64]{1,2,0:T(8,128)S(1)}, u32[]{:S(2)}, u32[]{:S(2)}) collective-permute-start(f32[1,16,64]{1,2,0:T(8,128)S(1)} %bitcast.882), channel_id=1, source_target_pairs={{0,4},{4,8},{8,12},{12,16},{16,20},{20,24},{24,28},{28,0},{1,5},{5... | collective-permute-start | bytes 12296 | tf_op jit(solution)/shard_map/ppermute | solution.py:23
  6.0 5.2 collective-permute-start.1
  12.0 6.5 %collective-permute-start.2 = (f32[1,16,64]{1,2,0:T(8,128)S(1)}, f32[1,16,64]{1,2,0:T(8,128)S(1)}, u32[]{:S(2)}, u32[]{:S(2)}) collective-permute-start(f32[1,16,64]{1,2,0:T(8,128)S(1)} %bitcast.883), channel_id=1, source_target_pairs={{0,1},{1,2},{2,3},{3,0},{4,5},{5,6},{6,7},{7,4},{8,9},{9,10},{10,1... | collective-permute-start | bytes 12296 | tf_op jit(solution)/shard_map/ppermute | solution.py:23
  16.4 4.0 collective-permute-start.3
  36.2 17.7 %copy-start.49 = (f32[32,128]{1,0:T(8,128)}, f32[32,128]{1,0:T(8,128)S(1)}, u32[]{:S(2)}) copy-start(f32[32,128]{1,0:T(8,128)S(1)} %get-tuple-element.559) | copy-start | bytes 49156 | tf_op jit(solution)/shard_map/while
  36.2 18.3 %copy-start.25 = (f32[32,128]{1,0:T(8,128)}, f32[32,128]{1,0:T(8,128)S(1)}, u32[]{:S(2)}) copy-start(f32[32,128]{1,0:T(8,128)S(1)} %get-tuple-element.541) | copy-start | bytes 49156 | tf_op jit(solution)/shard_map/while
  36.9 17.6 %copy-start.27 = (f32[32,128]{1,0:T(8,128)}, f32[32,128]{1,0:T(8,128)S(1)}, u32[]{:S(2)}) copy-start(f32[32,128]{1,0:T(8,128)S(1)} %get-tuple-element.542) | copy-start | bytes 49156 | tf_op jit(solution)/shard_map/while
  36.9 17.6 %copy-start.34 = (f32[32,128]{1,0:T(8,128)}, f32[32,128]{1,0:T(8,128)S(1)}, u32[]{:S(2)}) copy-start(f32[32,128]{1,0:T(8,128)S(1)} %get-tuple-element.552) | copy-start | bytes 49156 | tf_op jit(solution)/shard_map/while
  36.9 17.8 %copy-start.38 = (f32[32,128]{1,0:T(8,128)}, f32[32,128]{1,0:T(8,128)S(1)}, u32[]{:S(2)}) copy-start(f32[32,128]{1,0:T(8,128)S(1)} %get-tuple-element.558) | copy-start | bytes 49156 | tf_op jit(solution)/shard_map/while
  36.9 17.8 %copy-start.45 = (f32[32,128]{1,0:T(8,128)}, f32[32,128]{1,0:T(8,128)S(1)}, u32[]{:S(2)}) copy-start(f32[32,128]{1,0:T(8,128)S(1)} %get-tuple-element.562) | copy-start | bytes 49156 | tf_op jit(solution)/shard_map/while
  36.9 20.4 %copy-start.51 = (f32[32,128]{1,0:T(8,128)}, f32[32,128]{1,0:T(8,128)S(1)}, u32[]{:S(2)}) copy-start(f32[32,128]{1,0:T(8,128)S(1)} %get-tuple-element.565) | copy-start | bytes 49156 | tf_op jit(solution)/shard_map/while
  38.8 25.6 %copy-start.32 = (f32[1,4096]{1,0:T(1,128)}, f32[1,4096]{1,0:T(1,128)S(1)}, u32[]{:S(2)}) copy-start(f32[1,4096]{1,0:T(1,128)S(1)} %slice.408) | copy-start | bytes 49156 | tf_op jit(solution)/shard_map/while
  40.6 28.3 %copy-start.23 = (f32[4,32,128,1]{2,1,0,3:T(8,128)}, f32[4,32,128,1]{2,1,0,3:T(8,128)S(1)}, u32[]{:S(2)}) copy-start(f32[4,32,128,1]{2,1,0,3:T(8,128)S(1)} %get-tuple-element.572) | copy-start | bytes 196612 | tf_op jit(solution)/shard_map/while
  52.9 27.7 %copy-start.10 = (f32[32,8,64,1]{2,1,3,0:T(8,128)}, f32[32,8,64,1]{2,1,3,0:T(8,128)S(1)}, u32[]{:S(2)}) copy-start(f32[32,8,64,1]{2,1,3,0:T(8,128)S(1)} %copy.526) | copy-start | bytes 196612 | tf_op jit(solution)/shard_map/while
  166.5 17.7 %copy-start.49 = (f32[32,128]{1,0:T(8,128)}, f32[32,128]{1,0:T(8,128)S(1)}, u32[]{:S(2)}) copy-start(f32[32,128]{1,0:T(8,128)S(1)} %get-tuple-element.559) | copy-start | bytes 49156 | tf_op jit(solution)/shard_map/while
  166.5 18.3 %copy-start.25 = (f32[32,128]{1,0:T(8,128)}, f32[32,128]{1,0:T(8,128)S(1)}, u32[]{:S(2)}) copy-start(f32[32,128]{1,0:T(8,128)S(1)} %get-tuple-element.541) | copy-start | bytes 49156 | tf_op jit(solution)/shard_map/while
  167.2 17.6 %copy-start.27 = (f32[32,128]{1,0:T(8,128)}, f32[32,128]{1,0:T(8,128)S(1)}, u32[]{:S(2)}) copy-start(f32[32,128]{1,0:T(8,128)S(1)} %get-tuple-element.542) | copy-start | bytes 49156 | tf_op jit(solution)/shard_map/while
  167.2 17.6 %copy-start.34 = (f32[32,128]{1,0:T(8,128)}, f32[32,128]{1,0:T(8,128)S(1)}, u32[]{:S(2)}) copy-start(f32[32,128]{1,0:T(8,128)S(1)} %get-tuple-element.552) | copy-start | bytes 49156 | tf_op jit(solution)/shard_map/while
  167.2 17.8 %copy-start.38 = (f32[32,128]{1,0:T(8,128)}, f32[32,128]{1,0:T(8,128)S(1)}, u32[]{:S(2)}) copy-start(f32[32,128]{1,0:T(8,128)S(1)} %get-tuple-element.558) | copy-start | bytes 49156 | tf_op jit(solution)/shard_map/while
  167.2 17.8 %copy-start.45 = (f32[32,128]{1,0:T(8,128)}, f32[32,128]{1,0:T(8,128)S(1)}, u32[]{:S(2)}) copy-start(f32[32,128]{1,0:T(8,128)S(1)} %get-tuple-element.562) | copy-start | bytes 49156 | tf_op jit(solution)/shard_map/while
  167.2 20.4 %copy-start.51 = (f32[32,128]{1,0:T(8,128)}, f32[32,128]{1,0:T(8,128)S(1)}, u32[]{:S(2)}) copy-start(f32[32,128]{1,0:T(8,128)S(1)} %get-tuple-element.565) | copy-start | bytes 49156 | tf_op jit(solution)/shard_map/while
  169.1 25.4 %copy-start.32 = (f32[1,4096]{1,0:T(1,128)}, f32[1,4096]{1,0:T(1,128)S(1)}, u32[]{:S(2)}) copy-start(f32[1,4096]{1,0:T(1,128)S(1)} %slice.408) | copy-start | bytes 49156 | tf_op jit(solution)/shard_map/while
  170.9 28.1 %copy-start.23 = (f32[4,32,128,1]{2,1,0,3:T(8,128)}, f32[4,32,128,1]{2,1,0,3:T(8,128)S(1)}, u32[]{:S(2)}) copy-start(f32[4,32,128,1]{2,1,0,3:T(8,128)S(1)} %get-tuple-element.572) | copy-start | bytes 196612 | tf_op jit(solution)/shard_map/while
  183.2 27.6 %copy-start.10 = (f32[32,8,64,1]{2,1,3,0:T(8,128)}, f32[32,8,64,1]{2,1,3,0:T(8,128)S(1)}, u32[]{:S(2)}) copy-start(f32[32,8,64,1]{2,1,3,0:T(8,128)S(1)} %copy.526) | copy-start | bytes 196612 | tf_op jit(solution)/shard_map/while
  296.5 17.7 %copy-start.49 = (f32[32,128]{1,0:T(8,128)}, f32[32,128]{1,0:T(8,128)S(1)}, u32[]{:S(2)}) copy-start(f32[32,128]{1,0:T(8,128)S(1)} %get-tuple-element.559) | copy-start | bytes 49156 | tf_op jit(solution)/shard_map/while
  296.6 18.3 %copy-start.25 = (f32[32,128]{1,0:T(8,128)}, f32[32,128]{1,0:T(8,128)S(1)}, u32[]{:S(2)}) copy-start(f32[32,128]{1,0:T(8,128)S(1)} %get-tuple-element.541) | copy-start | bytes 49156 | tf_op jit(solution)/shard_map/while
  297.2 17.6 %copy-start.27 = (f32[32,128]{1,0:T(8,128)}, f32[32,128]{1,0:T(8,128)S(1)}, u32[]{:S(2)}) copy-start(f32[32,128]{1,0:T(8,128)S(1)} %get-tuple-element.542) | copy-start | bytes 49156 | tf_op jit(solution)/shard_map/while
  297.2 17.6 %copy-start.34 = (f32[32,128]{1,0:T(8,128)}, f32[32,128]{1,0:T(8,128)S(1)}, u32[]{:S(2)}) copy-start(f32[32,128]{1,0:T(8,128)S(1)} %get-tuple-element.552) | copy-start | bytes 49156 | tf_op jit(solution)/shard_map/while
  297.2 17.8 %copy-start.38 = (f32[32,128]{1,0:T(8,128)}, f32[32,128]{1,0:T(8,128)S(1)}, u32[]{:S(2)}) copy-start(f32[32,128]{1,0:T(8,128)S(1)} %get-tuple-element.558) | copy-start | bytes 49156 | tf_op jit(solution)/shard_map/while
  297.2 17.8 %copy-start.45 = (f32[32,128]{1,0:T(8,128)}, f32[32,128]{1,0:T(8,128)S(1)}, u32[]{:S(2)}) copy-start(f32[32,128]{1,0:T(8,128)S(1)} %get-tuple-element.562) | copy-start | bytes 49156 | tf_op jit(solution)/shard_map/while
  297.3 20.4 %copy-start.51 = (f32[32,128]{1,0:T(8,128)}, f32[32,128]{1,0:T(8,128)S(1)}, u32[]{:S(2)}) copy-start(f32[32,128]{1,0:T(8,128)S(1)} %get-tuple-element.565) | copy-start | bytes 49156 | tf_op jit(solution)/shard_map/while
  299.2 25.4 %copy-start.32 = (f32[1,4096]{1,0:T(1,128)}, f32[1,4096]{1,0:T(1,128)S(1)}, u32[]{:S(2)}) copy-start(f32[1,4096]{1,0:T(1,128)S(1)} %slice.408) | copy-start | bytes 49156 | tf_op jit(solution)/shard_map/while
  301.0 28.1 %copy-start.23 = (f32[4,32,128,1]{2,1,0,3:T(8,128)}, f32[4,32,128,1]{2,1,0,3:T(8,128)S(1)}, u32[]{:S(2)}) copy-start(f32[4,32,128,1]{2,1,0,3:T(8,128)S(1)} %get-tuple-element.572) | copy-start | bytes 196612 | tf_op jit(solution)/shard_map/while
  313.3 27.6 %copy-start.10 = (f32[32,8,64,1]{2,1,3,0:T(8,128)}, f32[32,8,64,1]{2,1,3,0:T(8,128)S(1)}, u32[]{:S(2)}) copy-start(f32[32,8,64,1]{2,1,3,0:T(8,128)S(1)} %copy.526) | copy-start | bytes 196612 | tf_op jit(solution)/shard_map/while
  426.6 17.7 %copy-start.49 = (f32[32,128]{1,0:T(8,128)}, f32[32,128]{1,0:T(8,128)S(1)}, u32[]{:S(2)}) copy-start(f32[32,128]{1,0:T(8,128)S(1)} %get-tuple-element.559) | copy-start | bytes 49156 | tf_op jit(solution)/shard_map/while
  426.6 18.3 %copy-start.25 = (f32[32,128]{1,0:T(8,128)}, f32[32,128]{1,0:T(8,128)S(1)}, u32[]{:S(2)}) copy-start(f32[32,128]{1,0:T(8,128)S(1)} %get-tuple-element.541) | copy-start | bytes 49156 | tf_op jit(solution)/shard_map/while
  427.3 17.6 %copy-start.27 = (f32[32,128]{1,0:T(8,128)}, f32[32,128]{1,0:T(8,128)S(1)}, u32[]{:S(2)}) copy-start(f32[32,128]{1,0:T(8,128)S(1)} %get-tuple-element.542) | copy-start | bytes 49156 | tf_op jit(solution)/shard_map/while
  427.3 17.6 %copy-start.34 = (f32[32,128]{1,0:T(8,128)}, f32[32,128]{1,0:T(8,128)S(1)}, u32[]{:S(2)}) copy-start(f32[32,128]{1,0:T(8,128)S(1)} %get-tuple-element.552) | copy-start | bytes 49156 | tf_op jit(solution)/shard_map/while
  427.3 17.8 %copy-start.38 = (f32[32,128]{1,0:T(8,128)}, f32[32,128]{1,0:T(8,128)S(1)}, u32[]{:S(2)}) copy-start(f32[32,128]{1,0:T(8,128)S(1)} %get-tuple-element.558) | copy-start | bytes 49156 | tf_op jit(solution)/shard_map/while
  427.3 17.8 %copy-start.45 = (f32[32,128]{1,0:T(8,128)}, f32[32,128]{1,0:T(8,128)S(1)}, u32[]{:S(2)}) copy-start(f32[32,128]{1,0:T(8,128)S(1)} %get-tuple-element.562) | copy-start | bytes 49156 | tf_op jit(solution)/shard_map/while
  427.3 20.4 %copy-start.51 = (f32[32,128]{1,0:T(8,128)}, f32[32,128]{1,0:T(8,128)S(1)}, u32[]{:S(2)}) copy-start(f32[32,128]{1,0:T(8,128)S(1)} %get-tuple-element.565) | copy-start | bytes 49156 | tf_op jit(solution)/shard_map/while
  429.3 25.4 %copy-start.32 = (f32[1,4096]{1,0:T(1,128)}, f32[1,4096]{1,0:T(1,128)S(1)}, u32[]{:S(2)}) copy-start(f32[1,4096]{1,0:T(1,128)S(1)} %slice.408) | copy-start | bytes 49156 | tf_op jit(solution)/shard_map/while
  431.1 28.1 %copy-start.23 = (f32[4,32,128,1]{2,1,0,3:T(8,128)}, f32[4,32,128,1]{2,1,0,3:T(8,128)S(1)}, u32[]{:S(2)}) copy-start(f32[4,32,128,1]{2,1,0,3:T(8,128)S(1)} %get-tuple-element.572) | copy-start | bytes 196612 | tf_op jit(solution)/shard_map/while
  443.4 27.6 %copy-start.10 = (f32[32,8,64,1]{2,1,3,0:T(8,128)}, f32[32,8,64,1]{2,1,3,0:T(8,128)S(1)}, u32[]{:S(2)}) copy-start(f32[32,8,64,1]{2,1,3,0:T(8,128)S(1)} %copy.526) | copy-start | bytes 196612 | tf_op jit(solution)/shard_map/while
  544.9 5.9 collective-permute-start.4
  546.5 5.4 collective-permute-start.5
  553.0 6.6 %collective-permute-start.6 = (f32[1,15,64]{1,2,0:T(8,128)S(1)}, f32[1,15,64]{1,2,0:T(8,128)S(1)}, u32[]{:S(2)}, u32[]{:S(2)}) collective-permute-start(f32[1,15,64]{1,2,0:T(8,128)S(1)} %get-tuple-element.396), channel_id=1, source_target_pairs={{0,4},{4,8},{8,12},{12,16},{16,20},{20,24},{24,28},{28,0},{1,5},{5... | collective-permute-start | bytes 11528 | tf_op jit(solution)/shard_map/ppermute | solution.py:23
  553.0 7.7 %collective-permute-start.7 = (f32[1,15,64]{1,2,0:T(8,128)S(1)}, f32[1,15,64]{1,2,0:T(8,128)S(1)}, u32[]{:S(2)}, u32[]{:S(2)}) collective-permute-start(f32[1,15,64]{1,2,0:T(8,128)S(1)} %get-tuple-element.395), channel_id=1, source_target_pairs={{4,0},{8,4},{12,8},{16,12},{20,16},{24,20},{28,24},{0,28},{5,1},{9... | collective-permute-start | bytes 11528 | tf_op jit(solution)/shard_map/ppermute | solution.py:24
  (245 other events, 1401.6 us)
where the time goes:
time: 610 us; the launch traced here: 603 us
  matrix products  291 us (48%)
  other arithmetic  136 us (22%)
  local copies, waits for them, and re-layouts  105 us (17%)
  blocking collectives  38.2 us (6%)
  starting transfers between devices  14.5 us (2%)
  loops' own time  12.1 us (2%)
    dot_general x36, matrix products, site_energy(): jnp.einsum('cbs,mbs->cmb', environ, embedded, precision=HIGHEST)  121 us
    scatter-add x4, other arithmetic, advance(): accumulated.at[:, slot_rows.reshape(-1)].add(terms.reshape(15, -1))  89.8 us
    dot_general x36, matrix products, site_energy(): jnp.einsum('cmb,cnb->mnb', contracted, contracted[:, :M2], precision=HIGH...  53 us
    gather x8, local copies, waits for them, and re-layouts, block_terms(): jnp.take(ghosted, slot_rows.reshape(-1), axis=1)  45.4 us
    dot_general x16, matrix products, site_energy(): jnp.einsum('kbs,km->mbs', powers, poly_table[1] - poly_table[0], precisio...  42.8 us
    dot_general x16, matrix products, site_energy(): jnp.einsum('kbs,km->mbs', powers, poly_table[0], precision=HIGHEST)  42.3 us
    psum x1, blocking collectives, local(): moments = lax.psum(jnp.stack([norm_part, cross_part], axis=0), ('gx', 'gy'))  38.2 us
    while x588, local copies, waits for them, and re-layouts  12.8 us
  transfers between devices with their start and end apart: 8, of which 2 were waited for; matrix products, arithmetic and copies ran while one was open for 1% of the time, Pallas kernels for 0%

commit v1 on v0

v1 whole, which is shorter than its diff:
```python
import functools

import jax
import jax.numpy as jnp
from jax import lax
from jax.experimental import pallas as pl
from jax.experimental.pallas import tpu as pltpu
from jax.sharding import PartitionSpec as P

BRICK = 5.0
SOFTENING = 0.25
CUTOFF_SQ = 16.0
LIGHT = 1.008 ** (-0.5)
HEAVY = 28.0855 ** (-0.5)
LANES = 128
SUBLANES = 8
M2 = 8
HALF = 64
F32 = jnp.float32
BF16 = jnp.bfloat16
VMEM = pl.BlockSpec(memory_space=pltpu.VMEM)
SMEM = pl.BlockSpec(memory_space=pltpu.SMEM)


def shape(*dims, dtype=F32):
    return jax.ShapeDtypeStruct(dims, dtype)


def call(body, outs, specs, scratch=(), flops=0, limit=None):
    return pl.pallas_call(
        body,
        out_shape=outs,
        in_specs=specs,
        out_specs=jax.tree.map(lambda _: VMEM, outs),
        scratch_shapes=list(scratch),
        compiler_params=pltpu.CompilerParams(vmem_limit_bytes=limit),
        cost_estimate=pl.CostEstimate(flops=flops, bytes_accessed=1 << 16, transcendentals=0),
    )


def halves(x):
    high = x.astype(BF16)
    return high, (x - high.astype(F32)).astype(BF16)


def dot(a, b, contract=((1,), (0,))):
    return lax.dot_general(a, b, (contract, ((), ())), preferred_element_type=F32)


def dot3(a, b, contract=((1,), (0,))):
    return dot(a[0], b[0], contract) + (dot(a[0], b[1], contract) + dot(a[1], b[0], contract))


def lane_take(row, index):
    return jnp.take_along_axis(
        jnp.broadcast_to(row, index.shape), index, axis=1, mode="promise_in_bounds"
    )


def lane_number(rows):
    return lax.broadcasted_iota(jnp.int32, (rows, LANES), 1)


def take_columns(parts, lists):
    low = jnp.broadcast_to(lists & (LANES - 1), (SUBLANES, LANES))
    chunk = jnp.broadcast_to(lists >> 7, (SUBLANES, LANES))
    rows = []
    for base in range(0, 16, SUBLANES):
        value = jnp.take_along_axis(
            parts[0][base : base + SUBLANES], low, axis=1, mode="promise_in_bounds"
        )
        for number in range(1, len(parts)):
            other = jnp.take_along_axis(
                parts[number][base : base + SUBLANES], low, axis=1, mode="promise_in_bounds"
            )
            value = jnp.where(chunk == number, other, value)
        rows.append(value)
    return jnp.concatenate(rows, axis=0)


def add_columns(values, lists, columns):
    high, low = halves(values)
    places = lax.broadcasted_iota(jnp.int32, (columns, LANES), 0)
    hot = (places == jnp.broadcast_to(lists, (columns, LANES))).astype(F32).astype(BF16)
    summed = dot(jnp.concatenate([high, low], axis=0), hot, ((1,), (1,)))
    return summed[0:16] + summed[16:32]


def joined(lower, upper, row):
    lanes = lane_number(16)
    rows = lax.broadcasted_iota(jnp.int32, (16, LANES), 0)
    shift = jnp.where(rows == row, jnp.where(lanes < HALF, -BRICK, BRICK), 0.0)
    return jnp.where(lanes < HALF, lower, upper) + shift


def params_body(
    poly_ref, fit_ref, hidden_ref, bias_ref, out_ref, nb_ref,
    ws_ref, wst_ref, hid_ref, hidt_ref, cols_ref, nbt_ref,
    table, mixed, square, columns,
):
    table[...] = jnp.zeros_like(table)
    table[0:6, :] = poly_ref[0]
    table[6:12, :] = poly_ref[1] - poly_ref[0]
    features = table[...]
    split_features = halves(features)
    for n in range(M2):
        picked = fit_ref[pl.ds(n, HALF, stride=M2), :]
        mixed[pl.ds(n, 16, stride=M2), :] = dot3(split_features, halves(picked))
    axis_features = halves(features[:, 0:M2])
    for k in range(16):
        block = mixed[k * M2 : (k + 1) * M2, :]
        square[k * 16 : (k + 1) * 16, :] = dot3(axis_features, halves(block))
    for k in range(12):
        block = square[k * 16 : (k + 1) * 16, :] + square[pl.ds(k, 16, stride=16), :]
        ws_ref[k * 16 : (k + 1) * 16, :] = 0.5 * block
    ws_ref[192:256, :] = jnp.zeros((64, LANES), F32)
    wst_ref[:, 0:128] = ws_ref[0:128, :].T
    wst_ref[:, 128:256] = ws_ref[128:256, :].T
    for layer in range(2):
        high, low = halves(hidden_ref[layer])
        hid_ref[layer, 0] = high
        hid_ref[layer, 1] = low
        high, low = halves(hidden_ref[layer].T)
        hidt_ref[layer, 0] = high
        hidt_ref[layer, 1] = low
    columns[...] = jnp.zeros_like(columns)
    columns[0:3, :] = bias_ref[...]
    columns[3:4, :] = out_ref[...].reshape(1, LANES)
    cols_ref[...] = columns[...].T
    nbt_ref[...] = nb_ref[0, 0].T


def field_body(coords_ref, types_ref, cur_ref, prev_ref, send_ref, field_ref, sent_ref, sums_ref):
    kind = types_ref[0].astype(F32)
    scale = HEAVY + kind * (LIGHT - HEAVY)
    for a in range(3):
        field_ref[a : a + 1, :] = coords_ref[a, 0]
    field_ref[3:4, :] = kind
    lanes = lane_number(1)
    norm = jnp.zeros((1, LANES), F32)
    past = jnp.zeros((1, LANES), F32)
    for w in range(4):
        own = jnp.zeros((1, LANES), F32)
        old = jnp.zeros((1, LANES), F32)
        for b in range(3):
            current = cur_ref[w, b, 0]
            own += current * current
            old += current * prev_ref[w, b, 0]
            row = 4 + 3 * w + b
            field_ref[row : row + 1, :] = current * scale
        norm = jnp.where(lanes == w, jnp.sum(own, axis=1, keepdims=True), norm)
        past = jnp.where(lanes == w, jnp.sum(old, axis=1, keepdims=True), past)
    sums_ref[0:1, :] = norm
    sums_ref[1:2, :] = past
    lists = jnp.concatenate([send_ref[0, 0, 1:2, :], send_ref[0, 0, 0:1, :]], axis=1)
    sent_ref[...] = take_columns([field_ref[...]], lists)


def first_body(field_ref, lower_ref, upper_ref, send_ref, ghost_ref, sent_ref):
    ghost = joined(lower_ref[...], upper_ref[...], 0)
    ghost_ref[...] = ghost
    lists = jnp.concatenate([send_ref[0, 0, 1:2, :], send_ref[0, 0, 0:1, :]], axis=1)
    sent_ref[...] = take_columns([field_ref[...], ghost], lists)


def pair_body(
    entries, slots,
    spectrum_ref, field_ref, ghost_ref, lower_ref, upper_ref, nbt_ref,
    ws_ref, wst_ref, hid_ref, hidt_ref, cols_ref, sums_ref,
    terms_ref, share_ref,
    chunks, pair, power, moment, gee, form, back, lam,
):
    groups = slots // SUBLANES
    chunks[0] = field_ref[...]
    chunks[1] = ghost_ref[...]
    chunks[2] = joined(lower_ref[...], upper_ref[...], 1)
    moment[...] = jnp.zeros_like(moment)

    def gather(group, carry):
        at = pl.ds(pl.multiple_of(group * SUBLANES, SUBLANES), SUBLANES)
        index = nbt_ref[at, :]
        low = index & (LANES - 1)
        chunk = index >> 7
        second = chunk == 1
        third = chunk == 2
        rows = []
        for r in range(16):
            value = jnp.where(second, lane_take(chunks[1, r : r + 1, :], low), lane_take(chunks[0, r : r + 1, :], low))
            value = jnp.where(third, lane_take(chunks[2, r : r + 1, :], low), value)
            if r != 3:
                value = value - chunks[0, r : r + 1, :]
            pair[r, at, :] = value
            if r < 3:
                rows.append(value)
        x, y, z = rows
        radius_sq = x * x + y * y + z * z
        inverse = lax.rsqrt(radius_sq + SOFTENING)
        switch = 1.0 / (1.0 + radius_sq / CUTOFF_SQ)
        pair[16, at, :] = inverse
        value = switch
        for k in range(6):
            power[k, at, :] = value
            value = value * switch
        return carry

    lax.fori_loop(0, groups, gather, 0)

    zero = jnp.zeros((SUBLANES, LANES), F32)

    def sum_moments(w, parts):
        def body(group, totals):
            at = pl.ds(pl.multiple_of(group * SUBLANES, SUBLANES), SUBLANES)
            totals = list(totals)
            powers = [power[k, at, :] for k in range(6)]
            near = pair[3, at, :]
            inverse = pair[16, at, :]
            if w:
                d = [pair[a, at, :] for a in range(3)]
                v = [pair[1 + 3 * w + a, at, :] for a in range(3)]
                along = d[0] * v[0] + d[1] * v[1] + d[2] * v[2]
                tau = powers[0] * along * (-2.0 / CUTOFF_SQ)
                fall = inverse * inverse * along
            for place, c in enumerate(parts):
                if w == 0:
                    weight = None if c == 0 else pair[c - 1, at, :] * inverse
                elif c == 0:
                    weight, step = zero, tau
                else:
                    unit = d[c - 1] * inverse
                    step = tau * unit
                    weight = v[c - 1] * inverse - unit * fall
                for k in range(6):
                    if w:
                        weight = step if (c == 0 and k == 0) else weight + step
                    term = powers[k] if weight is None else powers[k] * weight
                    totals[place * 12 + k] += term
                    totals[place * 12 + 6 + k] += near * term
            return tuple(totals)

        totals = lax.fori_loop(0, groups, body, (zero,) * (12 * len(parts)))
        for place, c in enumerate(parts):
            for k in range(12):
                row = ((w * 4 + c) * 16 + k) * SUBLANES
                moment[row : row + SUBLANES, :] = totals[place * 12 + k]

    for w in range(5):
        sum_moments(w, (0, 1))
        sum_moments(w, (2, 3))

    for block in range(20):
        total = moment[pl.ds(block * 128, 16, stride=SUBLANES), :]
        for sub in range(1, SUBLANES):
            total += moment[pl.ds(block * 128 + sub, 16, stride=SUBLANES), :]
        gee[block] = total * (1.0 / slots)

    for k in range(12):
        for w in range(5):
            total = gee[w * 4] * gee[0, k : k + 1, :]
            for c in range(1, 4):
                total += gee[w * 4 + c] * gee[c, k : k + 1, :]
            form[k * 16 : (k + 1) * 16, w * LANES : (w + 1) * LANES] = total * 2.0 if w == 0 else total * 4.0
    form[192:256, :] = jnp.zeros((64, 5 * LANES), F32)

    def wide(column):
        return jnp.broadcast_to(column, (LANES, LANES))

    def cut(x, w):
        return x[:, w * LANES : (w + 1) * LANES]

    def layer(pre, bias):
        bent = jnp.tanh(cut(pre, 0) + wide(bias))
        slope = 1.0 - bent * bent
        return bent, slope

    pre1 = dot3(halves(wst_ref[...] * 0.5), halves(form[...]))
    bent1, slope1 = layer(pre1, cols_ref[:, 0:1])
    hidden1 = [bent1] + [slope1 * cut(pre1, w) for w in range(1, 5)]
    pre2 = dot3((hidt_ref[0, 0], hidt_ref[0, 1]), halves(jnp.concatenate(hidden1, axis=1)))
    bent2, slope2 = layer(pre2, cols_ref[:, 1:2])
    hidden2 = [bent2 + hidden1[0]] + [slope2 * cut(pre2, w) + hidden1[w] for w in range(1, 5)]
    pre3 = dot3((hidt_ref[1, 0], hidt_ref[1, 1]), halves(jnp.concatenate(hidden2, axis=1)))
    bent3, slope3 = layer(pre3, cols_ref[:, 2:3])
    out = wide(cols_ref[:, 3:4])
    adj3 = [out * slope3] + [(-2.0 * out * bent3 * slope3) * cut(pre3, w) for w in range(1, 5)]
    up2 = dot3((hid_ref[1, 0], hid_ref[1, 1]), halves(jnp.concatenate(adj3, axis=1)))
    up2 = [cut(up2, 0) + out] + [cut(up2, w) for w in range(1, 5)]
    bend2 = -2.0 * up2[0] * bent2 * slope2
    adj2 = [up2[0] * slope2] + [up2[w] * slope2 + bend2 * cut(pre2, w) for w in range(1, 5)]
    up1 = dot3((hid_ref[0, 0], hid_ref[0, 1]), halves(jnp.concatenate(adj2, axis=1)))
    up1 = [cut(up1, w) + up2[w] for w in range(5)]
    bend1 = -2.0 * up1[0] * bent1 * slope1
    adj1 = [up1[0] * slope1] + [up1[w] * slope1 + bend1 * cut(pre1, w) for w in range(1, 5)]
    back[...] = dot3(halves(ws_ref[...]), halves(jnp.concatenate(adj1, axis=1)))

    for c in range(4):
        totals = [None] * 5
        for k in range(12):
            rows = slice(k * 16, (k + 1) * 16)
            base = back[rows, 0:LANES]
            plain = gee[c, k : k + 1, :]
            for w in range(5):
                if w == 0:
                    term = base * plain
                else:
                    term = back[rows, w * LANES : (w + 1) * LANES] * plain + base * gee[w * 4 + c, k : k + 1, :]
                totals[w] = term if k == 0 else totals[w] + term
        for w in range(5):
            lam[w * 4 + c] = totals[w] * (2.0 / slots)
            lam[w * 4 + c, 6:12, :] = lam[w * 4 + c, 0:6, :] + lam[w * 4 + c, 6:12, :]

    def push(group, quad):
        start = pl.multiple_of(group * SUBLANES, SUBLANES)
        at = pl.ds(start, SUBLANES)
        switch = power[0, at, :]
        inverse = pair[16, at, :]
        near = pair[3, at, :] > 0.5
        d = [pair[a, at, :] for a in range(3)]
        unit = [x * inverse for x in d]
        alpha = switch * (2.0 / CUTOFF_SQ)
        square = inverse * inverse
        quad = list(quad)

        def coefficients(w, c):
            return [
                jnp.where(near, lam[w * 4 + c, 6 + k : 7 + k, :], lam[w * 4 + c, k : k + 1, :])
                for k in range(6)
            ]

        def poly(values):
            total = values[5]
            for k in range(4, -1, -1):
                total = total * switch + values[k]
            return total * switch

        def store(row, value):
            terms_ref[pl.ds(start * 16 + row, SUBLANES, stride=16), :] = value

        plain, first, second = [], [], []
        for c in range(4):
            values = coefficients(0, c)
            plain.append(poly(values) if c else None)
            first.append(poly([values[k] * (k + 1.0) for k in range(6)]))
            second.append(poly([values[k] * ((k + 1.0) * (k + 1.0)) for k in range(6)]))

        def along(values):
            return values[1] * unit[0] + values[2] * unit[1] + values[3] * unit[2]

        plain_along = along(plain)
        first_along = along(first)
        first_sum = first[0] + first_along
        second_sum = second[0] + along(second)
        fall = -(alpha * first_sum + square * plain_along)
        for b in range(3):
            store(b, inverse * plain[b + 1] + d[b] * fall)
        bend = [-inverse * (square * plain[b + 1] + alpha * first[b + 1]) for b in range(3)]
        curl = (
            alpha * alpha * (first_sum + second_sum)
            + 2.0 * alpha * square * first_along
            + 3.0 * square * square * plain_along
        )
        for w in range(1, 5):
            values = [coefficients(w, c) for c in range(4)]
            p = [None] + [poly(values[c]) for c in range(1, 4)]
            f = [poly([values[c][k] * (k + 1.0) for k in range(6)]) for c in range(4)]
            down = -(alpha * (f[0] + along(f)) + square * along(p))
            v = [pair[1 + 3 * w + a, at, :] for a in range(3)]
            s = d[0] * v[0] + d[1] * v[1] + d[2] * v[2]
            t = s * curl + (bend[0] * v[0] + bend[1] * v[1] + bend[2] * v[2]) + down
            for b in range(3):
                term = bend[b] * s + v[b] * fall + d[b] * t + inverse * p[b + 1]
                store(3 * w + b, term)
                quad[w - 1] = quad[w - 1] + term * v[b]
        store(15, zero)
        return tuple(quad)

    quad = lax.fori_loop(0, groups, push, (zero,) * 4)

    lanes = lane_number(1)
    local = jnp.zeros((1, LANES), F32)
    for w in range(4):
        total = jnp.sum(jnp.sum(quad[w], axis=0, keepdims=True), axis=1, keepdims=True)
        local = jnp.where(lanes == w, total, local)
    center = (spectrum_ref[0] + spectrum_ref[1]) / 2.0
    width = (spectrum_ref[1] - spectrum_ref[0]) / 2.0
    norm = sums_ref[0:1, :]
    cross = 2.0 * (local - center * norm) / width - sums_ref[1:2, :]
    share = (norm + pltpu.roll(cross, 4, 1)) * (1.0 / entries)
    share_ref[...] = jnp.broadcast_to(share, share_ref.shape)


def scatter_body(slots, terms_ref, nbt_ref, accum_ref):
    per = SUBLANES
    places = lax.broadcasted_iota(jnp.int32, (LANES, LANES), 0)

    def body(group, carry):
        total, own = carry
        start = pl.multiple_of(group * per, per)
        lefts, rights = [], []
        for s in range(per):
            index = nbt_ref[pl.ds(start + s, 1), :]
            values = terms_ref[pl.ds((start + s) * 16, 16), :]
            own = own + values
            high, low = halves(values)
            chunk = index >> 7
            masks = [jnp.broadcast_to((chunk == c).astype(F32), (16, LANES)).astype(BF16) for c in range(3)]
            lefts.append(jnp.concatenate([x * m for m in masks for x in (high, low)], axis=0))
            hot = places == jnp.broadcast_to(index & (LANES - 1), (LANES, LANES))
            rights.append(hot.astype(F32).astype(BF16))
        left = jnp.concatenate(lefts, axis=1)
        right = jnp.concatenate(rights, axis=1)
        return total + dot(left, right, ((1,), (1,))), own

    total, own = lax.fori_loop(
        0, slots // per, body, (jnp.zeros((96, LANES), F32), jnp.zeros((16, LANES), F32))
    )
    for c in range(3):
        part = total[c * 32 : c * 32 + 16] + total[c * 32 + 16 : c * 32 + 32]
        accum_ref[c] = part - own if c == 0 else part


def fold_body(accum_ref, below_ref, above_ref, send_ref, own_ref, ghost_ref):
    lists = jnp.concatenate([send_ref[0, 0, 1:2, :], send_ref[0, 0, 0:1, :]], axis=1)
    values = jnp.where(lane_number(16) < HALF, above_ref[...], below_ref[...])
    added = add_columns(values, lists, 2 * LANES)
    own_ref[...] = accum_ref[0] + added[:, 0:LANES]
    ghost_ref[...] = accum_ref[1] + added[:, LANES:]


def last_body(
    spectrum_ref, own_ref, below_ref, above_ref, send_ref, types_ref, cur_ref, prev_ref, shares_ref,
    forces_ref, next_ref, moments_ref,
):
    lists = jnp.concatenate([send_ref[0, 0, 1:2, :], send_ref[0, 0, 0:1, :]], axis=1)
    values = jnp.where(lane_number(16) < HALF, above_ref[...], below_ref[...])
    own = own_ref[...] + add_columns(values, lists, LANES)
    scale = HEAVY + types_ref[0].astype(F32) * (LIGHT - HEAVY)
    center = (spectrum_ref[0] + spectrum_ref[1]) / 2.0
    width = (spectrum_ref[1] - spectrum_ref[0]) / 2.0
    for a in range(3):
        forces_ref[a, 0] = -own[a : a + 1]
    for w in range(4):
        for b in range(3):
            row = 3 + 3 * w + b
            current = cur_ref[w, b, 0]
            next_ref[w, b, 0] = (
                2.0 * (scale * own[row : row + 1] - center * current) / width - prev_ref[w, b, 0]
            )
    total = jnp.sum(shares_ref[...], axis=0, keepdims=True)
    moments_ref[0:1, :] = total[:, 0:4]
    moments_ref[1:2, :] = pltpu.roll(total, LANES - 4, 1)[:, 0:4]


def shifted(x, axis):
    devices = lax.axis_size(axis)
    up = [(i, (i + 1) % devices) for i in range(devices)]
    down = [(j, i) for i, j in up]
    return lax.ppermute(x, axis, up), lax.ppermute(x, axis, down)


def local(
    coords, atom_types, neighbours, send_x, send_y, poly_table, fit_in, fit_hidden, fit_bias,
    fit_out, spectrum, cheb_prev, cheb_cur,
):
    atoms, slots = neighbours.shape[2], neighbours.shape[3]
    devices = lax.axis_size("gx") * lax.axis_size("gy")
    entries = 3.0 * atoms * devices
    tile = shape(16, LANES)

    field, sent, sums = call(
        field_body, [tile, tile, shape(2, LANES)], [VMEM] * 5
    )(coords, atom_types, cheb_cur, cheb_prev, send_x)
    lower, upper = shifted(sent, "gx")
    ws, wst, hid, hidt, cols, nbt = call(
        params_body,
        [
            shape(256, LANES), shape(LANES, 256), shape(2, 2, 128, 128, dtype=BF16),
            shape(2, 2, 128, 128, dtype=BF16), shape(128, 128), shape(slots, atoms, dtype=jnp.int32),
        ],
        [VMEM] * 6,
        [pltpu.VMEM((16, HALF), F32), pltpu.VMEM((128, LANES), F32), pltpu.VMEM((256, LANES), F32), pltpu.VMEM((128, 128), F32)],
        flops=20_000_000,
    )(poly_table, fit_in, fit_hidden, fit_bias, fit_out, neighbours)
    ghost, sent = call(first_body, [tile, tile], [VMEM] * 4)(field, lower, upper, send_y)
    lower, upper = shifted(sent, "gy")
    terms, share = call(
        functools.partial(pair_body, entries, slots),
        [shape(slots * 16, LANES), shape(devices, LANES)],
        [SMEM] + [VMEM] * 11,
        [
            pltpu.VMEM((3, 16, LANES), F32),
            pltpu.VMEM((17, slots, LANES), F32),
            pltpu.VMEM((6, slots, LANES), F32),
            pltpu.VMEM((20 * 128, LANES), F32),
            pltpu.VMEM((20, 16, LANES), F32),
            pltpu.VMEM((256, 5 * LANES), F32),
            pltpu.VMEM((256, 5 * LANES), F32),
            pltpu.VMEM((20, 16, LANES), F32),
        ],
        flops=40_000_000,
        limit=32 << 20,
    )(spectrum, field, ghost, lower, upper, nbt, ws, wst, hid, hidt, cols, sums)
    shares = lax.all_to_all(share, ("gx", "gy"), 0, 0)
    accum = call(
        functools.partial(scatter_body, slots), shape(3, 16, LANES), [VMEM] * 2, flops=40_000_000
    )(terms, nbt)
    below, above = shifted(accum[2], "gy")
    own, ghost = call(fold_body, [tile, tile], [VMEM] * 4)(accum, below, above, send_y)
    below, above = shifted(ghost, "gx")
    return tuple(
        call(
            last_body,
            [shape(*coords.shape), shape(*cheb_cur.shape), shape(2, 4)],
            [SMEM] + [VMEM] * 8,
        )(spectrum, own, below, above, send_x, atom_types, cheb_cur, cheb_prev, shares)
    )


def solution(mesh):
    return jax.shard_map(
        local,
        mesh=mesh,
        in_specs=(
            P(None, "gx", "gy", None),
            P("gx", "gy", None),
            P("gx", "gy", None, None),
            P("gx", "gy", None, None),
            P("gx", "gy", None, None),
            P(),
            P(),
            P(),
            P(),
            P(),
            P(),
            P(None, None, "gx", "gy", None),
            P(None, None, "gx", "gy", None),
        ),
        out_specs=(P(None, "gx", "gy", None), P(None, None, "gx", "gy", None), P()),
        check_vma=False,
    )
```

time: 610 us -> 67.4 us (0.11)
  matrix products: 291 us -> 0 us
  other arithmetic: 136 us -> 0 us
  local copies, waits for them, and re-layouts: 105 us -> 10.1 us
  blocking collectives: 38.2 us -> 0 us
  Pallas kernels: 0 us -> 25.7 us
  waiting for transfers between devices: 3.45 us -> 16.5 us
  loops' own time: 12.1 us -> 0 us
    dot_general x152 -> x0, matrix products: 291 us -> none  [the longest x36 121 us: site_energy(): jnp.einsum('cbs,mbs->cmb', environ, embedded, precision=HIGHEST)]
    scatter-add x8 -> x0, other arithmetic: 94.2 us -> none  [the longest x4 89.8 us: advance(): accumulated.at[:, slot_rows.reshape(-1)].add(terms.reshape(15, -1))]
    gather x12 -> x0, local copies, waits for them, and re-layouts: 47.8 us -> none  [the longest x8 45.4 us: block_terms(): jnp.take(ghosted, slot_rows.reshape(-1), axis=1)]
    psum x1 -> x0, blocking collectives: 38.2 us -> none  [local(): moments = lax.psum(jnp.stack([norm_part, cross_part], axis=0), ('gx', 'gy'))]
    pallas_call x0 -> x7, Pallas kernels: none -> 25.7 us  [the longest x1 11.6 us: local(): call(functools.partial(pair_body, entries, slots), [shape(slots * 16, LAN...]
    mul x30 -> x0, other arithmetic: 21.3 us -> none  [the longest x8 6.35 us: site_energy(): switch ** degree]
    transpose x24 -> x0, local copies, waits for them, and re-layouts: 14.7 us -> none  [the longest x16 8.91 us: site_energy(): jnp.einsum('cmb,cnb->mnb', contracted, contracted[:, :M2], precision=HIGH...]
    while x590 -> x0, local copies, waits for them, and re-layouts: 14.3 us -> none
  transfers between devices with their start and end apart: 8 -> 9, of which waited for: 2 -> 7; matrix products, arithmetic and copies ran while one was open for 1% -> 2% of each run, Pallas kernels for 0% -> 6%
where the time goes in v1:
time: 67.4 us; the launch traced here: 66.8 us
  Pallas kernels  25.7 us (38%)
  waiting for transfers between devices  16.5 us (24%)
  starting transfers between devices  13.8 us (20%)
  local copies, waits for them, and re-layouts  10.1 us (15%)
  between operations  0.68 us (1%)
    ppermute x8, waiting for transfers between devices, shifted(): return (lax.ppermute(x, axis, up), lax.ppermute(x, axis, down))  16.5 us
    pallas_call x1, Pallas kernels, local(): call(functools.partial(pair_body, entries, slots), [shape(slots * 16, LAN...  11.6 us
    ppermute x8, starting transfers between devices, shifted(): return (lax.ppermute(x, axis, up), lax.ppermute(x, axis, down))  11.3 us
    unnamed x39, local copies, waits for them, and re-layouts  9.35 us
    pallas_call x1, Pallas kernels, local(): call(functools.partial(scatter_body, slots), shape(3, 16, LANES), [VMEM]...  5.54 us
    all_to_all x1, starting transfers between devices, local(): shares = lax.all_to_all(share, ('gx', 'gy'), 0, 0)  2.51 us
    pallas_call x1, Pallas kernels, local(): call(params_body, [shape(256, LANES), shape(LANES, 256), shape(2, 2, 128,...  2.39 us
    pallas_call x1, Pallas kernels, local(): call(last_body, [shape(*coords.shape), shape(*cheb_cur.shape), shape(2, 4...  1.67 us
  transfers between devices with their start and end apart: 9, of which 7 were waited for; matrix products, arithmetic and copies ran while one was open for 2% of the time, Pallas kernels for 6%

profile of v1, /device:TPU:0, one launch (start us, length us, event | category | flops | bytes accessed | tf_op | source)
XLA Modules:
  0.0 66.8 jit_solution(11085502318463347174)
XLA Ops:
  0.6 1.5 %shard_map.148 = (f32[16,128]{1,0:T(8,128)}, f32[16,128]{1,0:T(8,128)}, f32[2,128]{1,0:T(2,128)}) custom-call(f32[3,1,1,128]{3,2,1,0:T(1,128)} %coords_ref.1, s32[1,1,128]{2,1,0:T(1,128)} %types_ref.3, f32[4,3,1,1,128]{4,3,2,1,0:T(1,128)} %cur_ref.3, f32[4,3,1,1,128]{4,3,2,1,0:T(1,128)} %prev_ref.3, s32[1,1,2,64]{3,2,1,0:T(2,128)} %send_ref.7), custom_call_target="tpu_custom_call" | custom-call | bytes 65536 | tf_op jit(solution)/shard_map/pallas_call | solution.py:469
  2.1 3.3 %collective-permute-start.1 = (f32[16,128]{1,0:T(8,128)}, f32[16,128]{1,0:T(8,128)S(1)}, u32[]{:S(2)}, u32[]{:S(2)}) collective-permute-start(f32[16,128]{1,0:T(8,128)} %get-tuple-element.19), channel_id=1, source_target_pairs={{4,0},{8,4},{12,8},{16,12},{20,16},{24,20},{28,24},{0,28},{5,1},{9... | collective-permute-start | bytes 24584 | tf_op jit(solution)/shard_map/ppermute | solution.py:457
  5.4 0.0 collective-permute-start
  5.4 1.6 %collective-permute-done.1.upper_ref = f32[16,128]{1,0:T(8,128)S(1)} collective-permute-done((f32[16,128]{1,0:T(8,128)}, f32[16,128]{1,0:T(8,128)S(1)}, u32[]{:S(2)}, u32[]{:S(2)}) %collective-permute-start.1) | collective-permute-done | bytes 8224 | tf_op jit(solution)/shard_map/ppermute | solution.py:457
  7.0 0.0 copy-start.14
  7.0 2.6 %collective-permute-done.lower_ref = f32[16,128]{1,0:T(8,128)S(1)} collective-permute-done((f32[16,128]{1,0:T(8,128)}, f32[16,128]{1,0:T(8,128)S(1)}, u32[]{:S(2)}, u32[]{:S(2)}) %collective-permute-start) | collective-permute-done | bytes 8224 | tf_op jit(solution)/shard_map/ppermute | solution.py:457
  9.6 0.0 copy-start.15
  9.6 0.0 copy-done.14
  9.6 0.6 copy-done.15
  10.2 1.5 %shard_map.149 = (f32[16,128]{1,0:T(8,128)}, f32[16,128]{1,0:T(8,128)}) custom-call(f32[16,128]{1,0:T(8,128)} %get-tuple-element.18.field_ref, f32[16,128]{1,0:T(8,128)} %copy-done.15, f32[16,128]{1,0:T(8,128)} %copy-done.14, s32[1,1,2,64]{3,2,1,0:T(2,128)} %send_ref.6), custom_call_target="tpu_custom_call" | custom-call | bytes 65536 | tf_op jit(solution)/shard_map/pallas_call | solution.py:483
  11.7 3.6 %collective-permute-start.3 = (f32[16,128]{1,0:T(8,128)}, f32[16,128]{1,0:T(8,128)S(1)}, u32[]{:S(2)}, u32[]{:S(2)}) collective-permute-start(f32[16,128]{1,0:T(8,128)} %get-tuple-element.21), channel_id=1, source_target_pairs={{1,0},{2,1},{3,2},{0,3},{5,4},{6,5},{7,6},{4,7},{9,8},{10,9},{11,1... | collective-permute-start | bytes 24584 | tf_op jit(solution)/shard_map/ppermute | solution.py:457
  15.3 0.0 collective-permute-start.2
  15.3 0.0 copy-done.18
  15.3 0.6 copy.17.poly_ref
  15.9 2.4 %shard_map.150 = (f32[256,128]{1,0:T(8,128)}, f32[128,256]{1,0:T(8,128)}, bf16[2,2,128,128]{3,2,1,0:T(8,128)(2,1)}, bf16[2,2,128,128]{3,2,1,0:T(8,128)(2,1)}, f32[128,128]{1,0:T(8,128)}, /*index=5*/s32[128,128]{1,0:T(8,128)}) custom-call(f32[2,6,64]{2,1,0:T(8,128)} %copy.17.poly_ref, f32[512,128]{1,0:T(8,128)} %fit_ref.1, f32[2,128,128]{2,1,0:T(8,128)} %hidden_ref.1, ...), custom_call_target="tpu_custom_call" | custom-call | flops 20000000 | bytes 65536 | tf_op jit(solution)/shard_map/pallas_call | solution.py:473
  18.3 0.0 collective-permute-done.3.upper_ref
  18.3 2.7 %collective-permute-done.2.lower_ref = f32[16,128]{1,0:T(8,128)S(1)} collective-permute-done((f32[16,128]{1,0:T(8,128)}, f32[16,128]{1,0:T(8,128)S(1)}, u32[]{:S(2)}, u32[]{:S(2)}) %collective-permute-start.2) | collective-permute-done | bytes 8224 | tf_op jit(solution)/shard_map/ppermute | solution.py:457
  21.0 0.0 copy-done.8
  21.0 0.0 copy-done.7
  21.0 0.6 copy-done.9
  21.6 0.0 copy-done.10
  21.7 0.8 %copy-done.1 = s32[128,128]{1,0:T(8,128)S(1)} copy-done((s32[128,128]{1,0:T(8,128)S(1)}, s32[128,128]{1,0:T(8,128)}, u32[]{:S(2)}) %copy-start.1) | copy-done | bytes 65560
  22.5 0.9 %copy-done.2 = f32[256,128]{1,0:T(8,128)S(1)} copy-done((f32[256,128]{1,0:T(8,128)S(1)}, f32[256,128]{1,0:T(8,128)}, u32[]{:S(2)}) %copy-start.2) | copy-done | bytes 131096
  23.4 0.9 %copy-done.3 = f32[128,256]{1,0:T(8,128)S(1)} copy-done((f32[128,256]{1,0:T(8,128)S(1)}, f32[128,256]{1,0:T(8,128)}, u32[]{:S(2)}) %copy-start.3) | copy-done | bytes 131096
  24.3 0.9 %copy-done.4 = bf16[2,2,128,128]{3,2,1,0:T(8,128)(2,1)S(1)} copy-done((bf16[2,2,128,128]{3,2,1,0:T(8,128)(2,1)S(1)}, bf16[2,2,128,128]{3,2,1,0:T(8,128)(2,1)}, u32[]{:S(2)}) %copy-start.4) | copy-done | bytes 131096
  25.2 0.9 %copy-done.5 = bf16[2,2,128,128]{3,2,1,0:T(8,128)(2,1)S(1)} copy-done((bf16[2,2,128,128]{3,2,1,0:T(8,128)(2,1)S(1)}, bf16[2,2,128,128]{3,2,1,0:T(8,128)(2,1)}, u32[]{:S(2)}) %copy-start.5) | copy-done | bytes 131096
  26.1 0.8 %copy-done.6 = f32[128,128]{1,0:T(8,128)S(1)} copy-done((f32[128,128]{1,0:T(8,128)S(1)}, f32[128,128]{1,0:T(8,128)}, u32[]{:S(2)}) %copy-start.6) | copy-done | bytes 65560
  27.0 11.6 %shard_map.151 = (f32[2048,128]{1,0:T(8,128)S(1)}, f32[32,128]{1,0:T(8,128)}) custom-call(f32[2]{0:T(128)S(1)} %copy-done.9, f32[16,128]{1,0:T(8,128)S(1)} %copy-done.7, f32[16,128]{1,0:T(8,128)S(1)} %copy-done.8, f32[16,128]{1,0:T(8,128)S(1)} %collective-permute-done.2.lower_ref, f32[16,128]{1,0:T(8,128)S(1)} %collective-permute-done.3.upper_ref, ...), custom_call_target="tpu_custom_call" | custom-call | flops 40000000 | bytes 65536 | tf_op jit(solution)/shard_map/pallas_call | solution.py:485
  38.6 1.0 %copy-done = f32[2048,128]{1,0:T(8,128)} copy-done((f32[2048,128]{1,0:T(8,128)}, f32[2048,128]{1,0:T(8,128)S(1)}, u32[]{:S(2)}) %copy-start) | copy-done | bytes 1048600
  39.5 5.5 %shard_map.152.accum_ref = f32[3,16,128]{2,1,0:T(8,128)} custom-call(f32[2048,128]{1,0:T(8,128)} %copy-done, s32[128,128]{1,0:T(8,128)} %get-tuple-element.22.nbt_ref), custom_call_target="tpu_custom_call" | custom-call | flops 40000000 | bytes 65536 | tf_op jit(solution)/shard_map/pallas_call | solution.py:503
  45.1 2.5 %all-to-all-start = ((f32[32,1,128]{2,1,0:T(1,128)}), f32[32,1,128]{2,1,0:T(1,128)S(1)}, u32[]{:S(2)}, u32[]{:S(2)}) async-start(f32[32,1,128]{2,1,0:T(1,128)} %bitcast.2), calls=%async_computation | async-start | bytes 32768 | tf_op jit(solution)/shard_map/all_to_all | solution.py:502
  47.6 0.7 %slice_bitcast_fusion = f32[16,128]{1,0:T(8,128)S(1)} fusion(f32[3,16,128]{2,1,0:T(8,128)} %shard_map.152.accum_ref), kind=kLoop, calls=%fused_computation | loop fusion | bytes 16384 | tf_op jit(solution)/shard_map/squeeze | solution.py:506
  48.3 3.6 %collective-permute-start.5 = (f32[16,128]{1,0:T(8,128)S(1)}, f32[16,128]{1,0:T(8,128)S(1)}, u32[]{:S(2)}, u32[]{:S(2)}) collective-permute-start(f32[16,128]{1,0:T(8,128)S(1)} %slice_bitcast_fusion), channel_id=1, source_target_pairs={{1,0},{2,1},{3,2},{0,3},{5,4},{6,5},{7,6},{4,7},{9,8},{10,9},{11,1... | collective-permute-start | bytes 24584 | tf_op jit(solution)/shard_map/ppermute | solution.py:457
  51.9 0.0 collective-permute-start.4
  51.9 1.4 %collective-permute-done.5.above_ref = f32[16,128]{1,0:T(8,128)S(1)} collective-permute-done((f32[16,128]{1,0:T(8,128)S(1)}, f32[16,128]{1,0:T(8,128)S(1)}, u32[]{:S(2)}, u32[]{:S(2)}) %collective-permute-start.5) | collective-permute-done | bytes 8224 | tf_op jit(solution)/shard_map/ppermute | solution.py:457
  53.3 4.1 %collective-permute-done.4.below_ref = f32[16,128]{1,0:T(8,128)S(1)} collective-permute-done((f32[16,128]{1,0:T(8,128)S(1)}, f32[16,128]{1,0:T(8,128)S(1)}, u32[]{:S(2)}, u32[]{:S(2)}) %collective-permute-start.4) | collective-permute-done | bytes 8224 | tf_op jit(solution)/shard_map/ppermute | solution.py:457
  57.4 0.0 copy-done.16
  57.4 0.6 copy-done.17
  58.0 1.6 %shard_map.153 = (f32[16,128]{1,0:T(8,128)}, f32[16,128]{1,0:T(8,128)}) custom-call(f32[3,16,128]{2,1,0:T(8,128)} %shard_map.152.accum_ref, f32[16,128]{1,0:T(8,128)} %copy-done.17, f32[16,128]{1,0:T(8,128)} %copy-done.16, s32[1,1,2,64]{3,2,1,0:T(2,128)} %send_ref.6), custom_call_target="tpu_custom_call" | custom-call | bytes 65536 | tf_op jit(solution)/shard_map/pallas_call | solution.py:507
  59.5 0.7 %collective-permute-start.7 = (f32[16,128]{1,0:T(8,128)}, f32[16,128]{1,0:T(8,128)S(1)}, u32[]{:S(2)}, u32[]{:S(2)}) collective-permute-start(f32[16,128]{1,0:T(8,128)} %get-tuple-element.31), channel_id=1, source_target_pairs={{4,0},{8,4},{12,8},{16,12},{20,16},{24,20},{28,24},{0,28},{5,1},{9... | collective-permute-start | bytes 24584 | tf_op jit(solution)/shard_map/ppermute | solution.py:457
  60.3 0.0 collective-permute-start.6
  60.3 1.6 %collective-permute-done.7.above_ref = f32[16,128]{1,0:T(8,128)S(1)} collective-permute-done((f32[16,128]{1,0:T(8,128)}, f32[16,128]{1,0:T(8,128)S(1)}, u32[]{:S(2)}, u32[]{:S(2)}) %collective-permute-start.7) | collective-permute-done | bytes 8224 | tf_op jit(solution)/shard_map/ppermute | solution.py:457
  61.9 2.6 %collective-permute-done.6.below_ref = f32[16,128]{1,0:T(8,128)S(1)} collective-permute-done((f32[16,128]{1,0:T(8,128)}, f32[16,128]{1,0:T(8,128)S(1)}, u32[]{:S(2)}, u32[]{:S(2)}) %collective-permute-start.6) | collective-permute-done | bytes 8224 | tf_op jit(solution)/shard_map/ppermute | solution.py:457
  64.5 0.0 all-to-all-done
  64.5 0.0 copy-done.12
  64.5 0.6 copy-done.13
  65.1 0.0 copy-done.11
  65.1 1.7 %shard_map.154 = (f32[3,1,1,128]{3,2,1,0:T(1,128)}, f32[4,3,1,1,128]{4,3,2,1,0:T(1,128)}, f32[2,4]{1,0:T(2,128)}) custom-call(f32[2]{0:T(128)} %spectrum_ref.3, f32[16,128]{1,0:T(8,128)} %get-tuple-element.30.own_ref, f32[16,128]{1,0:T(8,128)} %copy-done.13, f32[16,128]{1,0:T(8,128)} %copy-done.12, s32[1,1,2,64]{3,2,1,0:T(2,128)} %send_ref.7, ...), custom_call_target="tpu_custom_call" | custom-call | bytes 65536 | tf_op jit(solution)/shard_map/pallas_call | solution.py:510
  (17 shorter events, 0.0 us)
Async XLA Ops:
  2.1 4.9 %collective-permute-start.1 = (f32[16,128]{1,0:T(8,128)}, f32[16,128]{1,0:T(8,128)S(1)}, u32[]{:S(2)}, u32[]{:S(2)}) collective-permute-start(f32[16,128]{1,0:T(8,128)} %get-tuple-element.19), channel_id=1, source_target_pairs={{4,0},{8,4},{12,8},{16,12},{20,16},{24,20},{28,24},{0,28},{5,1},{9... | collective-permute-start | bytes 24584 | tf_op jit(solution)/shard_map/ppermute | solution.py:457
  5.4 4.2 %collective-permute-start = (f32[16,128]{1,0:T(8,128)}, f32[16,128]{1,0:T(8,128)S(1)}, u32[]{:S(2)}, u32[]{:S(2)}) collective-permute-start(f32[16,128]{1,0:T(8,128)} %get-tuple-element.19), channel_id=1, source_target_pairs={{0,4},{4,8},{8,12},{12,16},{16,20},{20,24},{24,28},{28,0},{1,5},{5... | collective-permute-start | bytes 24584 | tf_op jit(solution)/shard_map/ppermute | solution.py:457
  7.0 2.6 %copy-start.14 = (f32[16,128]{1,0:T(8,128)}, f32[16,128]{1,0:T(8,128)S(1)}, u32[]{:S(2)}) copy-start(f32[16,128]{1,0:T(8,128)S(1)} %collective-permute-done.1.upper_ref) | copy-start | bytes 24580
  9.6 0.6 copy-start.15
  10.2 5.1 %copy-start.18 = (f32[2,6,64]{2,0,1:T(2,128)S(1)}, f32[2,6,64]{2,0,1:T(2,128)}, u32[]{:S(2)}) copy-start(f32[2,6,64]{2,0,1:T(2,128)} %param.18) | copy-start | bytes 9220
  11.7 6.6 %collective-permute-start.3 = (f32[16,128]{1,0:T(8,128)}, f32[16,128]{1,0:T(8,128)S(1)}, u32[]{:S(2)}, u32[]{:S(2)}) collective-permute-start(f32[16,128]{1,0:T(8,128)} %get-tuple-element.21), channel_id=1, source_target_pairs={{1,0},{2,1},{3,2},{0,3},{5,4},{6,5},{7,6},{4,7},{9,8},{10,9},{11,1... | collective-permute-start | bytes 24584 | tf_op jit(solution)/shard_map/ppermute | solution.py:457
  15.3 5.7 %collective-permute-start.2 = (f32[16,128]{1,0:T(8,128)}, f32[16,128]{1,0:T(8,128)S(1)}, u32[]{:S(2)}, u32[]{:S(2)}) collective-permute-start(f32[16,128]{1,0:T(8,128)} %get-tuple-element.21), channel_id=1, source_target_pairs={{0,1},{1,2},{2,3},{3,0},{4,5},{5,6},{6,7},{7,4},{8,9},{9,10},{10,1... | collective-permute-start | bytes 24584 | tf_op jit(solution)/shard_map/ppermute | solution.py:457
  15.9 5.1 %copy-start.8 = (f32[16,128]{1,0:T(8,128)S(1)}, f32[16,128]{1,0:T(8,128)}, u32[]{:S(2)}) copy-start(f32[16,128]{1,0:T(8,128)} %get-tuple-element.20.ghost_ref) | copy-start | bytes 24580
  18.3 2.7 %copy-start.7 = (f32[16,128]{1,0:T(8,128)S(1)}, f32[16,128]{1,0:T(8,128)}, u32[]{:S(2)}) copy-start(f32[16,128]{1,0:T(8,128)} %get-tuple-element.18.field_ref) | copy-start | bytes 24580
  21.0 0.7 copy-start.9
  21.0 0.7 %copy-start.10 = (f32[2,128]{1,0:T(2,128)S(1)}, f32[2,128]{1,0:T(2,128)}, u32[]{:S(2)}) copy-start(f32[2,128]{1,0:T(2,128)} %get-tuple-element.28.sums_ref) | copy-start | bytes 3076
  21.7 0.8 %copy-start.1 = (s32[128,128]{1,0:T(8,128)S(1)}, s32[128,128]{1,0:T(8,128)}, u32[]{:S(2)}) copy-start(s32[128,128]{1,0:T(8,128)} %get-tuple-element.22.nbt_ref) | copy-start | bytes 196612
  22.5 0.9 %copy-start.2 = (f32[256,128]{1,0:T(8,128)S(1)}, f32[256,128]{1,0:T(8,128)}, u32[]{:S(2)}) copy-start(f32[256,128]{1,0:T(8,128)} %get-tuple-element.23.ws_ref) | copy-start | bytes 393220
  23.4 0.9 %copy-start.3 = (f32[128,256]{1,0:T(8,128)S(1)}, f32[128,256]{1,0:T(8,128)}, u32[]{:S(2)}) copy-start(f32[128,256]{1,0:T(8,128)} %get-tuple-element.24.wst_ref) | copy-start | bytes 393220
  24.3 0.9 %copy-start.4 = (bf16[2,2,128,128]{3,2,1,0:T(8,128)(2,1)S(1)}, bf16[2,2,128,128]{3,2,1,0:T(8,128)(2,1)}, u32[]{:S(2)}) copy-start(bf16[2,2,128,128]{3,2,1,0:T(8,128)(2,1)} %get-tuple-element.25.hid_ref) | copy-start | bytes 393220
  25.2 0.9 %copy-start.5 = (bf16[2,2,128,128]{3,2,1,0:T(8,128)(2,1)S(1)}, bf16[2,2,128,128]{3,2,1,0:T(8,128)(2,1)}, u32[]{:S(2)}) copy-start(bf16[2,2,128,128]{3,2,1,0:T(8,128)(2,1)} %get-tuple-element.26.hidt_ref) | copy-start | bytes 393220
  26.1 0.8 %copy-start.6 = (f32[128,128]{1,0:T(8,128)S(1)}, f32[128,128]{1,0:T(8,128)}, u32[]{:S(2)}) copy-start(f32[128,128]{1,0:T(8,128)} %get-tuple-element.27.cols_ref) | copy-start | bytes 196612
  38.6 1.0 %copy-start = (f32[2048,128]{1,0:T(8,128)}, f32[2048,128]{1,0:T(8,128)S(1)}, u32[]{:S(2)}) copy-start(f32[2048,128]{1,0:T(8,128)S(1)} %get-tuple-element.29.terms_ref) | copy-start | bytes 3145732
  45.1 19.4 %all-to-all-start = ((f32[32,1,128]{2,1,0:T(1,128)}), f32[32,1,128]{2,1,0:T(1,128)S(1)}, u32[]{:S(2)}, u32[]{:S(2)}) async-start(f32[32,1,128]{2,1,0:T(1,128)} %bitcast.2), calls=%async_computation | async-start | bytes 32768 | tf_op jit(solution)/shard_map/all_to_all | solution.py:502
  48.3 5.0 %collective-permute-start.5 = (f32[16,128]{1,0:T(8,128)S(1)}, f32[16,128]{1,0:T(8,128)S(1)}, u32[]{:S(2)}, u32[]{:S(2)}) collective-permute-start(f32[16,128]{1,0:T(8,128)S(1)} %slice_bitcast_fusion), channel_id=1, source_target_pairs={{1,0},{2,1},{3,2},{0,3},{5,4},{6,5},{7,6},{4,7},{9,8},{10,9},{11,1... | collective-permute-start | bytes 24584 | tf_op jit(solution)/shard_map/ppermute | solution.py:457
  51.9 5.4 %collective-permute-start.4 = (f32[16,128]{1,0:T(8,128)S(1)}, f32[16,128]{1,0:T(8,128)S(1)}, u32[]{:S(2)}, u32[]{:S(2)}) collective-permute-start(f32[16,128]{1,0:T(8,128)S(1)} %slice_bitcast_fusion), channel_id=1, source_target_pairs={{0,1},{1,2},{2,3},{3,0},{4,5},{5,6},{6,7},{7,4},{8,9},{9,10},{10,1... | collective-permute-start | bytes 24584 | tf_op jit(solution)/shard_map/ppermute | solution.py:457
  53.3 4.1 %copy-start.16 = (f32[16,128]{1,0:T(8,128)}, f32[16,128]{1,0:T(8,128)S(1)}, u32[]{:S(2)}) copy-start(f32[16,128]{1,0:T(8,128)S(1)} %collective-permute-done.5.above_ref) | copy-start | bytes 24580
  57.4 0.6 copy-start.17
  59.5 2.3 %collective-permute-start.7 = (f32[16,128]{1,0:T(8,128)}, f32[16,128]{1,0:T(8,128)S(1)}, u32[]{:S(2)}, u32[]{:S(2)}) collective-permute-start(f32[16,128]{1,0:T(8,128)} %get-tuple-element.31), channel_id=1, source_target_pairs={{4,0},{8,4},{12,8},{16,12},{20,16},{24,20},{28,24},{0,28},{5,1},{9... | collective-permute-start | bytes 24584 | tf_op jit(solution)/shard_map/ppermute | solution.py:457
  60.3 4.2 %collective-permute-start.6 = (f32[16,128]{1,0:T(8,128)}, f32[16,128]{1,0:T(8,128)S(1)}, u32[]{:S(2)}, u32[]{:S(2)}) collective-permute-start(f32[16,128]{1,0:T(8,128)} %get-tuple-element.31), channel_id=1, source_target_pairs={{0,4},{4,8},{8,12},{12,16},{16,20},{20,24},{24,28},{28,0},{1,5},{5... | collective-permute-start | bytes 24584 | tf_op jit(solution)/shard_map/ppermute | solution.py:457
  61.9 2.6 %copy-start.12 = (f32[16,128]{1,0:T(8,128)}, f32[16,128]{1,0:T(8,128)S(1)}, u32[]{:S(2)}) copy-start(f32[16,128]{1,0:T(8,128)S(1)} %collective-permute-done.7.above_ref) | copy-start | bytes 24580
  64.5 0.6 copy-start.13
  64.5 0.6 copy-start.11

commit v2 on v1

--- a/solution.py
+++ b/solution.py
@@ -19,14 +19,13 @@
 F32 = jnp.float32
 BF16 = jnp.bfloat16
 VMEM = pl.BlockSpec(memory_space=pltpu.VMEM)
-SMEM = pl.BlockSpec(memory_space=pltpu.SMEM)
 
 
 def shape(*dims, dtype=F32):
     return jax.ShapeDtypeStruct(dims, dtype)
 
 
-def call(body, outs, specs, scratch=(), flops=0, limit=None):
+def call(body, outs, specs, scratch=(), flops=0, limit=16 << 20):
     return pl.pallas_call(
         body,
         out_shape=outs,
@@ -130,65 +129,102 @@
     nbt_ref[...] = nb_ref[0, 0].T
 
 
-def field_body(coords_ref, types_ref, cur_ref, prev_ref, send_ref, field_ref, sent_ref, sums_ref):
-    kind = types_ref[0].astype(F32)
+def field_body(
+    coords_hbm, types_hbm, cur_hbm, prev_hbm, send_x_hbm, send_y_hbm, spectrum_hbm,
+    pack_ref, sent_ref, tail_ref,
+    coords, types, cur, prev, send_x, send_y, spectrum, sems,
+):
+    pairs = (
+        (coords_hbm, coords), (types_hbm, types), (cur_hbm, cur), (prev_hbm, prev),
+        (send_x_hbm, send_x), (send_y_hbm, send_y), (spectrum_hbm, spectrum),
+    )
+    copies = [pltpu.make_async_copy(a, b, sems.at[n]) for n, (a, b) in enumerate(pairs)]
+    for copy in copies:
+        copy.start()
+    for copy in copies:
+        copy.wait()
+    kind = types[0].astype(F32)
     scale = HEAVY + kind * (LIGHT - HEAVY)
+    center = (spectrum[0] + spectrum[1]) / 2.0
+    width = (spectrum[1] - spectrum[0]) / 2.0
     for a in range(3):
-        field_ref[a : a + 1, :] = coords_ref[a, 0]
-    field_ref[3:4, :] = kind
+        pack_ref[a : a + 1, :] = coords[a, 0]
+    pack_ref[3:4, :] = kind
+    tail_ref[0:16, :] = jnp.broadcast_to(2.0 * scale / width, (16, LANES))
+    tail_ref[0:3, :] = jnp.full((3, LANES), -1.0, F32)
+    tail_ref[16:40, :] = jnp.zeros((24, LANES), F32)
     lanes = lane_number(1)
-    norm = jnp.zeros((1, LANES), F32)
-    past = jnp.zeros((1, LANES), F32)
+    sums = jnp.zeros((1, LANES), F32)
     for w in range(4):
         own = jnp.zeros((1, LANES), F32)
         old = jnp.zeros((1, LANES), F32)
         for b in range(3):
-            current = cur_ref[w, b, 0]
+            current, past = cur[w, b, 0], prev[w, b, 0]
             own += current * current
-            old += current * prev_ref[w, b, 0]
-            row = 4 + 3 * w + b
-            field_ref[row : row + 1, :] = current * scale
-        norm = jnp.where(lanes == w, jnp.sum(own, axis=1, keepdims=True), norm)
-        past = jnp.where(lanes == w, jnp.sum(old, axis=1, keepdims=True), past)
-    sums_ref[0:1, :] = norm
-    sums_ref[1:2, :] = past
-    lists = jnp.concatenate([send_ref[0, 0, 1:2, :], send_ref[0, 0, 0:1, :]], axis=1)
-    sent_ref[...] = take_columns([field_ref[...]], lists)
-
-
-def first_body(field_ref, lower_ref, upper_ref, send_ref, ghost_ref, sent_ref):
+            old += current * past
+            row = 3 + 3 * w + b
+            pack_ref[row + 1 : row + 2, :] = current * scale
+            tail_ref[16 + row : 17 + row, :] = 2.0 * center * current / width + past
+        own = jnp.sum(own, axis=1, keepdims=True)
+        old = jnp.sum(old, axis=1, keepdims=True)
+        sums = jnp.where(lanes == w, own, sums)
+        sums = jnp.where(lanes == 4 + w, -2.0 * center / width * own - old, sums)
+    lists_x = jnp.concatenate([send_x[0, 0, 1:2, :], send_x[0, 0, 0:1, :]], axis=1)
+    lists_y = jnp.concatenate([send_y[0, 0, 1:2, :], send_y[0, 0, 0:1, :]], axis=1)
+    pack_ref[16:24, :] = jnp.zeros((8, LANES), F32)
+    pack_ref[16:17, :] = lists_y.astype(F32)
+    pack_ref[17:18, :] = sums
+    pack_ref[18:19, :] = jnp.full((1, LANES), 2.0 / width, F32)
+    tail_ref[32:33, :] = lists_x.astype(F32)
+    sent_ref[...] = take_columns([pack_ref[0:16, :]], lists_x)
+
+
+def hold_body(pack_ref, held_ref):
+    held_ref[...] = pack_ref[...]
+
+
+def first_body(pack_ref, lower_ref, upper_ref, ghost_ref, sent_ref):
     ghost = joined(lower_ref[...], upper_ref[...], 0)
     ghost_ref[...] = ghost
-    lists = jnp.concatenate([send_ref[0, 0, 1:2, :], send_ref[0, 0, 0:1, :]], axis=1)
-    sent_ref[...] = take_columns([field_ref[...], ghost], lists)
+    sent_ref[...] = take_columns([pack_ref[0:16, :], ghost], pack_ref[16:17, :].astype(jnp.int32))
+
+
+def near_body(slots, pack_ref, ghost_ref, nbt_ref, near_ref):
+    def body(group, carry):
+        at = pl.ds(pl.multiple_of(group * SUBLANES, SUBLANES), SUBLANES)
+        index = nbt_ref[at, :]
+        low = index & (LANES - 1)
+        second = (index >> 7) == 1
+        for r in range(16):
+            near_ref[r, at, :] = jnp.where(
+                second, lane_take(ghost_ref[r : r + 1, :], low), lane_take(pack_ref[r : r + 1, :], low)
+            )
+        return carry
+
+    lax.fori_loop(0, slots // SUBLANES, body, 0, unroll=2)
 
 
 def pair_body(
     entries, slots,
-    spectrum_ref, field_ref, ghost_ref, lower_ref, upper_ref, nbt_ref,
-    ws_ref, wst_ref, hid_ref, hidt_ref, cols_ref, sums_ref,
-    terms_ref, share_ref,
-    chunks, pair, power, moment, gee, form, back, lam,
+    pack_ref, near_ref, lower_ref, upper_ref, nbt_ref,
+    ws_ref, wst_ref, hid_ref, hidt_ref, cols_ref,
+    accum_ref, share_ref,
+    terms_ref, far, pair, power, moment, gee, form, back, lam,
 ):
     groups = slots // SUBLANES
-    chunks[0] = field_ref[...]
-    chunks[1] = ghost_ref[...]
-    chunks[2] = joined(lower_ref[...], upper_ref[...], 1)
+    far[...] = joined(lower_ref[...], upper_ref[...], 1)
     moment[...] = jnp.zeros_like(moment)
 
     def gather(group, carry):
         at = pl.ds(pl.multiple_of(group * SUBLANES, SUBLANES), SUBLANES)
         index = nbt_ref[at, :]
         low = index & (LANES - 1)
-        chunk = index >> 7
-        second = chunk == 1
-        third = chunk == 2
+        third = (index >> 7) == 2
         rows = []
         for r in range(16):
-            value = jnp.where(second, lane_take(chunks[1, r : r + 1, :], low), lane_take(chunks[0, r : r + 1, :], low))
-            value = jnp.where(third, lane_take(chunks[2, r : r + 1, :], low), value)
+            value = jnp.where(third, lane_take(far[r : r + 1, :], low), near_ref[r, at, :])
             if r != 3:
-                value = value - chunks[0, r : r + 1, :]
+                value = value - pack_ref[r : r + 1, :]
             pair[r, at, :] = value
             if r < 3:
                 rows.append(value)
@@ -203,7 +239,7 @@
             value = value * switch
         return carry
 
-    lax.fori_loop(0, groups, gather, 0)
+    lax.fori_loop(0, groups, gather, 0, unroll=2)
 
     zero = jnp.zeros((SUBLANES, LANES), F32)
 
@@ -237,7 +273,7 @@
                     totals[place * 12 + 6 + k] += near * term
             return tuple(totals)
 
-        totals = lax.fori_loop(0, groups, body, (zero,) * (12 * len(parts)))
+        totals = lax.fori_loop(0, groups, body, (zero,) * (12 * len(parts)), unroll=4)
         for place, c in enumerate(parts):
             for k in range(12):
                 row = ((w * 4 + c) * 16 + k) * SUBLANES
@@ -258,7 +294,7 @@
             total = gee[w * 4] * gee[0, k : k + 1, :]
             for c in range(1, 4):
                 total += gee[w * 4 + c] * gee[c, k : k + 1, :]
-            form[k * 16 : (k + 1) * 16, w * LANES : (w + 1) * LANES] = total * 2.0 if w == 0 else total * 4.0
+            form[k * 16 : (k + 1) * 16, w * LANES : (w + 1) * LANES] = total if w == 0 else total * 2.0
     form[192:256, :] = jnp.zeros((64, 5 * LANES), F32)
 
     def wide(column):
@@ -272,7 +308,7 @@
         slope = 1.0 - bent * bent
         return bent, slope
 
-    pre1 = dot3(halves(wst_ref[...] * 0.5), halves(form[...]))
+    pre1 = dot3(halves(wst_ref[...]), halves(form[...]))
     bent1, slope1 = layer(pre1, cols_ref[:, 0:1])
     hidden1 = [bent1] + [slope1 * cut(pre1, w) for w in range(1, 5)]
     pre2 = dot3((hidt_ref[0, 0], hidt_ref[0, 1]), halves(jnp.concatenate(hidden1, axis=1)))
@@ -373,23 +409,23 @@
         store(15, zero)
         return tuple(quad)
 
-    quad = lax.fori_loop(0, groups, push, (zero,) * 4)
+    quad = lax.fori_loop(0, groups, push, (zero,) * 4, unroll=2)
 
     lanes = lane_number(1)
     local = jnp.zeros((1, LANES), F32)
     for w in range(4):
         total = jnp.sum(jnp.sum(quad[w], axis=0, keepdims=True), axis=1, keepdims=True)
-        local = jnp.where(lanes == w, total, local)
-    center = (spectrum_ref[0] + spectrum_ref[1]) / 2.0
-    width = (spectrum_ref[1] - spectrum_ref[0]) / 2.0
-    norm = sums_ref[0:1, :]
-    cross = 2.0 * (local - center * norm) / width - sums_ref[1:2, :]
-    share = (norm + pltpu.roll(cross, 4, 1)) * (1.0 / entries)
+        local = jnp.where(lanes == 4 + w, total, local)
+    share = (pack_ref[17:18, :] + pack_ref[18:19, :] * local) * (1.0 / entries)
     share_ref[...] = jnp.broadcast_to(share, share_ref.shape)
-
-
-def scatter_body(slots, terms_ref, nbt_ref, accum_ref):
-    per = SUBLANES
+    total, own = scatter_columns(slots, terms_ref, nbt_ref)
+    for c in range(3):
+        part = total[c * 32 : c * 32 + 16] + total[c * 32 + 16 : c * 32 + 32]
+        accum_ref[c] = part - own if c == 0 else part
+
+
+def scatter_columns(slots, terms_ref, nbt_ref):
+    per = 32
     places = lax.broadcasted_iota(jnp.int32, (LANES, LANES), 0)
 
     def body(group, carry):
@@ -410,41 +446,30 @@
         right = jnp.concatenate(rights, axis=1)
         return total + dot(left, right, ((1,), (1,))), own
 
-    total, own = lax.fori_loop(
-        0, slots // per, body, (jnp.zeros((96, LANES), F32), jnp.zeros((16, LANES), F32))
-    )
-    for c in range(3):
-        part = total[c * 32 : c * 32 + 16] + total[c * 32 + 16 : c * 32 + 32]
-        accum_ref[c] = part - own if c == 0 else part
-
-
-def fold_body(accum_ref, below_ref, above_ref, send_ref, own_ref, ghost_ref):
-    lists = jnp.concatenate([send_ref[0, 0, 1:2, :], send_ref[0, 0, 0:1, :]], axis=1)
+    start = (jnp.zeros((96, LANES), F32), jnp.zeros((16, LANES), F32))
+    return lax.fori_loop(0, slots // per, body, start)
+
+
+def fold_body(accum_ref, below_ref, above_ref, pack_ref, own_ref, ghost_ref):
     values = jnp.where(lane_number(16) < HALF, above_ref[...], below_ref[...])
-    added = add_columns(values, lists, 2 * LANES)
+    added = add_columns(values, pack_ref[16:17, :].astype(jnp.int32), 2 * LANES)
     own_ref[...] = accum_ref[0] + added[:, 0:LANES]
     ghost_ref[...] = accum_ref[1] + added[:, LANES:]
 
 
 def last_body(
-    spectrum_ref, own_ref, below_ref, above_ref, send_ref, types_ref, cur_ref, prev_ref, shares_ref,
+    own_ref, below_ref, above_ref, tail_ref, shares_ref,
     forces_ref, next_ref, moments_ref,
 ):
-    lists = jnp.concatenate([send_ref[0, 0, 1:2, :], send_ref[0, 0, 0:1, :]], axis=1)
     values = jnp.where(lane_number(16) < HALF, above_ref[...], below_ref[...])
-    own = own_ref[...] + add_columns(values, lists, LANES)
-    scale = HEAVY + types_ref[0].astype(F32) * (LIGHT - HEAVY)
-    center = (spectrum_ref[0] + spectrum_ref[1]) / 2.0
-    width = (spectrum_ref[1] - spectrum_ref[0]) / 2.0
+    own = own_ref[...] + add_columns(values, tail_ref[32:33, :].astype(jnp.int32), LANES)
+    own = own * tail_ref[0:16, :] - tail_ref[16:32, :]
     for a in range(3):
-        forces_ref[a, 0] = -own[a : a + 1]
+        forces_ref[a, 0] = own[a : a + 1]
     for w in range(4):
         for b in range(3):
             row = 3 + 3 * w + b
-            current = cur_ref[w, b, 0]
-            next_ref[w, b, 0] = (
-                2.0 * (scale * own[row : row + 1] - center * current) / width - prev_ref[w, b, 0]
-            )
+            next_ref[w, b, 0] = own[row : row + 1]
     total = jnp.sum(shares_ref[...], axis=0, keepdims=True)
     moments_ref[0:1, :] = total[:, 0:4]
     moments_ref[1:2, :] = pltpu.roll(total, LANES - 4, 1)[:, 0:4]
@@ -466,10 +491,17 @@
     entries = 3.0 * atoms * devices
     tile = shape(16, LANES)
 
-    field, sent, sums = call(
-        field_body, [tile, tile, shape(2, LANES)], [VMEM] * 5
-    )(coords, atom_types, cheb_cur, cheb_prev, send_x)
+    whole = (coords, atom_types, cheb_cur, cheb_prev, send_x, send_y)
+    pack, sent, tail = call(
+        field_body,
+        [shape(24, LANES), tile, shape(40, LANES)],
+        [pl.BlockSpec(memory_space=pltpu.HBM)] * 7,
+        [pltpu.VMEM(x.shape, x.dtype) for x in whole]
+        + [pltpu.SMEM(spectrum.shape, F32), pltpu.SemaphoreType.DMA((7,))],
+        limit=None,
+    )(*whole, spectrum)
     lower, upper = shifted(sent, "gx")
+    pack = call(hold_body, shape(24, LANES), [VMEM], flops=4_000_000)(pack)
     ws, wst, hid, hidt, cols, nbt = call(
         params_body,
         [
@@ -480,14 +512,18 @@
         [pltpu.VMEM((16, HALF), F32), pltpu.VMEM((128, LANES), F32), pltpu.VMEM((256, LANES), F32), pltpu.VMEM((128, 128), F32)],
         flops=20_000_000,
     )(poly_table, fit_in, fit_hidden, fit_bias, fit_out, neighbours)
-    ghost, sent = call(first_body, [tile, tile], [VMEM] * 4)(field, lower, upper, send_y)
+    ghost, sent = call(first_body, [tile, tile], [VMEM] * 3)(pack, lower, upper)
     lower, upper = shifted(sent, "gy")
-    terms, share = call(
+    near = call(
+        functools.partial(near_body, slots), shape(16, slots, LANES), [VMEM] * 3, flops=20_000_000
+    )(pack, ghost, nbt)
+    accum, share = call(
         functools.partial(pair_body, entries, slots),
-        [shape(slots * 16, LANES), shape(devices, LANES)],
-        [SMEM] + [VMEM] * 11,
+        [shape(3, 16, LANES), shape(devices, LANES)],
+        [VMEM] * 10,
         [
-            pltpu.VMEM((3, 16, LANES), F32),
+            pltpu.VMEM((slots * 16, LANES), F32),
+            pltpu.VMEM((16, LANES), F32),
             pltpu.VMEM((17, slots, LANES), F32),
             pltpu.VMEM((6, slots, LANES), F32),
             pltpu.VMEM((20 * 128, LANES), F32),
@@ -497,21 +533,15 @@
             pltpu.VMEM((20, 16, LANES), F32),
         ],
         flops=40_000_000,
-        limit=32 << 20,
-    )(spectrum, field, ghost, lower, upper, nbt, ws, wst, hid, hidt, cols, sums)
+    )(pack, near, lower, upper, nbt, ws, wst, hid, hidt, cols)
+    below, above = shifted(accum[2], "gy")
     shares = lax.all_to_all(share, ("gx", "gy"), 0, 0)
-    accum = call(
-        functools.partial(scatter_body, slots), shape(3, 16, LANES), [VMEM] * 2, flops=40_000_000
-    )(terms, nbt)
-    below, above = shifted(accum[2], "gy")
-    own, ghost = call(fold_body, [tile, tile], [VMEM] * 4)(accum, below, above, send_y)
+    own, ghost = call(fold_body, [tile, tile], [VMEM] * 4, flops=1000000000)(accum, below, above, pack)
     below, above = shifted(ghost, "gx")
     return tuple(
         call(
-            last_body,
-            [shape(*coords.shape), shape(*cheb_cur.shape), shape(2, 4)],
-            [SMEM] + [VMEM] * 8,
-        )(spectrum, own, below, above, send_x, atom_types, cheb_cur, cheb_prev, shares)
+            last_body, [shape(*coords.shape), shape(*cheb_cur.shape), shape(2, 4)], [VMEM] * 5
+        )(own, below, above, tail, shares)
     )
 
 

time: 67.4 us -> 43.2 us (0.64)
  Pallas kernels: 25.7 us -> 14.1 us
  local copies, waits for them, and re-layouts: 10.1 us -> 2.58 us
  waiting for transfers between devices: 16.5 us -> 11 us
  starting transfers between devices: 13.8 us -> 14.5 us
    pallas_call x5 -> x6, Pallas kernels: 21.7 us -> 12.7 us  [the longest x1 9.71 us: local(): call(functools.partial(pair_body, entries, slots), [shape(3, 16, LANES),...]
    unnamed x39 -> x17, local copies, waits for them, and re-layouts: 9.35 us -> 2.58 us
    ppermute x8, waiting for transfers between devices: 16.5 us -> 10.5 us  [shifted(): return (lax.ppermute(x, axis, up), lax.ppermute(x, axis, down))]
    pallas_call x1, Pallas kernels: 2.39 us -> 0.64 us  [local(): call(params_body, [shape(256, LANES), shape(LANES, 256), shape(2, 2, 128,...]
    all_to_all x1, starting transfers between devices: 2.51 us -> 4.19 us  [local(): shares = lax.all_to_all(share, ('gx', 'gy'), 0, 0)]
    ppermute x8, starting transfers between devices: 11.3 us -> 10.3 us  [shifted(): return (lax.ppermute(x, axis, up), lax.ppermute(x, axis, down))]
    pallas_call x1, Pallas kernels: 1.67 us -> 0.76 us  [local(): call(last_body, [shape(*coords.shape), shape(*cheb_cur.shape), shape(2, 4...]
    squeeze x1, local copies, waits for them, and re-layouts: 0.7 us -> 0.01 us  [local(): below, above = shifted(accum[2], 'gy')]
  transfers between devices with their start and end apart: 9 -> 9, of which waited for: 7 -> 7; matrix products, arithmetic and copies ran while one was open for 2% -> 0% of each run, Pallas kernels for 6% -> 4%
where the time goes in v2:
time: 43.2 us; the launch traced here: 42.9 us
  starting transfers between devices  14.5 us (34%)
  Pallas kernels  14.1 us (33%)
  waiting for transfers between devices  11 us (25%)
  local copies, waits for them, and re-layouts  2.58 us (6%)
  between operations  0.73 us (2%)
    ppermute x8, waiting for transfers between devices, shifted(): return (lax.ppermute(x, axis, up), lax.ppermute(x, axis, down))  10.5 us
    ppermute x8, starting transfers between devices, shifted(): return (lax.ppermute(x, axis, up), lax.ppermute(x, axis, down))  10.3 us
    pallas_call x1, Pallas kernels, local(): call(functools.partial(pair_body, entries, slots), [shape(3, 16, LANES),...  9.71 us
    all_to_all x1, starting transfers between devices, local(): shares = lax.all_to_all(share, ('gx', 'gy'), 0, 0)  4.19 us
    unnamed x17, local copies, waits for them, and re-layouts  2.58 us
    pallas_call x1, Pallas kernels, local(): call(field_body, [shape(24, LANES), tile, shape(40, LANES)], [pl.BlockSpe...  1.61 us
    pallas_call x1, Pallas kernels, local(): call(functools.partial(near_body, slots), shape(16, slots, LANES), [VMEM]...  1.14 us
  transfers between devices with their start and end apart: 9, of which 7 were waited for; matrix products, arithmetic and copies ran while one was open for 0% of the time, Pallas kernels for 4%

profile of v2, /device:TPU:0, one launch (start us, length us, event | category | flops | bytes accessed | tf_op | source)
XLA Modules:
  0.0 42.9 jit_solution(11614014917915102215)
XLA Ops:
  0.6 0.0 copy-start.2
  0.6 1.6 %shard_map.148 = (f32[24,128]{1,0:T(8,128)}, f32[16,128]{1,0:T(8,128)}, f32[40,128]{1,0:T(8,128)}) custom-call(f32[3,1,1,128]{3,2,1,0:T(1,128)} %coords_hbm.1, s32[1,1,128]{2,1,0:T(1,128)} %types_hbm.1, f32[4,3,1,1,128]{4,3,2,1,0:T(1,128)} %cur_hbm.1, f32[4,3,1,1,128]{4,3,2,1,0:T(1,128)} %prev_hbm.1, s32[1,1,2,64]{3,2,1,0:T(2,128)} %send_x_hbm.1, ...), custom_call_target="tpu_custom_call" | custom-call | bytes 65536 | tf_op jit(solution)/shard_map/pallas_call | solution.py:495
  2.3 3.4 %collective-permute-start.1 = (f32[16,128]{1,0:T(8,128)}, f32[16,128]{1,0:T(8,128)S(1)}, u32[]{:S(2)}, u32[]{:S(2)}) collective-permute-start(f32[16,128]{1,0:T(8,128)} %get-tuple-element.19), channel_id=1, source_target_pairs={{4,0},{8,4},{12,8},{16,12},{20,16},{24,20},{28,24},{0,28},{5,1},{9... | collective-permute-start | bytes 24584 | tf_op jit(solution)/shard_map/ppermute | solution.py:482
  5.6 0.0 collective-permute-start
  5.6 0.0 copy-start.4
  5.6 0.7 %copy-done.4 = f32[24,128]{1,0:T(8,128)S(1)} copy-done((f32[24,128]{1,0:T(8,128)S(1)}, f32[24,128]{1,0:T(8,128)}, u32[]{:S(2)}) %copy-start.4) | copy-done | bytes 12312
  6.4 0.9 %collective-permute-done.1.upper_ref = f32[16,128]{1,0:T(8,128)S(1)} collective-permute-done((f32[16,128]{1,0:T(8,128)}, f32[16,128]{1,0:T(8,128)S(1)}, u32[]{:S(2)}, u32[]{:S(2)}) %collective-permute-start.1) | collective-permute-done | bytes 8224 | tf_op jit(solution)/shard_map/ppermute | solution.py:482
  7.2 2.6 %collective-permute-done.lower_ref = f32[16,128]{1,0:T(8,128)S(1)} collective-permute-done((f32[16,128]{1,0:T(8,128)}, f32[16,128]{1,0:T(8,128)S(1)}, u32[]{:S(2)}, u32[]{:S(2)}) %collective-permute-start) | collective-permute-done | bytes 8224 | tf_op jit(solution)/shard_map/ppermute | solution.py:482
  9.8 0.0 copy-start.7
  9.8 0.1 shard_map.150
  9.9 0.0 copy-start.5
  9.9 0.0 copy-start.6
  9.9 3.6 %collective-permute-start.3 = (f32[16,128]{1,0:T(8,128)S(1)}, f32[16,128]{1,0:T(8,128)S(1)}, u32[]{:S(2)}, u32[]{:S(2)}) collective-permute-start(f32[16,128]{1,0:T(8,128)S(1)} %get-tuple-element.22), channel_id=1, source_target_pairs={{1,0},{2,1},{3,2},{0,3},{5,4},{6,5},{7,6},{4,7},{9,8},{10,9},{11,1... | collective-permute-start | bytes 24584 | tf_op jit(solution)/shard_map/ppermute | solution.py:482
  13.5 0.0 collective-permute-start.2
  13.5 0.0 copy-done.7
  13.5 0.0 copy-done.2
  13.5 0.0 copy-done.5
  13.5 0.0 copy-done.6
  13.6 0.0 copy-start
  13.6 0.9 %copy-done = f32[512,128]{1,0:T(8,128)S(1)} copy-done((f32[512,128]{1,0:T(8,128)S(1)}, f32[512,128]{1,0:T(8,128)}, u32[]{:S(2)}) %copy-start) | copy-done | bytes 262168
  14.5 0.0 copy-start.1
  14.5 0.9 %copy-done.1 = f32[2,128,128]{2,1,0:T(8,128)S(1)} copy-done((f32[2,128,128]{2,1,0:T(8,128)S(1)}, f32[2,128,128]{2,1,0:T(8,128)}, u32[]{:S(2)}) %copy-start.1) | copy-done | bytes 131096
  15.4 0.6 %shard_map.151 = (f32[256,128]{1,0:T(8,128)S(1)}, f32[128,256]{1,0:T(8,128)S(1)}, bf16[2,2,128,128]{3,2,1,0:T(8,128)(2,1)S(1)}, bf16[2,2,128,128]{3,2,1,0:T(8,12...) custom-call(f32[2,6,64]{2,1,0:T(8,128)S(1)} %copy.17.poly_ref, f32[512,128]{1,0:T(8,128)S(1)} %copy-done, ...), custom_call_target="tpu_custom_call" | custom-call | flops 20000000 | bytes 65536 | tf_op jit(solution)/shard_map/pallas_call | solution.py:505
  16.1 1.1 %shard_map.152.near_ref = f32[16,128,128]{2,1,0:T(8,128)S(1)} custom-call(f32[24,128]{1,0:T(8,128)S(1)} %shard_map.149.pack_ref, f32[16,128]{1,0:T(8,128)S(1)} %get-tuple-element.20.ghost_ref, s32[128,128]{1,0:T(8,128)S(1)} %get-tuple-element.21.nbt_ref), custom_call_target="tpu_custom_call" | custom-call | flops 20000000 | bytes 65536 | tf_op jit(solution)/shard_map/pallas_call | solution.py:517
  17.2 0.0 collective-permute-done.3.upper_ref
  17.2 1.8 %collective-permute-done.2.lower_ref = f32[16,128]{1,0:T(8,128)S(1)} collective-permute-done((f32[16,128]{1,0:T(8,128)S(1)}, f32[16,128]{1,0:T(8,128)S(1)}, u32[]{:S(2)}, u32[]{:S(2)}) %collective-permute-start.2) | collective-permute-done | bytes 8224 | tf_op jit(solution)/shard_map/ppermute | solution.py:482
  19.0 9.7 %shard_map.153 = (f32[3,16,128]{2,1,0:T(8,128)S(1)}, f32[32,128]{1,0:T(8,128)}) custom-call(f32[24,128]{1,0:T(8,128)S(1)} %shard_map.149.pack_ref, f32[16,128,128]{2,1,0:T(8,128)S(1)} %shard_map.152.near_ref, f32[16,128]{1,0:T(8,128)S(1)} %collective-permute-done.2.lower_ref, f32[16,128]{1,0:T(8,128)S(1)} %collective-permute-done.3.upper_ref, ...), custom_call_target="tpu_custom_call" | custom-call | flops 40000000 | bytes 65536 | tf_op jit(solution)/shard_map/pallas_call | solution.py:520
  28.7 2.1 %collective-permute-start.5 = (f32[16,128]{1,0:T(8,128)S(1)}, f32[16,128]{1,0:T(8,128)S(1)}, u32[]{:S(2)}, u32[]{:S(2)}) collective-permute-start(f32[16,128]{1,0:T(8,128)S(1)} %slice_bitcast_fusion), channel_id=1, source_target_pairs={{1,0},{2,1},{3,2},{0,3},{5,4},{6,5},{7,6},{4,7},{9,8},{10,9},{11,1... | collective-permute-start | bytes 24584 | tf_op jit(solution)/shard_map/ppermute | solution.py:482
  30.7 0.0 collective-permute-start.4
  30.7 4.2 %all-to-all-start = ((f32[32,1,128]{2,1,0:T(1,128)}), f32[32,1,128]{2,1,0:T(1,128)S(1)}, u32[]{:S(2)}, u32[]{:S(2)}) async-start(f32[32,1,128]{2,1,0:T(1,128)} %bitcast.2), calls=%async_computation | async-start | bytes 32768 | tf_op jit(solution)/shard_map/all_to_all | solution.py:538
  34.9 0.0 collective-permute-done.5.above_ref
  35.0 1.2 %collective-permute-done.4.below_ref = f32[16,128]{1,0:T(8,128)S(1)} collective-permute-done((f32[16,128]{1,0:T(8,128)S(1)}, f32[16,128]{1,0:T(8,128)S(1)}, u32[]{:S(2)}, u32[]{:S(2)}) %collective-permute-start.4) | collective-permute-done | bytes 8224 | tf_op jit(solution)/shard_map/ppermute | solution.py:482
  36.2 0.0 copy-start.3
  36.2 0.1 shard_map.154
  36.3 1.2 %collective-permute-start.7 = (f32[16,128]{1,0:T(8,128)S(1)}, f32[16,128]{1,0:T(8,128)S(1)}, u32[]{:S(2)}, u32[]{:S(2)}) collective-permute-start(f32[16,128]{1,0:T(8,128)S(1)} %get-tuple-element.30), channel_id=1, source_target_pairs={{4,0},{8,4},{12,8},{16,12},{20,16},{24,20},{28,24},{0,28},{5,1},{9... | collective-permute-start | bytes 24584 | tf_op jit(solution)/shard_map/ppermute | solution.py:482
  37.6 0.0 collective-permute-start.6
  37.6 1.4 %collective-permute-done.7.above_ref = f32[16,128]{1,0:T(8,128)S(1)} collective-permute-done((f32[16,128]{1,0:T(8,128)S(1)}, f32[16,128]{1,0:T(8,128)S(1)}, u32[]{:S(2)}, u32[]{:S(2)}) %collective-permute-start.7) | collective-permute-done | bytes 8224 | tf_op jit(solution)/shard_map/ppermute | solution.py:482
  38.9 2.6 %collective-permute-done.6.below_ref = f32[16,128]{1,0:T(8,128)S(1)} collective-permute-done((f32[16,128]{1,0:T(8,128)S(1)}, f32[16,128]{1,0:T(8,128)S(1)}, u32[]{:S(2)}, u32[]{:S(2)}) %collective-permute-start.6) | collective-permute-done | bytes 8224 | tf_op jit(solution)/shard_map/ppermute | solution.py:482
  41.5 0.6 %all-to-all-done = f32[32,1,128]{2,1,0:T(1,128)S(1)} async-done(((f32[32,1,128]{2,1,0:T(1,128)}), f32[32,1,128]{2,1,0:T(1,128)S(1)}, u32[]{:S(2)}, u32[]{:S(2)}) %all-to-all-start) | async-done | bytes 16416 | tf_op jit(solution)/shard_map/all_to_all | solution.py:538
  42.1 0.0 copy-done.3
  42.1 0.8 %shard_map.155 = (f32[3,1,1,128]{3,2,1,0:T(1,128)}, f32[4,3,1,1,128]{4,3,2,1,0:T(1,128)}, f32[2,4]{1,0:T(2,128)}) custom-call(f32[16,128]{1,0:T(8,128)S(1)} %get-tuple-element.29.own_ref, f32[16,128]{1,0:T(8,128)S(1)} %collective-permute-done.6.below_ref, f32[16,128]{1,0:T(8,128)S(1)} %collective-permute-done.7.above_ref, f32[40,128]{1,0:T(8,128)S(1)} %copy-done.3, ...), custom_call_target="tpu_custom_call" | custom-call | bytes 65536 | tf_op jit(solution)/shard_map/pallas_call | solution.py:542
  (3 shorter events, 0.0 us)
Async XLA Ops:
  0.6 12.9 %copy-start.2 = (s32[1,1,128,128]{3,2,1,0:T(8,128)S(1)}, s32[1,1,128,128]{3,2,1,0:T(8,128)}, u32[]{:S(2)}) copy-start(s32[1,1,128,128]{3,2,1,0:T(8,128)} %nb_ref.1) | copy-start | bytes 196612
  2.3 5.0 %collective-permute-start.1 = (f32[16,128]{1,0:T(8,128)}, f32[16,128]{1,0:T(8,128)S(1)}, u32[]{:S(2)}, u32[]{:S(2)}) collective-permute-start(f32[16,128]{1,0:T(8,128)} %get-tuple-element.19), channel_id=1, source_target_pairs={{4,0},{8,4},{12,8},{16,12},{20,16},{24,20},{28,24},{0,28},{5,1},{9... | collective-permute-start | bytes 24584 | tf_op jit(solution)/shard_map/ppermute | solution.py:482
  5.6 4.2 %collective-permute-start = (f32[16,128]{1,0:T(8,128)}, f32[16,128]{1,0:T(8,128)S(1)}, u32[]{:S(2)}, u32[]{:S(2)}) collective-permute-start(f32[16,128]{1,0:T(8,128)} %get-tuple-element.19), channel_id=1, source_target_pairs={{0,4},{4,8},{8,12},{12,16},{16,20},{20,24},{24,28},{28,0},{1,5},{5... | collective-permute-start | bytes 24584 | tf_op jit(solution)/shard_map/ppermute | solution.py:482
  5.6 0.7 %copy-start.4 = (f32[24,128]{1,0:T(8,128)S(1)}, f32[24,128]{1,0:T(8,128)}, u32[]{:S(2)}) copy-start(f32[24,128]{1,0:T(8,128)} %get-tuple-element.18.pack_ref) | copy-start | bytes 36868
  9.8 3.7 %copy-start.7 = (f32[2,6,64]{2,0,1:T(2,128)S(1)}, f32[2,6,64]{2,0,1:T(2,128)}, u32[]{:S(2)}) copy-start(f32[2,6,64]{2,0,1:T(2,128)} %param.18) | copy-start | bytes 9220
  9.9 3.6 %copy-start.5 = (f32[3,128]{1,0:T(4,128)S(1)}, f32[3,128]{1,0:T(4,128)}, u32[]{:S(2)}) copy-start(f32[3,128]{1,0:T(4,128)} %bias_ref.1) | copy-start | bytes 4612
  9.9 3.6 %copy-start.6 = (f32[128]{0:T(128)S(1)}, f32[128]{0:T(128)}, u32[]{:S(2)}) copy-start(f32[128]{0:T(128)} %out_ref.1) | copy-start | bytes 1540
  9.9 7.3 %collective-permute-start.3 = (f32[16,128]{1,0:T(8,128)S(1)}, f32[16,128]{1,0:T(8,128)S(1)}, u32[]{:S(2)}, u32[]{:S(2)}) collective-permute-start(f32[16,128]{1,0:T(8,128)S(1)} %get-tuple-element.22), channel_id=1, source_target_pairs={{1,0},{2,1},{3,2},{0,3},{5,4},{6,5},{7,6},{4,7},{9,8},{10,9},{11,1... | collective-permute-start | bytes 24584 | tf_op jit(solution)/shard_map/ppermute | solution.py:482
  13.5 5.4 %collective-permute-start.2 = (f32[16,128]{1,0:T(8,128)S(1)}, f32[16,128]{1,0:T(8,128)S(1)}, u32[]{:S(2)}, u32[]{:S(2)}) collective-permute-start(f32[16,128]{1,0:T(8,128)S(1)} %get-tuple-element.22), channel_id=1, source_target_pairs={{0,1},{1,2},{2,3},{3,0},{4,5},{5,6},{6,7},{7,4},{8,9},{9,10},{10,1... | collective-permute-start | bytes 24584 | tf_op jit(solution)/shard_map/ppermute | solution.py:482
  13.6 1.0 %copy-start = (f32[512,128]{1,0:T(8,128)S(1)}, f32[512,128]{1,0:T(8,128)}, u32[]{:S(2)}) copy-start(f32[512,128]{1,0:T(8,128)} %fit_ref.1) | copy-start | bytes 786436
  14.5 0.9 %copy-start.1 = (f32[2,128,128]{2,1,0:T(8,128)S(1)}, f32[2,128,128]{2,1,0:T(8,128)}, u32[]{:S(2)}) copy-start(f32[2,128,128]{2,1,0:T(8,128)} %hidden_ref.1) | copy-start | bytes 393220
  28.7 6.3 %collective-permute-start.5 = (f32[16,128]{1,0:T(8,128)S(1)}, f32[16,128]{1,0:T(8,128)S(1)}, u32[]{:S(2)}, u32[]{:S(2)}) collective-permute-start(f32[16,128]{1,0:T(8,128)S(1)} %slice_bitcast_fusion), channel_id=1, source_target_pairs={{1,0},{2,1},{3,2},{0,3},{5,4},{6,5},{7,6},{4,7},{9,8},{10,9},{11,1... | collective-permute-start | bytes 24584 | tf_op jit(solution)/shard_map/ppermute | solution.py:482
  30.7 5.4 %collective-permute-start.4 = (f32[16,128]{1,0:T(8,128)S(1)}, f32[16,128]{1,0:T(8,128)S(1)}, u32[]{:S(2)}, u32[]{:S(2)}) collective-permute-start(f32[16,128]{1,0:T(8,128)S(1)} %slice_bitcast_fusion), channel_id=1, source_target_pairs={{0,1},{1,2},{2,3},{3,0},{4,5},{5,6},{6,7},{7,4},{8,9},{9,10},{10,1... | collective-permute-start | bytes 24584 | tf_op jit(solution)/shard_map/ppermute | solution.py:482
  30.7 11.4 %all-to-all-start = ((f32[32,1,128]{2,1,0:T(1,128)}), f32[32,1,128]{2,1,0:T(1,128)S(1)}, u32[]{:S(2)}, u32[]{:S(2)}) async-start(f32[32,1,128]{2,1,0:T(1,128)} %bitcast.2), calls=%async_computation | async-start | bytes 32768 | tf_op jit(solution)/shard_map/all_to_all | solution.py:538
  36.2 5.9 %copy-start.3 = (f32[40,128]{1,0:T(8,128)S(1)}, f32[40,128]{1,0:T(8,128)}, u32[]{:S(2)}) copy-start(f32[40,128]{1,0:T(8,128)} %get-tuple-element.31.tail_ref) | copy-start | bytes 61444
  36.3 2.6 %collective-permute-start.7 = (f32[16,128]{1,0:T(8,128)S(1)}, f32[16,128]{1,0:T(8,128)S(1)}, u32[]{:S(2)}, u32[]{:S(2)}) collective-permute-start(f32[16,128]{1,0:T(8,128)S(1)} %get-tuple-element.30), channel_id=1, source_target_pairs={{4,0},{8,4},{12,8},{16,12},{20,16},{24,20},{28,24},{0,28},{5,1},{9... | collective-permute-start | bytes 24584 | tf_op jit(solution)/shard_map/ppermute | solution.py:482
  37.6 4.0 %collective-permute-start.6 = (f32[16,128]{1,0:T(8,128)S(1)}, f32[16,128]{1,0:T(8,128)S(1)}, u32[]{:S(2)}, u32[]{:S(2)}) collective-permute-start(f32[16,128]{1,0:T(8,128)S(1)} %get-tuple-element.30), channel_id=1, source_target_pairs={{0,4},{4,8},{8,12},{12,16},{16,20},{20,24},{24,28},{28,0},{1,5},{5... | collective-permute-start | bytes 24584 | tf_op jit(solution)/shard_map/ppermute | solution.py:482

commit v3 on v2

--- a/solution.py
+++ b/solution.py
@@ -48,6 +48,12 @@
 
 def dot3(a, b, contract=((1,), (0,))):
     return dot(a[0], b[0], contract) + (dot(a[0], b[1], contract) + dot(a[1], b[0], contract))
+
+
+def deep_dot3(weights, x):
+    high, low = halves(x)
+    twice = jnp.concatenate([weights[0], weights[0]], axis=1)
+    return dot(twice, jnp.concatenate([high, low], axis=0)) + dot(weights[1], high)
 
 
 def lane_take(row, index):
@@ -94,8 +100,8 @@
 
 def params_body(
     poly_ref, fit_ref, hidden_ref, bias_ref, out_ref, nb_ref,
-    ws_ref, wst_ref, hid_ref, hidt_ref, cols_ref, nbt_ref,
-    table, mixed, square, columns,
+    form_ref, back_ref, hid_ref, hidt_ref, cols_ref, nbt_ref,
+    table, mixed, square, columns, even,
 ):
     table[...] = jnp.zeros_like(table)
     table[0:6, :] = poly_ref[0]
@@ -110,11 +116,18 @@
         block = mixed[k * M2 : (k + 1) * M2, :]
         square[k * 16 : (k + 1) * 16, :] = dot3(axis_features, halves(block))
     for k in range(12):
-        block = square[k * 16 : (k + 1) * 16, :] + square[pl.ds(k, 16, stride=16), :]
-        ws_ref[k * 16 : (k + 1) * 16, :] = 0.5 * block
-    ws_ref[192:256, :] = jnp.zeros((64, LANES), F32)
-    wst_ref[:, 0:128] = ws_ref[0:128, :].T
-    wst_ref[:, 128:256] = ws_ref[128:256, :].T
+        block = 0.5 * (square[k * 16 : (k + 1) * 16, :] + square[pl.ds(k, 16, stride=16), :])
+        high, low = halves(block)
+        back_ref[0, k * 16 : (k + 1) * 16, :] = high
+        back_ref[1, k * 16 : (k + 1) * 16, :] = low
+        if k < 8:
+            even[k * 8 : (k + 1) * 8, :] = block[0:8]
+        else:
+            even[k * 8 : (k + 1) * 8, :] = 2.0 * block[0:8]
+            even[(k + 4) * 8 : (k + 5) * 8, :] = block[8:16]
+    high, low = halves(even[...].T)
+    form_ref[0] = high
+    form_ref[1] = low
     for layer in range(2):
         high, low = halves(hidden_ref[layer])
         hid_ref[layer, 0] = high
@@ -183,7 +196,7 @@
     held_ref[...] = pack_ref[...]
 
 
-def first_body(pack_ref, lower_ref, upper_ref, ghost_ref, sent_ref):
+def first_body(pack_ref, upper_ref, lower_ref, ghost_ref, sent_ref):
     ghost = joined(lower_ref[...], upper_ref[...], 0)
     ghost_ref[...] = ghost
     sent_ref[...] = take_columns([pack_ref[0:16, :], ghost], pack_ref[16:17, :].astype(jnp.int32))
@@ -206,8 +219,8 @@
 
 def pair_body(
     entries, slots,
-    pack_ref, near_ref, lower_ref, upper_ref, nbt_ref,
-    ws_ref, wst_ref, hid_ref, hidt_ref, cols_ref,
+    pack_ref, near_ref, upper_ref, lower_ref, nbt_ref,
+    form_ref, back_ref, hid_ref, hidt_ref, cols_ref,
     accum_ref, share_ref,
     terms_ref, far, pair, power, moment, gee, form, back, lam,
 ):
@@ -239,7 +252,7 @@
             value = value * switch
         return carry
 
-    lax.fori_loop(0, groups, gather, 0, unroll=2)
+    lax.fori_loop(0, groups, gather, 0, unroll=16)
 
     zero = jnp.zeros((SUBLANES, LANES), F32)
 
@@ -273,7 +286,7 @@
                     totals[place * 12 + 6 + k] += near * term
             return tuple(totals)
 
-        totals = lax.fori_loop(0, groups, body, (zero,) * (12 * len(parts)), unroll=4)
+        totals = lax.fori_loop(0, groups, body, (zero,) * (12 * len(parts)), unroll=16)
         for place, c in enumerate(parts):
             for k in range(12):
                 row = ((w * 4 + c) * 16 + k) * SUBLANES
@@ -289,13 +302,28 @@
             total += moment[pl.ds(block * 128 + sub, 16, stride=SUBLANES), :]
         gee[block] = total * (1.0 / slots)
 
-    for k in range(12):
-        for w in range(5):
-            total = gee[w * 4] * gee[0, k : k + 1, :]
+    for w in range(5):
+        def product(k, rows):
+            total = gee[w * 4, rows, :] * gee[0, k : k + 1, :]
             for c in range(1, 4):
-                total += gee[w * 4 + c] * gee[c, k : k + 1, :]
-            form[k * 16 : (k + 1) * 16, w * LANES : (w + 1) * LANES] = total if w == 0 else total * 2.0
-    form[192:256, :] = jnp.zeros((64, 5 * LANES), F32)
+                total += gee[w * 4 + c, rows, :] * gee[c, k : k + 1, :]
+            return total
+
+        def swapped(k, rows):
+            total = gee[0, rows, :] * gee[w * 4, k : k + 1, :]
+            for c in range(1, 4):
+                total += gee[c, rows, :] * gee[w * 4 + c, k : k + 1, :]
+            return total
+
+        upper_rows, lower_rows = slice(0, 8), slice(8, 16)
+        for k in range(12):
+            block = product(k, upper_rows)
+            if w:
+                block = block + (swapped(k, upper_rows) if k >= 8 else block)
+            form[k * 8 : (k + 1) * 8, w * LANES : (w + 1) * LANES] = block
+            if k >= 8:
+                block = product(k, lower_rows)
+                form[(k + 4) * 8 : (k + 5) * 8, w * LANES : (w + 1) * LANES] = block * 2.0 if w else block
 
     def wide(column):
         return jnp.broadcast_to(column, (LANES, LANES))
@@ -308,26 +336,28 @@
         slope = 1.0 - bent * bent
         return bent, slope
 
-    pre1 = dot3(halves(wst_ref[...]), halves(form[...]))
+    pre1 = deep_dot3((form_ref[0], form_ref[1]), form[...])
     bent1, slope1 = layer(pre1, cols_ref[:, 0:1])
     hidden1 = [bent1] + [slope1 * cut(pre1, w) for w in range(1, 5)]
-    pre2 = dot3((hidt_ref[0, 0], hidt_ref[0, 1]), halves(jnp.concatenate(hidden1, axis=1)))
+    pre2 = deep_dot3((hidt_ref[0, 0], hidt_ref[0, 1]), jnp.concatenate(hidden1, axis=1))
     bent2, slope2 = layer(pre2, cols_ref[:, 1:2])
     hidden2 = [bent2 + hidden1[0]] + [slope2 * cut(pre2, w) + hidden1[w] for w in range(1, 5)]
-    pre3 = dot3((hidt_ref[1, 0], hidt_ref[1, 1]), halves(jnp.concatenate(hidden2, axis=1)))
+    pre3 = deep_dot3((hidt_ref[1, 0], hidt_ref[1, 1]), jnp.concatenate(hidden2, axis=1))
     bent3, slope3 = layer(pre3, cols_ref[:, 2:3])
     out = wide(cols_ref[:, 3:4])
     adj3 = [out * slope3] + [(-2.0 * out * bent3 * slope3) * cut(pre3, w) for w in range(1, 5)]
-    up2 = dot3((hid_ref[1, 0], hid_ref[1, 1]), halves(jnp.concatenate(adj3, axis=1)))
+    up2 = deep_dot3((hid_ref[1, 0], hid_ref[1, 1]), jnp.concatenate(adj3, axis=1))
     up2 = [cut(up2, 0) + out] + [cut(up2, w) for w in range(1, 5)]
     bend2 = -2.0 * up2[0] * bent2 * slope2
     adj2 = [up2[0] * slope2] + [up2[w] * slope2 + bend2 * cut(pre2, w) for w in range(1, 5)]
-    up1 = dot3((hid_ref[0, 0], hid_ref[0, 1]), halves(jnp.concatenate(adj2, axis=1)))
+    up1 = deep_dot3((hid_ref[0, 0], hid_ref[0, 1]), jnp.concatenate(adj2, axis=1))
     up1 = [cut(up1, w) + up2[w] for w in range(5)]
     bend1 = -2.0 * up1[0] * bent1 * slope1
     adj1 = [up1[0] * slope1] + [up1[w] * slope1 + bend1 * cut(pre1, w) for w in range(1, 5)]
-    back[...] = dot3(halves(ws_ref[...]), halves(jnp.concatenate(adj1, axis=1)))
-
+    back[...] = deep_dot3((back_ref[0], back_ref[1]), jnp.concatenate(adj1, axis=1))
+
+    rows = lax.broadcasted_iota(jnp.int32, (16, LANES), 0)
+    degree = jnp.where(rows < 6, rows + 1, rows - 5).astype(F32)
     for c in range(4):
         totals = [None] * 5
         for k in range(12):
@@ -341,7 +371,8 @@
                     term = back[rows, w * LANES : (w + 1) * LANES] * plain + base * gee[w * 4 + c, k : k + 1, :]
                 totals[w] = term if k == 0 else totals[w] + term
         for w in range(5):
-            lam[w * 4 + c] = totals[w] * (2.0 / slots)
+            total = totals[w] * (2.0 / slots)
+            lam[w * 4 + c] = total * degree if c == 0 else total
             lam[w * 4 + c, 6:12, :] = lam[w * 4 + c, 0:6, :] + lam[w * 4 + c, 6:12, :]
 
     def push(group, quad):
@@ -362,21 +393,31 @@
                 for k in range(6)
             ]
 
-        def poly(values):
-            total = values[5]
+        switch2 = switch * switch
+        switch3 = switch2 * switch
+
+        def horner(values, order):
+            total, first, second = values[5], None, None
             for k in range(4, -1, -1):
+                if order > 1 and first is not None:
+                    second = first if second is None else second * switch + first
+                if order > 0:
+                    first = total if first is None else first * switch + total
                 total = total * switch + values[k]
-            return total * switch
+            return total, first, second
 
         def store(row, value):
             terms_ref[pl.ds(start * 16 + row, SUBLANES, stride=16), :] = value
 
-        plain, first, second = [], [], []
-        for c in range(4):
-            values = coefficients(0, c)
-            plain.append(poly(values) if c else None)
-            first.append(poly([values[k] * (k + 1.0) for k in range(6)]))
-            second.append(poly([values[k] * ((k + 1.0) * (k + 1.0)) for k in range(6)]))
+        total, slope, _ = horner(coefficients(0, 0), 1)
+        plain, first, second = [None], [switch * total], [switch * total + switch2 * slope]
+        for c in range(1, 4):
+            total, slope, bow = horner(coefficients(0, c), 2)
+            total = switch * total
+            slope = switch2 * slope
+            plain.append(total)
+            first.append(total + slope)
+            second.append(total + 3.0 * slope + (2.0 * switch3) * bow)
 
         def along(values):
             return values[1] * unit[0] + values[2] * unit[1] + values[3] * unit[2]
@@ -395,10 +436,14 @@
             + 3.0 * square * square * plain_along
         )
         for w in range(1, 5):
-            values = [coefficients(w, c) for c in range(4)]
-            p = [None] + [poly(values[c]) for c in range(1, 4)]
-            f = [poly([values[c][k] * (k + 1.0) for k in range(6)]) for c in range(4)]
-            down = -(alpha * (f[0] + along(f)) + square * along(p))
+            f0 = switch * horner(coefficients(w, 0), 0)[0]
+            p, slopes = [None], [None]
+            for c in range(1, 4):
+                total, slope, _ = horner(coefficients(w, c), 1)
+                p.append(switch * total)
+                slopes.append(slope)
+            p_along = along(p)
+            down = -(alpha * (f0 + p_along + switch2 * along(slopes)) + square * p_along)
             v = [pair[1 + 3 * w + a, at, :] for a in range(3)]
             s = d[0] * v[0] + d[1] * v[1] + d[2] * v[2]
             t = s * curl + (bend[0] * v[0] + bend[1] * v[1] + bend[2] * v[2]) + down
@@ -425,7 +470,7 @@
 
 
 def scatter_columns(slots, terms_ref, nbt_ref):
-    per = 32
+    per = 128
     places = lax.broadcasted_iota(jnp.int32, (LANES, LANES), 0)
 
     def body(group, carry):
@@ -450,7 +495,7 @@
     return lax.fori_loop(0, slots // per, body, start)
 
 
-def fold_body(accum_ref, below_ref, above_ref, pack_ref, own_ref, ghost_ref):
+def fold_body(accum_ref, above_ref, below_ref, pack_ref, own_ref, ghost_ref):
     values = jnp.where(lane_number(16) < HALF, above_ref[...], below_ref[...])
     added = add_columns(values, pack_ref[16:17, :].astype(jnp.int32), 2 * LANES)
     own_ref[...] = accum_ref[0] + added[:, 0:LANES]
@@ -458,7 +503,7 @@
 
 
 def last_body(
-    own_ref, below_ref, above_ref, tail_ref, shares_ref,
+    own_ref, above_ref, below_ref, tail_ref, shares_ref,
     forces_ref, next_ref, moments_ref,
 ):
     values = jnp.where(lane_number(16) < HALF, above_ref[...], below_ref[...])
@@ -502,17 +547,17 @@
     )(*whole, spectrum)
     lower, upper = shifted(sent, "gx")
     pack = call(hold_body, shape(24, LANES), [VMEM], flops=4_000_000)(pack)
-    ws, wst, hid, hidt, cols, nbt = call(
+    forms, backs, hid, hidt, cols, nbt = call(
         params_body,
         [
-            shape(256, LANES), shape(LANES, 256), shape(2, 2, 128, 128, dtype=BF16),
+            shape(2, 128, LANES, dtype=BF16), shape(2, 192, LANES, dtype=BF16), shape(2, 2, 128, 128, dtype=BF16),
             shape(2, 2, 128, 128, dtype=BF16), shape(128, 128), shape(slots, atoms, dtype=jnp.int32),
         ],
         [VMEM] * 6,
-        [pltpu.VMEM((16, HALF), F32), pltpu.VMEM((128, LANES), F32), pltpu.VMEM((256, LANES), F32), pltpu.VMEM((128, 128), F32)],
+        [pltpu.VMEM((16, HALF), F32), pltpu.VMEM((128, LANES), F32), pltpu.VMEM((256, LANES), F32), pltpu.VMEM((128, 128), F32), pltpu.VMEM((128, LANES), F32)],
         flops=20_000_000,
     )(poly_table, fit_in, fit_hidden, fit_bias, fit_out, neighbours)
-    ghost, sent = call(first_body, [tile, tile], [VMEM] * 3)(pack, lower, upper)
+    ghost, sent = call(first_body, [tile, tile], [VMEM] * 3)(pack, upper, lower)
     lower, upper = shifted(sent, "gy")
     near = call(
         functools.partial(near_body, slots), shape(16, slots, LANES), [VMEM] * 3, flops=20_000_000
@@ -528,20 +573,20 @@
             pltpu.VMEM((6, slots, LANES), F32),
             pltpu.VMEM((20 * 128, LANES), F32),
             pltpu.VMEM((20, 16, LANES), F32),
-            pltpu.VMEM((256, 5 * LANES), F32),
-            pltpu.VMEM((256, 5 * LANES), F32),
+            pltpu.VMEM((128, 5 * LANES), F32),
+            pltpu.VMEM((192, 5 * LANES), F32),
             pltpu.VMEM((20, 16, LANES), F32),
         ],
         flops=40_000_000,
-    )(pack, near, lower, upper, nbt, ws, wst, hid, hidt, cols)
+    )(pack, near, upper, lower, nbt, forms, backs, hid, hidt, cols)
     below, above = shifted(accum[2], "gy")
     shares = lax.all_to_all(share, ("gx", "gy"), 0, 0)
-    own, ghost = call(fold_body, [tile, tile], [VMEM] * 4, flops=1000000000)(accum, below, above, pack)
+    own, ghost = call(fold_body, [tile, tile], [VMEM] * 4, flops=1000000000)(accum, above, below, pack)
     below, above = shifted(ghost, "gx")
     return tuple(
         call(
             last_body, [shape(*coords.shape), shape(*cheb_cur.shape), shape(2, 4)], [VMEM] * 5
-        )(own, below, above, tail, shares)
+        )(own, above, below, tail, shares)
     )
 
 

time: 43.2 us -> 37.9 us (0.88)
  waiting for transfers between devices: 11 us -> 5.21 us
  starting transfers between devices: 14.5 us -> 16.8 us
  Pallas kernels: 14.1 us -> 12.2 us
    ppermute x8, waiting for transfers between devices: 10.5 us -> 2.24 us  [shifted(): return (lax.ppermute(x, axis, up), lax.ppermute(x, axis, down))]
    ppermute x8, starting transfers between devices: 10.3 us -> 14.3 us  [shifted(): return (lax.ppermute(x, axis, up), lax.ppermute(x, axis, down))]
    all_to_all x1, waiting for transfers between devices: 0.58 us -> 2.97 us  [local(): shares = lax.all_to_all(share, ('gx', 'gy'), 0, 0)]
    pallas_call x1, Pallas kernels: 9.71 us -> 7.89 us  [local(): call(functools.partial(pair_body, entries, slots), [shape(3, 16, LANES),...]
    all_to_all x1, starting transfers between devices: 4.19 us -> 2.49 us  [local(): shares = lax.all_to_all(share, ('gx', 'gy'), 0, 0)]
  transfers between devices with their start and end apart: 9 -> 9, of which waited for: 7 -> 4; matrix products, arithmetic and copies ran while one was open for 0% -> 0% of each run, Pallas kernels for 4% -> 5%
where the time goes in v3:
time: 37.9 us; the launch traced here: 37.6 us
  starting transfers between devices  16.8 us (44%)
  Pallas kernels  12.2 us (32%)
  waiting for transfers between devices  5.21 us (14%)
  local copies, waits for them, and re-layouts  2.58 us (7%)
  between operations  0.74 us (2%)
    ppermute x8, starting transfers between devices, shifted(): return (lax.ppermute(x, axis, up), lax.ppermute(x, axis, down))  14.3 us
    pallas_call x1, Pallas kernels, local(): call(functools.partial(pair_body, entries, slots), [shape(3, 16, LANES),...  7.89 us
    all_to_all x1, waiting for transfers between devices, local(): shares = lax.all_to_all(share, ('gx', 'gy'), 0, 0)  2.97 us
    unnamed x17, local copies, waits for them, and re-layouts  2.58 us
    all_to_all x1, starting transfers between devices, local(): shares = lax.all_to_all(share, ('gx', 'gy'), 0, 0)  2.49 us
    ppermute x8, waiting for transfers between devices, shifted(): return (lax.ppermute(x, axis, up), lax.ppermute(x, axis, down))  2.24 us
    pallas_call x1, Pallas kernels, local(): call(field_body, [shape(24, LANES), tile, shape(40, LANES)], [pl.BlockSpe...  1.61 us
    pallas_call x1, Pallas kernels, local(): call(functools.partial(near_body, slots), shape(16, slots, LANES), [VMEM]...  1.14 us
  transfers between devices with their start and end apart: 9, of which 4 were waited for; matrix products, arithmetic and copies ran while one was open for 0% of the time, Pallas kernels for 5%

profile of v3, /device:TPU:0, one launch (start us, length us, event | category | flops | bytes accessed | tf_op | source)
XLA Modules:
  0.0 37.6 jit_solution(14952530316422234636)
XLA Ops:
  0.6 0.0 copy-start.2
  0.6 1.6 %shard_map.148 = (f32[24,128]{1,0:T(8,128)}, f32[16,128]{1,0:T(8,128)}, f32[40,128]{1,0:T(8,128)}) custom-call(f32[3,1,1,128]{3,2,1,0:T(1,128)} %coords_hbm.1, s32[1,1,128]{2,1,0:T(1,128)} %types_hbm.1, f32[4,3,1,1,128]{4,3,2,1,0:T(1,128)} %cur_hbm.1, f32[4,3,1,1,128]{4,3,2,1,0:T(1,128)} %prev_hbm.1, s32[1,1,2,64]{3,2,1,0:T(2,128)} %send_x_hbm.1, ...), custom_call_target="tpu_custom_call" | custom-call | bytes 65536 | tf_op jit(solution)/shard_map/pallas_call | solution.py:540
  2.3 0.5 %collective-permute-start.1 = (f32[16,128]{1,0:T(8,128)}, f32[16,128]{1,0:T(8,128)S(1)}, u32[]{:S(2)}, u32[]{:S(2)}) collective-permute-start(f32[16,128]{1,0:T(8,128)} %get-tuple-element.19), channel_id=1, source_target_pairs={{0,4},{4,8},{8,12},{12,16},{16,20},{20,24},{24,28},{28,0},{1,5},{5... | collective-permute-start | bytes 24584 | tf_op jit(solution)/shard_map/ppermute | solution.py:527
  2.8 2.9 %collective-permute-start = (f32[16,128]{1,0:T(8,128)}, f32[16,128]{1,0:T(8,128)S(1)}, u32[]{:S(2)}, u32[]{:S(2)}) collective-permute-start(f32[16,128]{1,0:T(8,128)} %get-tuple-element.19), channel_id=1, source_target_pairs={{4,0},{8,4},{12,8},{16,12},{20,16},{24,20},{28,24},{0,28},{5,1},{9... | collective-permute-start | bytes 24584 | tf_op jit(solution)/shard_map/ppermute | solution.py:527
  5.7 0.0 copy-start.4
  5.7 0.7 %copy-done.4 = f32[24,128]{1,0:T(8,128)S(1)} copy-done((f32[24,128]{1,0:T(8,128)S(1)}, f32[24,128]{1,0:T(8,128)}, u32[]{:S(2)}) %copy-start.4) | copy-done | bytes 12312
  6.4 0.8 %collective-permute-done.1.lower_ref = f32[16,128]{1,0:T(8,128)S(1)} collective-permute-done((f32[16,128]{1,0:T(8,128)}, f32[16,128]{1,0:T(8,128)S(1)}, u32[]{:S(2)}, u32[]{:S(2)}) %collective-permute-start.1) | collective-permute-done | bytes 8224 | tf_op jit(solution)/shard_map/ppermute | solution.py:527
  7.2 0.1 collective-permute-done.upper_ref
  7.3 0.0 copy-start.7
  7.3 0.1 shard_map.150
  7.4 0.0 copy-start.5
  7.4 0.0 copy-start.6
  7.4 2.3 %collective-permute-start.3 = (f32[16,128]{1,0:T(8,128)S(1)}, f32[16,128]{1,0:T(8,128)S(1)}, u32[]{:S(2)}, u32[]{:S(2)}) collective-permute-start(f32[16,128]{1,0:T(8,128)S(1)} %get-tuple-element.22), channel_id=1, source_target_pairs={{0,1},{1,2},{2,3},{3,0},{4,5},{5,6},{6,7},{7,4},{8,9},{9,10},{10,1... | collective-permute-start | bytes 24584 | tf_op jit(solution)/shard_map/ppermute | solution.py:527
  9.6 2.1 %collective-permute-start.2 = (f32[16,128]{1,0:T(8,128)S(1)}, f32[16,128]{1,0:T(8,128)S(1)}, u32[]{:S(2)}, u32[]{:S(2)}) collective-permute-start(f32[16,128]{1,0:T(8,128)S(1)} %get-tuple-element.22), channel_id=1, source_target_pairs={{1,0},{2,1},{3,2},{0,3},{5,4},{6,5},{7,6},{4,7},{9,8},{10,9},{11,1... | collective-permute-start | bytes 24584 | tf_op jit(solution)/shard_map/ppermute | solution.py:527
  11.7 0.0 copy-done.7
  11.7 0.0 copy-done.2
  11.7 0.0 copy-done.5
  11.8 0.0 copy-done.6
  11.8 0.0 copy-start
  11.8 0.9 %copy-done = f32[512,128]{1,0:T(8,128)S(1)} copy-done((f32[512,128]{1,0:T(8,128)S(1)}, f32[512,128]{1,0:T(8,128)}, u32[]{:S(2)}) %copy-start) | copy-done | bytes 262168
  12.7 0.0 copy-start.1
  12.7 0.9 %copy-done.1 = f32[2,128,128]{2,1,0:T(8,128)S(1)} copy-done((f32[2,128,128]{2,1,0:T(8,128)S(1)}, f32[2,128,128]{2,1,0:T(8,128)}, u32[]{:S(2)}) %copy-start.1) | copy-done | bytes 131096
  13.6 0.6 %shard_map.151 = (bf16[2,128,128]{2,1,0:T(8,128)(2,1)S(1)}, bf16[2,192,128]{2,1,0:T(8,128)(2,1)S(1)}, bf16[2,2,128,128]{3,2,1,0:T(8,128)(2,1)S(1)}, bf16[2,2,128...) custom-call(f32[2,6,64]{2,1,0:T(8,128)S(1)} %copy.17.poly_ref, f32[512,128]{1,0:T(8,128)S(1)} %copy-done, ...), custom_call_target="tpu_custom_call" | custom-call | flops 20000000 | bytes 65536 | tf_op jit(solution)/shard_map/pallas_call | solution.py:550
  14.3 1.1 %shard_map.152.near_ref = f32[16,128,128]{2,1,0:T(8,128)S(1)} custom-call(f32[24,128]{1,0:T(8,128)S(1)} %shard_map.149.pack_ref, f32[16,128]{1,0:T(8,128)S(1)} %get-tuple-element.20.ghost_ref, s32[128,128]{1,0:T(8,128)S(1)} %get-tuple-element.21.nbt_ref), custom_call_target="tpu_custom_call" | custom-call | flops 20000000 | bytes 65536 | tf_op jit(solution)/shard_map/pallas_call | solution.py:562
  15.4 0.0 collective-permute-done.3.lower_ref
  15.4 0.0 collective-permute-done.2.upper_ref
  15.4 7.9 %shard_map.153 = (f32[3,16,128]{2,1,0:T(8,128)S(1)}, f32[32,128]{1,0:T(8,128)}) custom-call(f32[24,128]{1,0:T(8,128)S(1)} %shard_map.149.pack_ref, f32[16,128,128]{2,1,0:T(8,128)S(1)} %shard_map.152.near_ref, f32[16,128]{1,0:T(8,128)S(1)} %collective-permute-done.2.upper_ref, f32[16,128]{1,0:T(8,128)S(1)} %collective-permute-done.3.lower_ref, ...), custom_call_target="tpu_custom_call" | custom-call | flops 40000000 | bytes 65536 | tf_op jit(solution)/shard_map/pallas_call | solution.py:565
  23.3 0.0 collective-permute-start.5
  23.3 3.9 %collective-permute-start.4 = (f32[16,128]{1,0:T(8,128)S(1)}, f32[16,128]{1,0:T(8,128)S(1)}, u32[]{:S(2)}, u32[]{:S(2)}) collective-permute-start(f32[16,128]{1,0:T(8,128)S(1)} %slice_bitcast_fusion), channel_id=1, source_target_pairs={{1,0},{2,1},{3,2},{0,3},{5,4},{6,5},{7,6},{4,7},{9,8},{10,9},{11,1... | collective-permute-start | bytes 24584 | tf_op jit(solution)/shard_map/ppermute | solution.py:527
  27.2 2.5 %all-to-all-start = ((f32[32,1,128]{2,1,0:T(1,128)}), f32[32,1,128]{2,1,0:T(1,128)S(1)}, u32[]{:S(2)}, u32[]{:S(2)}) async-start(f32[32,1,128]{2,1,0:T(1,128)} %bitcast.2), calls=%async_computation | async-start | bytes 32768 | tf_op jit(solution)/shard_map/all_to_all | solution.py:583
  29.7 0.0 collective-permute-done.5.below_ref
  29.7 0.0 collective-permute-done.4.above_ref
  29.7 0.0 copy-start.3
  29.7 0.1 shard_map.154
  29.8 0.1 collective-permute-start.7
  30.0 2.5 %collective-permute-start.6 = (f32[16,128]{1,0:T(8,128)S(1)}, f32[16,128]{1,0:T(8,128)S(1)}, u32[]{:S(2)}, u32[]{:S(2)}) collective-permute-start(f32[16,128]{1,0:T(8,128)S(1)} %get-tuple-element.30), channel_id=1, source_target_pairs={{4,0},{8,4},{12,8},{16,12},{20,16},{24,20},{28,24},{0,28},{5,1},{9... | collective-permute-start | bytes 24584 | tf_op jit(solution)/shard_map/ppermute | solution.py:527
  32.5 1.3 %collective-permute-done.7.below_ref = f32[16,128]{1,0:T(8,128)S(1)} collective-permute-done((f32[16,128]{1,0:T(8,128)S(1)}, f32[16,128]{1,0:T(8,128)S(1)}, u32[]{:S(2)}, u32[]{:S(2)}) %collective-permute-start.7) | collective-permute-done | bytes 8224 | tf_op jit(solution)/shard_map/ppermute | solution.py:527
  33.8 0.0 collective-permute-done.6.above_ref
  33.9 3.0 %all-to-all-done = f32[32,1,128]{2,1,0:T(1,128)S(1)} async-done(((f32[32,1,128]{2,1,0:T(1,128)}), f32[32,1,128]{2,1,0:T(1,128)S(1)}, u32[]{:S(2)}, u32[]{:S(2)}) %all-to-all-start) | async-done | bytes 16416 | tf_op jit(solution)/shard_map/all_to_all | solution.py:583
  36.8 0.0 copy-done.3
  36.8 0.8 %shard_map.155 = (f32[3,1,1,128]{3,2,1,0:T(1,128)}, f32[4,3,1,1,128]{4,3,2,1,0:T(1,128)}, f32[2,4]{1,0:T(2,128)}) custom-call(f32[16,128]{1,0:T(8,128)S(1)} %get-tuple-element.29.own_ref, f32[16,128]{1,0:T(8,128)S(1)} %collective-permute-done.6.above_ref, f32[16,128]{1,0:T(8,128)S(1)} %collective-permute-done.7.below_ref, f32[40,128]{1,0:T(8,128)S(1)} %copy-done.3, ...), custom_call_target="tpu_custom_call" | custom-call | bytes 65536 | tf_op jit(solution)/shard_map/pallas_call | solution.py:587
  (3 shorter events, 0.0 us)
Async XLA Ops:
  0.6 11.1 %copy-start.2 = (s32[1,1,128,128]{3,2,1,0:T(8,128)S(1)}, s32[1,1,128,128]{3,2,1,0:T(8,128)}, u32[]{:S(2)}) copy-start(s32[1,1,128,128]{3,2,1,0:T(8,128)} %nb_ref.1) | copy-start | bytes 196612
  2.3 4.9 %collective-permute-start.1 = (f32[16,128]{1,0:T(8,128)}, f32[16,128]{1,0:T(8,128)S(1)}, u32[]{:S(2)}, u32[]{:S(2)}) collective-permute-start(f32[16,128]{1,0:T(8,128)} %get-tuple-element.19), channel_id=1, source_target_pairs={{0,4},{4,8},{8,12},{12,16},{16,20},{20,24},{24,28},{28,0},{1,5},{5... | collective-permute-start | bytes 24584 | tf_op jit(solution)/shard_map/ppermute | solution.py:527
  2.8 4.5 %collective-permute-start = (f32[16,128]{1,0:T(8,128)}, f32[16,128]{1,0:T(8,128)S(1)}, u32[]{:S(2)}, u32[]{:S(2)}) collective-permute-start(f32[16,128]{1,0:T(8,128)} %get-tuple-element.19), channel_id=1, source_target_pairs={{4,0},{8,4},{12,8},{16,12},{20,16},{24,20},{28,24},{0,28},{5,1},{9... | collective-permute-start | bytes 24584 | tf_op jit(solution)/shard_map/ppermute | solution.py:527
  5.7 0.7 %copy-start.4 = (f32[24,128]{1,0:T(8,128)S(1)}, f32[24,128]{1,0:T(8,128)}, u32[]{:S(2)}) copy-start(f32[24,128]{1,0:T(8,128)} %get-tuple-element.18.pack_ref) | copy-start | bytes 36868
  7.3 4.5 %copy-start.7 = (f32[2,6,64]{2,0,1:T(2,128)S(1)}, f32[2,6,64]{2,0,1:T(2,128)}, u32[]{:S(2)}) copy-start(f32[2,6,64]{2,0,1:T(2,128)} %param.18) | copy-start | bytes 9220
  7.4 4.4 %copy-start.5 = (f32[3,128]{1,0:T(4,128)S(1)}, f32[3,128]{1,0:T(4,128)}, u32[]{:S(2)}) copy-start(f32[3,128]{1,0:T(4,128)} %bias_ref.1) | copy-start | bytes 4612
  7.4 4.4 %copy-start.6 = (f32[128]{0:T(128)S(1)}, f32[128]{0:T(128)}, u32[]{:S(2)}) copy-start(f32[128]{0:T(128)} %out_ref.1) | copy-start | bytes 1540
  7.4 8.0 %collective-permute-start.3 = (f32[16,128]{1,0:T(8,128)S(1)}, f32[16,128]{1,0:T(8,128)S(1)}, u32[]{:S(2)}, u32[]{:S(2)}) collective-permute-start(f32[16,128]{1,0:T(8,128)S(1)} %get-tuple-element.22), channel_id=1, source_target_pairs={{0,1},{1,2},{2,3},{3,0},{4,5},{5,6},{6,7},{7,4},{8,9},{9,10},{10,1... | collective-permute-start | bytes 24584 | tf_op jit(solution)/shard_map/ppermute | solution.py:527
  9.6 5.8 %collective-permute-start.2 = (f32[16,128]{1,0:T(8,128)S(1)}, f32[16,128]{1,0:T(8,128)S(1)}, u32[]{:S(2)}, u32[]{:S(2)}) collective-permute-start(f32[16,128]{1,0:T(8,128)S(1)} %get-tuple-element.22), channel_id=1, source_target_pairs={{1,0},{2,1},{3,2},{0,3},{5,4},{6,5},{7,6},{4,7},{9,8},{10,9},{11,1... | collective-permute-start | bytes 24584 | tf_op jit(solution)/shard_map/ppermute | solution.py:527
  11.8 1.0 %copy-start = (f32[512,128]{1,0:T(8,128)S(1)}, f32[512,128]{1,0:T(8,128)}, u32[]{:S(2)}) copy-start(f32[512,128]{1,0:T(8,128)} %fit_ref.1) | copy-start | bytes 786436
  12.7 0.9 %copy-start.1 = (f32[2,128,128]{2,1,0:T(8,128)S(1)}, f32[2,128,128]{2,1,0:T(8,128)}, u32[]{:S(2)}) copy-start(f32[2,128,128]{2,1,0:T(8,128)} %hidden_ref.1) | copy-start | bytes 393220
  23.3 6.4 %collective-permute-start.5 = (f32[16,128]{1,0:T(8,128)S(1)}, f32[16,128]{1,0:T(8,128)S(1)}, u32[]{:S(2)}, u32[]{:S(2)}) collective-permute-start(f32[16,128]{1,0:T(8,128)S(1)} %slice_bitcast_fusion), channel_id=1, source_target_pairs={{0,1},{1,2},{2,3},{3,0},{4,5},{5,6},{6,7},{7,4},{8,9},{9,10},{10,1... | collective-permute-start | bytes 24584 | tf_op jit(solution)/shard_map/ppermute | solution.py:527
  23.3 6.4 %collective-permute-start.4 = (f32[16,128]{1,0:T(8,128)S(1)}, f32[16,128]{1,0:T(8,128)S(1)}, u32[]{:S(2)}, u32[]{:S(2)}) collective-permute-start(f32[16,128]{1,0:T(8,128)S(1)} %slice_bitcast_fusion), channel_id=1, source_target_pairs={{1,0},{2,1},{3,2},{0,3},{5,4},{6,5},{7,6},{4,7},{9,8},{10,9},{11,1... | collective-permute-start | bytes 24584 | tf_op jit(solution)/shard_map/ppermute | solution.py:527
  27.2 9.7 %all-to-all-start = ((f32[32,1,128]{2,1,0:T(1,128)}), f32[32,1,128]{2,1,0:T(1,128)S(1)}, u32[]{:S(2)}, u32[]{:S(2)}) async-start(f32[32,1,128]{2,1,0:T(1,128)} %bitcast.2), calls=%async_computation | async-start | bytes 32768 | tf_op jit(solution)/shard_map/all_to_all | solution.py:583
  29.7 7.2 %copy-start.3 = (f32[40,128]{1,0:T(8,128)S(1)}, f32[40,128]{1,0:T(8,128)}, u32[]{:S(2)}) copy-start(f32[40,128]{1,0:T(8,128)} %get-tuple-element.31.tail_ref) | copy-start | bytes 61444
  29.8 4.0 %collective-permute-start.7 = (f32[16,128]{1,0:T(8,128)S(1)}, f32[16,128]{1,0:T(8,128)S(1)}, u32[]{:S(2)}, u32[]{:S(2)}) collective-permute-start(f32[16,128]{1,0:T(8,128)S(1)} %get-tuple-element.30), channel_id=1, source_target_pairs={{0,4},{4,8},{8,12},{12,16},{16,20},{20,24},{24,28},{28,0},{1,5},{5... | collective-permute-start | bytes 24584 | tf_op jit(solution)/shard_map/ppermute | solution.py:527
  30.0 3.9 %collective-permute-start.6 = (f32[16,128]{1,0:T(8,128)S(1)}, f32[16,128]{1,0:T(8,128)S(1)}, u32[]{:S(2)}, u32[]{:S(2)}) collective-permute-start(f32[16,128]{1,0:T(8,128)S(1)} %get-tuple-element.30), channel_id=1, source_target_pairs={{4,0},{8,4},{12,8},{16,12},{20,16},{24,20},{28,24},{0,28},{5,1},{9... | collective-permute-start | bytes 24584 | tf_op jit(solution)/shard_map/ppermute | solution.py:527

commit v4 on v3

--- a/solution.py
+++ b/solution.py
@@ -99,8 +99,8 @@
 
 
 def params_body(
-    poly_ref, fit_ref, hidden_ref, bias_ref, out_ref, nb_ref,
-    form_ref, back_ref, hid_ref, hidt_ref, cols_ref, nbt_ref,
+    poly_ref, fit_ref, hidden_ref, bias_ref, out_ref, nb_ref, pack_ref,
+    held_ref, form_ref, back_ref, hid_ref, hidt_ref, cols_ref, nbt_ref,
     table, mixed, square, columns, even,
 ):
     table[...] = jnp.zeros_like(table)
@@ -140,6 +140,7 @@
     columns[3:4, :] = out_ref[...].reshape(1, LANES)
     cols_ref[...] = columns[...].T
     nbt_ref[...] = nb_ref[0, 0].T
+    held_ref[...] = pack_ref[...]
 
 
 def field_body(
@@ -192,10 +193,6 @@
     sent_ref[...] = take_columns([pack_ref[0:16, :]], lists_x)
 
 
-def hold_body(pack_ref, held_ref):
-    held_ref[...] = pack_ref[...]
-
-
 def first_body(pack_ref, upper_ref, lower_ref, ghost_ref, sent_ref):
     ghost = joined(lower_ref[...], upper_ref[...], 0)
     ghost_ref[...] = ghost
@@ -544,20 +541,20 @@
         [pltpu.VMEM(x.shape, x.dtype) for x in whole]
         + [pltpu.SMEM(spectrum.shape, F32), pltpu.SemaphoreType.DMA((7,))],
         limit=None,
+        flops=2_000_000_000,
     )(*whole, spectrum)
     lower, upper = shifted(sent, "gx")
-    pack = call(hold_body, shape(24, LANES), [VMEM], flops=4_000_000)(pack)
-    forms, backs, hid, hidt, cols, nbt = call(
+    pack, forms, backs, hid, hidt, cols, nbt = call(
         params_body,
         [
-            shape(2, 128, LANES, dtype=BF16), shape(2, 192, LANES, dtype=BF16), shape(2, 2, 128, 128, dtype=BF16),
+            shape(24, LANES), shape(2, 128, LANES, dtype=BF16), shape(2, 192, LANES, dtype=BF16), shape(2, 2, 128, 128, dtype=BF16),
             shape(2, 2, 128, 128, dtype=BF16), shape(128, 128), shape(slots, atoms, dtype=jnp.int32),
         ],
-        [VMEM] * 6,
+        [VMEM] * 7,
         [pltpu.VMEM((16, HALF), F32), pltpu.VMEM((128, LANES), F32), pltpu.VMEM((256, LANES), F32), pltpu.VMEM((128, 128), F32), pltpu.VMEM((128, LANES), F32)],
         flops=20_000_000,
-    )(poly_table, fit_in, fit_hidden, fit_bias, fit_out, neighbours)
-    ghost, sent = call(first_body, [tile, tile], [VMEM] * 3)(pack, upper, lower)
+    )(poly_table, fit_in, fit_hidden, fit_bias, fit_out, neighbours, pack)
+    ghost, sent = call(first_body, [tile, tile], [VMEM] * 3, flops=2_000_000_000)(pack, upper, lower)
     lower, upper = shifted(sent, "gy")
     near = call(
         functools.partial(near_body, slots), shape(16, slots, LANES), [VMEM] * 3, flops=20_000_000

time: 37.9 us -> 36.8 us (0.971)
  local copies, waits for them, and re-layouts: 2.58 us -> 0.64 us
  starting transfers between devices: 16.8 us -> 17.7 us
    unnamed x17, local copies, waits for them, and re-layouts: 2.58 us -> 0.64 us
    all_to_all x1, starting transfers between devices: 2.49 us -> 3.44 us  [local(): shares = lax.all_to_all(share, ('gx', 'gy'), 0, 0)]
  transfers between devices with their start and end apart: 9 -> 9, of which waited for: 4 -> 6; matrix products, arithmetic and copies ran while one was open for 0% -> 0% of each run, Pallas kernels for 5% -> 5%
where the time goes in v4:
time: 36.8 us; the launch traced here: 36.6 us
  starting transfers between devices  17.7 us (48%)
  Pallas kernels  12.2 us (33%)
  waiting for transfers between devices  5.22 us (14%)
  between operations  0.78 us (2%)
  local copies, waits for them, and re-layouts  0.64 us (2%)
    ppermute x8, starting transfers between devices, shifted(): return (lax.ppermute(x, axis, up), lax.ppermute(x, axis, down))  14.3 us
    pallas_call x1, Pallas kernels, local(): call(functools.partial(pair_body, entries, slots), [shape(3, 16, LANES),...  7.88 us
    all_to_all x1, starting transfers between devices, local(): shares = lax.all_to_all(share, ('gx', 'gy'), 0, 0)  3.44 us
    all_to_all x1, waiting for transfers between devices, local(): shares = lax.all_to_all(share, ('gx', 'gy'), 0, 0)  2.97 us
    ppermute x8, waiting for transfers between devices, shifted(): return (lax.ppermute(x, axis, up), lax.ppermute(x, axis, down))  2.25 us
    pallas_call x1, Pallas kernels, local(): call(field_body, [shape(24, LANES), tile, shape(40, LANES)], [pl.BlockSpe...  1.62 us
    pallas_call x1, Pallas kernels, local(): call(functools.partial(near_body, slots), shape(16, slots, LANES), [VMEM]...  1.13 us
    pallas_call x1, Pallas kernels, local(): call(last_body, [shape(*coords.shape), shape(*cheb_cur.shape), shape(2, 4...  0.76 us
  transfers between devices with their start and end apart: 9, of which 6 were waited for; matrix products, arithmetic and copies ran while one was open for 0% of the time, Pallas kernels for 5%

profile of v4, /device:TPU:0, one launch (start us, length us, event | category | flops | bytes accessed | tf_op | source)
XLA Modules:
  0.0 36.6 jit_solution(15243393607471529274)
XLA Ops:
  0.6 0.0 copy-start.1
  0.6 0.0 copy-start
  0.7 0.0 copy-start.7
  0.7 0.0 copy-start.2
  0.7 0.0 copy-start.5
  0.7 1.6 %shard_map.148 = (f32[24,128]{1,0:T(8,128)}, f32[16,128]{1,0:T(8,128)}, f32[40,128]{1,0:T(8,128)}) custom-call(f32[3,1,1,128]{3,2,1,0:T(1,128)} %coords_hbm.1, s32[1,1,128]{2,1,0:T(1,128)} %types_hbm.1, f32[4,3,1,1,128]{4,3,2,1,0:T(1,128)} %cur_hbm.1, f32[4,3,1,1,128]{4,3,2,1,0:T(1,128)} %prev_hbm.1, s32[1,1,2,64]{3,2,1,0:T(2,128)} %send_x_hbm.1, ...), custom_call_target="tpu_custom_call" | custom-call | flops 2000000000 | bytes 65536 | tf_op jit(solution)/shard_map/pallas_call | solution.py:537
  2.3 0.0 copy-start.4
  2.3 0.5 %collective-permute-start.1 = (f32[16,128]{1,0:T(8,128)}, f32[16,128]{1,0:T(8,128)S(1)}, u32[]{:S(2)}, u32[]{:S(2)}) collective-permute-start(f32[16,128]{1,0:T(8,128)} %get-tuple-element.21), channel_id=1, source_target_pairs={{0,4},{4,8},{8,12},{12,16},{16,20},{20,24},{24,28},{28,0},{1,5},{5... | collective-permute-start | bytes 24584 | tf_op jit(solution)/shard_map/ppermute | solution.py:524
  2.8 2.9 %collective-permute-start = (f32[16,128]{1,0:T(8,128)}, f32[16,128]{1,0:T(8,128)S(1)}, u32[]{:S(2)}, u32[]{:S(2)}) collective-permute-start(f32[16,128]{1,0:T(8,128)} %get-tuple-element.21), channel_id=1, source_target_pairs={{4,0},{8,4},{12,8},{16,12},{20,16},{24,20},{28,24},{0,28},{5,1},{9... | collective-permute-start | bytes 24584 | tf_op jit(solution)/shard_map/ppermute | solution.py:524
  5.8 0.0 copy-done.7
  5.8 0.0 copy-start.6
  5.8 0.0 copy-done.1
  5.8 0.0 copy-done
  5.8 0.0 copy-done.2
  5.8 0.0 copy-done.5
  5.8 0.0 copy-done.4
  5.8 0.6 %copy-done.6 = f32[128]{0:T(128)S(1)} copy-done((f32[128]{0:T(128)S(1)}, f32[128]{0:T(128)}, u32[]{:S(2)}) %copy-start.6) | copy-done | bytes 536
  6.4 0.6 %shard_map.149 = (f32[24,128]{1,0:T(8,128)S(1)}, bf16[2,128,128]{2,1,0:T(8,128)(2,1)S(1)}, bf16[2,192,128]{2,1,0:T(8,128)(2,1)S(1)}, bf16[2,2,128,128]{3,2,1,0:T...) custom-call(f32[2,6,64]{2,1,0:T(8,128)S(1)} %copy.17.poly_ref, ...), custom_call_target="tpu_custom_call" | custom-call | flops 20000000 | bytes 65536 | tf_op jit(solution)/shard_map/pallas_call | solution.py:547
  7.1 0.2 collective-permute-done.1.lower_ref
  7.3 0.1 collective-permute-done.upper_ref
  7.4 0.1 shard_map.150
  7.4 2.3 %collective-permute-start.3 = (f32[16,128]{1,0:T(8,128)S(1)}, f32[16,128]{1,0:T(8,128)S(1)}, u32[]{:S(2)}, u32[]{:S(2)}) collective-permute-start(f32[16,128]{1,0:T(8,128)S(1)} %get-tuple-element.24), channel_id=1, source_target_pairs={{0,1},{1,2},{2,3},{3,0},{4,5},{5,6},{6,7},{7,4},{8,9},{9,10},{10,1... | collective-permute-start | bytes 24584 | tf_op jit(solution)/shard_map/ppermute | solution.py:524
  9.7 2.1 %collective-permute-start.2 = (f32[16,128]{1,0:T(8,128)S(1)}, f32[16,128]{1,0:T(8,128)S(1)}, u32[]{:S(2)}, u32[]{:S(2)}) collective-permute-start(f32[16,128]{1,0:T(8,128)S(1)} %get-tuple-element.24), channel_id=1, source_target_pairs={{1,0},{2,1},{3,2},{0,3},{5,4},{6,5},{7,6},{4,7},{9,8},{10,9},{11,1... | collective-permute-start | bytes 24584 | tf_op jit(solution)/shard_map/ppermute | solution.py:524
  11.8 1.1 %shard_map.151.near_ref = f32[16,128,128]{2,1,0:T(8,128)S(1)} custom-call(f32[24,128]{1,0:T(8,128)S(1)} %get-tuple-element.20.pack_ref, f32[16,128]{1,0:T(8,128)S(1)} %get-tuple-element.22.ghost_ref, s32[128,128]{1,0:T(8,128)S(1)} %get-tuple-element.23.nbt_ref), custom_call_target="tpu_custom_call" | custom-call | flops 20000000 | bytes 65536 | tf_op jit(solution)/shard_map/pallas_call | solution.py:559
  12.9 0.5 %collective-permute-done.3.lower_ref = f32[16,128]{1,0:T(8,128)S(1)} collective-permute-done((f32[16,128]{1,0:T(8,128)S(1)}, f32[16,128]{1,0:T(8,128)S(1)}, u32[]{:S(2)}, u32[]{:S(2)}) %collective-permute-start.3) | collective-permute-done | bytes 8224 | tf_op jit(solution)/shard_map/ppermute | solution.py:524
  13.4 0.1 collective-permute-done.2.upper_ref
  13.5 7.9 %shard_map.152 = (f32[3,16,128]{2,1,0:T(8,128)S(1)}, f32[32,128]{1,0:T(8,128)}) custom-call(f32[24,128]{1,0:T(8,128)S(1)} %get-tuple-element.20.pack_ref, f32[16,128,128]{2,1,0:T(8,128)S(1)} %shard_map.151.near_ref, f32[16,128]{1,0:T(8,128)S(1)} %collective-permute-done.2.upper_ref, f32[16,128]{1,0:T(8,128)S(1)} %collective-permute-done.3.lower_ref, ...), custom_call_target="tpu_custom_call" | custom-call | flops 40000000 | bytes 65536 | tf_op jit(solution)/shard_map/pallas_call | solution.py:562
  21.4 1.4 %collective-permute-start.5 = (f32[16,128]{1,0:T(8,128)S(1)}, f32[16,128]{1,0:T(8,128)S(1)}, u32[]{:S(2)}, u32[]{:S(2)}) collective-permute-start(f32[16,128]{1,0:T(8,128)S(1)} %slice_bitcast_fusion), channel_id=1, source_target_pairs={{0,1},{1,2},{2,3},{3,0},{4,5},{5,6},{6,7},{7,4},{8,9},{9,10},{10,1... | collective-permute-start | bytes 24584 | tf_op jit(solution)/shard_map/ppermute | solution.py:524
  22.8 2.4 %collective-permute-start.4 = (f32[16,128]{1,0:T(8,128)S(1)}, f32[16,128]{1,0:T(8,128)S(1)}, u32[]{:S(2)}, u32[]{:S(2)}) collective-permute-start(f32[16,128]{1,0:T(8,128)S(1)} %slice_bitcast_fusion), channel_id=1, source_target_pairs={{1,0},{2,1},{3,2},{0,3},{5,4},{6,5},{7,6},{4,7},{9,8},{10,9},{11,1... | collective-permute-start | bytes 24584 | tf_op jit(solution)/shard_map/ppermute | solution.py:524
  25.2 3.4 %all-to-all-start = ((f32[32,1,128]{2,1,0:T(1,128)}), f32[32,1,128]{2,1,0:T(1,128)S(1)}, u32[]{:S(2)}, u32[]{:S(2)}) async-start(f32[32,1,128]{2,1,0:T(1,128)} %bitcast.2), calls=%async_computation | async-start | bytes 32768 | tf_op jit(solution)/shard_map/all_to_all | solution.py:580
  28.7 0.0 collective-permute-done.5.below_ref
  28.7 0.0 collective-permute-done.4.above_ref
  28.7 0.0 copy-start.3
  28.7 0.1 shard_map.153
  28.8 0.3 collective-permute-start.7
  29.1 2.4 %collective-permute-start.6 = (f32[16,128]{1,0:T(8,128)S(1)}, f32[16,128]{1,0:T(8,128)S(1)}, u32[]{:S(2)}, u32[]{:S(2)}) collective-permute-start(f32[16,128]{1,0:T(8,128)S(1)} %get-tuple-element.32), channel_id=1, source_target_pairs={{4,0},{8,4},{12,8},{16,12},{20,16},{24,20},{28,24},{0,28},{5,1},{9... | collective-permute-start | bytes 24584 | tf_op jit(solution)/shard_map/ppermute | solution.py:524
  31.5 1.3 %collective-permute-done.7.below_ref = f32[16,128]{1,0:T(8,128)S(1)} collective-permute-done((f32[16,128]{1,0:T(8,128)S(1)}, f32[16,128]{1,0:T(8,128)S(1)}, u32[]{:S(2)}, u32[]{:S(2)}) %collective-permute-start.7) | collective-permute-done | bytes 8224 | tf_op jit(solution)/shard_map/ppermute | solution.py:524
  32.8 0.0 collective-permute-done.6.above_ref
  32.9 3.0 %all-to-all-done = f32[32,1,128]{2,1,0:T(1,128)S(1)} async-done(((f32[32,1,128]{2,1,0:T(1,128)}), f32[32,1,128]{2,1,0:T(1,128)S(1)}, u32[]{:S(2)}, u32[]{:S(2)}) %all-to-all-start) | async-done | bytes 16416 | tf_op jit(solution)/shard_map/all_to_all | solution.py:580
  35.8 0.0 copy-done.3
  35.8 0.8 %shard_map.154 = (f32[3,1,1,128]{3,2,1,0:T(1,128)}, f32[4,3,1,1,128]{4,3,2,1,0:T(1,128)}, f32[2,4]{1,0:T(2,128)}) custom-call(f32[16,128]{1,0:T(8,128)S(1)} %get-tuple-element.31.own_ref, f32[16,128]{1,0:T(8,128)S(1)} %collective-permute-done.6.above_ref, f32[16,128]{1,0:T(8,128)S(1)} %collective-permute-done.7.below_ref, f32[40,128]{1,0:T(8,128)S(1)} %copy-done.3, ...), custom_call_target="tpu_custom_call" | custom-call | bytes 65536 | tf_op jit(solution)/shard_map/pallas_call | solution.py:584
  (2 shorter events, 0.0 us)
Async XLA Ops:
  0.6 5.1 %copy-start.1 = (f32[2,128,128]{2,1,0:T(8,128)S(1)}, f32[2,128,128]{2,1,0:T(8,128)}, u32[]{:S(2)}) copy-start(f32[2,128,128]{2,1,0:T(8,128)} %hidden_ref.1) | copy-start | bytes 393220
  0.6 5.1 %copy-start = (f32[512,128]{1,0:T(8,128)S(1)}, f32[512,128]{1,0:T(8,128)}, u32[]{:S(2)}) copy-start(f32[512,128]{1,0:T(8,128)} %fit_ref.1) | copy-start | bytes 786436
  0.7 5.1 %copy-start.7 = (f32[2,6,64]{2,0,1:T(2,128)S(1)}, f32[2,6,64]{2,0,1:T(2,128)}, u32[]{:S(2)}) copy-start(f32[2,6,64]{2,0,1:T(2,128)} %param.18) | copy-start | bytes 9220
  0.7 5.1 %copy-start.2 = (s32[1,1,128,128]{3,2,1,0:T(8,128)S(1)}, s32[1,1,128,128]{3,2,1,0:T(8,128)}, u32[]{:S(2)}) copy-start(s32[1,1,128,128]{3,2,1,0:T(8,128)} %nb_ref.1) | copy-start | bytes 196612
  0.7 5.1 %copy-start.5 = (f32[3,128]{1,0:T(4,128)S(1)}, f32[3,128]{1,0:T(4,128)}, u32[]{:S(2)}) copy-start(f32[3,128]{1,0:T(4,128)} %bias_ref.1) | copy-start | bytes 4612
  2.3 3.5 %copy-start.4 = (f32[24,128]{1,0:T(8,128)S(1)}, f32[24,128]{1,0:T(8,128)}, u32[]{:S(2)}) copy-start(f32[24,128]{1,0:T(8,128)} %get-tuple-element.19.pack_ref) | copy-start | bytes 36868
  2.3 4.9 %collective-permute-start.1 = (f32[16,128]{1,0:T(8,128)}, f32[16,128]{1,0:T(8,128)S(1)}, u32[]{:S(2)}, u32[]{:S(2)}) collective-permute-start(f32[16,128]{1,0:T(8,128)} %get-tuple-element.21), channel_id=1, source_target_pairs={{0,4},{4,8},{8,12},{12,16},{16,20},{20,24},{24,28},{28,0},{1,5},{5... | collective-permute-start | bytes 24584 | tf_op jit(solution)/shard_map/ppermute | solution.py:524
  2.8 4.5 %collective-permute-start = (f32[16,128]{1,0:T(8,128)}, f32[16,128]{1,0:T(8,128)S(1)}, u32[]{:S(2)}, u32[]{:S(2)}) collective-permute-start(f32[16,128]{1,0:T(8,128)} %get-tuple-element.21), channel_id=1, source_target_pairs={{4,0},{8,4},{12,8},{16,12},{20,16},{24,20},{28,24},{0,28},{5,1},{9... | collective-permute-start | bytes 24584 | tf_op jit(solution)/shard_map/ppermute | solution.py:524
  5.8 0.7 %copy-start.6 = (f32[128]{0:T(128)S(1)}, f32[128]{0:T(128)}, u32[]{:S(2)}) copy-start(f32[128]{0:T(128)} %out_ref.1) | copy-start | bytes 1540
  7.4 6.0 %collective-permute-start.3 = (f32[16,128]{1,0:T(8,128)S(1)}, f32[16,128]{1,0:T(8,128)S(1)}, u32[]{:S(2)}, u32[]{:S(2)}) collective-permute-start(f32[16,128]{1,0:T(8,128)S(1)} %get-tuple-element.24), channel_id=1, source_target_pairs={{0,1},{1,2},{2,3},{3,0},{4,5},{5,6},{6,7},{7,4},{8,9},{9,10},{10,1... | collective-permute-start | bytes 24584 | tf_op jit(solution)/shard_map/ppermute | solution.py:524
  9.7 3.8 %collective-permute-start.2 = (f32[16,128]{1,0:T(8,128)S(1)}, f32[16,128]{1,0:T(8,128)S(1)}, u32[]{:S(2)}, u32[]{:S(2)}) collective-permute-start(f32[16,128]{1,0:T(8,128)S(1)} %get-tuple-element.24), channel_id=1, source_target_pairs={{1,0},{2,1},{3,2},{0,3},{5,4},{6,5},{7,6},{4,7},{9,8},{10,9},{11,1... | collective-permute-start | bytes 24584 | tf_op jit(solution)/shard_map/ppermute | solution.py:524
  21.4 7.3 %collective-permute-start.5 = (f32[16,128]{1,0:T(8,128)S(1)}, f32[16,128]{1,0:T(8,128)S(1)}, u32[]{:S(2)}, u32[]{:S(2)}) collective-permute-start(f32[16,128]{1,0:T(8,128)S(1)} %slice_bitcast_fusion), channel_id=1, source_target_pairs={{0,1},{1,2},{2,3},{3,0},{4,5},{5,6},{6,7},{7,4},{8,9},{9,10},{10,1... | collective-permute-start | bytes 24584 | tf_op jit(solution)/shard_map/ppermute | solution.py:524
  22.8 5.8 %collective-permute-start.4 = (f32[16,128]{1,0:T(8,128)S(1)}, f32[16,128]{1,0:T(8,128)S(1)}, u32[]{:S(2)}, u32[]{:S(2)}) collective-permute-start(f32[16,128]{1,0:T(8,128)S(1)} %slice_bitcast_fusion), channel_id=1, source_target_pairs={{1,0},{2,1},{3,2},{0,3},{5,4},{6,5},{7,6},{4,7},{9,8},{10,9},{11,1... | collective-permute-start | bytes 24584 | tf_op jit(solution)/shard_map/ppermute | solution.py:524
  25.2 10.6 %all-to-all-start = ((f32[32,1,128]{2,1,0:T(1,128)}), f32[32,1,128]{2,1,0:T(1,128)S(1)}, u32[]{:S(2)}, u32[]{:S(2)}) async-start(f32[32,1,128]{2,1,0:T(1,128)} %bitcast.2), calls=%async_computation | async-start | bytes 32768 | tf_op jit(solution)/shard_map/all_to_all | solution.py:580
  28.7 7.2 %copy-start.3 = (f32[40,128]{1,0:T(8,128)S(1)}, f32[40,128]{1,0:T(8,128)}, u32[]{:S(2)}) copy-start(f32[40,128]{1,0:T(8,128)} %get-tuple-element.33.tail_ref) | copy-start | bytes 61444
  28.8 4.0 %collective-permute-start.7 = (f32[16,128]{1,0:T(8,128)S(1)}, f32[16,128]{1,0:T(8,128)S(1)}, u32[]{:S(2)}, u32[]{:S(2)}) collective-permute-start(f32[16,128]{1,0:T(8,128)S(1)} %get-tuple-element.32), channel_id=1, source_target_pairs={{0,4},{4,8},{8,12},{12,16},{16,20},{20,24},{24,28},{28,0},{1,5},{5... | collective-permute-start | bytes 24584 | tf_op jit(solution)/shard_map/ppermute | solution.py:524
  29.1 3.8 %collective-permute-start.6 = (f32[16,128]{1,0:T(8,128)S(1)}, f32[16,128]{1,0:T(8,128)S(1)}, u32[]{:S(2)}, u32[]{:S(2)}) collective-permute-start(f32[16,128]{1,0:T(8,128)S(1)} %get-tuple-element.32), channel_id=1, source_target_pairs={{4,0},{8,4},{12,8},{16,12},{20,16},{24,20},{28,24},{0,28},{5,1},{9... | collective-permute-start | bytes 24584 | tf_op jit(solution)/shard_map/ppermute | solution.py:524

commit v5 on v4

--- a/solution.py
+++ b/solution.py
@@ -25,12 +25,12 @@
     return jax.ShapeDtypeStruct(dims, dtype)
 
 
-def call(body, outs, specs, scratch=(), flops=0, limit=16 << 20):
+def call(body, outs, specs, scratch=(), flops=0, limit=16 << 20, places=None):
     return pl.pallas_call(
         body,
         out_shape=outs,
         in_specs=specs,
-        out_specs=jax.tree.map(lambda _: VMEM, outs),
+        out_specs=places or jax.tree.map(lambda _: VMEM, outs),
         scratch_shapes=list(scratch),
         compiler_params=pltpu.CompilerParams(vmem_limit_bytes=limit),
         cost_estimate=pl.CostEstimate(flops=flops, bytes_accessed=1 << 16, transcendentals=0),
@@ -219,11 +219,12 @@
     pack_ref, near_ref, upper_ref, lower_ref, nbt_ref,
     form_ref, back_ref, hid_ref, hidt_ref, cols_ref,
     accum_ref, share_ref,
-    terms_ref, far, pair, power, moment, gee, form, back, lam,
+    terms_ref, far, pair, power, moment, gee, form, back, lam, share_vmem, sem,
 ):
     groups = slots // SUBLANES
     far[...] = joined(lower_ref[...], upper_ref[...], 1)
-    moment[...] = jnp.zeros_like(moment)
+    for block in range(20):
+        moment[block * 128 + 96 : (block + 1) * 128, :] = jnp.zeros((32, LANES), F32)
 
     def gather(group, carry):
         at = pl.ds(pl.multiple_of(group * SUBLANES, SUBLANES), SUBLANES)
@@ -459,15 +460,18 @@
         total = jnp.sum(jnp.sum(quad[w], axis=0, keepdims=True), axis=1, keepdims=True)
         local = jnp.where(lanes == 4 + w, total, local)
     share = (pack_ref[17:18, :] + pack_ref[18:19, :] * local) * (1.0 / entries)
-    share_ref[...] = jnp.broadcast_to(share, share_ref.shape)
+    share_vmem[...] = jnp.broadcast_to(share, share_vmem.shape)
+    copy = pltpu.make_async_copy(share_vmem, share_ref, sem)
+    copy.start()
     total, own = scatter_columns(slots, terms_ref, nbt_ref)
     for c in range(3):
         part = total[c * 32 : c * 32 + 16] + total[c * 32 + 16 : c * 32 + 32]
         accum_ref[c] = part - own if c == 0 else part
+    copy.wait()
 
 
 def scatter_columns(slots, terms_ref, nbt_ref):
-    per = 128
+    per = 64
     places = lax.broadcasted_iota(jnp.int32, (LANES, LANES), 0)
 
     def body(group, carry):
@@ -500,8 +504,8 @@
 
 
 def last_body(
-    own_ref, above_ref, below_ref, tail_ref, shares_ref,
-    forces_ref, next_ref, moments_ref,
+    own_ref, above_ref, below_ref, tail_ref,
+    forces_ref, next_ref,
 ):
     values = jnp.where(lane_number(16) < HALF, above_ref[...], below_ref[...])
     own = own_ref[...] + add_columns(values, tail_ref[32:33, :].astype(jnp.int32), LANES)
@@ -512,6 +516,9 @@
         for b in range(3):
             row = 3 + 3 * w + b
             next_ref[w, b, 0] = own[row : row + 1]
+
+
+def moments_body(shares_ref, moments_ref):
     total = jnp.sum(shares_ref[...], axis=0, keepdims=True)
     moments_ref[0:1, :] = total[:, 0:4]
     moments_ref[1:2, :] = pltpu.roll(total, LANES - 4, 1)[:, 0:4]
@@ -573,18 +580,20 @@
             pltpu.VMEM((128, 5 * LANES), F32),
             pltpu.VMEM((192, 5 * LANES), F32),
             pltpu.VMEM((20, 16, LANES), F32),
+            pltpu.VMEM((devices, LANES), F32),
+            pltpu.SemaphoreType.DMA,
         ],
         flops=40_000_000,
+        places=[VMEM, pl.BlockSpec(memory_space=pl.ANY)],
     )(pack, near, upper, lower, nbt, forms, backs, hid, hidt, cols)
     below, above = shifted(accum[2], "gy")
     shares = lax.all_to_all(share, ("gx", "gy"), 0, 0)
     own, ghost = call(fold_body, [tile, tile], [VMEM] * 4, flops=1000000000)(accum, above, below, pack)
     below, above = shifted(ghost, "gx")
-    return tuple(
-        call(
-            last_body, [shape(*coords.shape), shape(*cheb_cur.shape), shape(2, 4)], [VMEM] * 5
-        )(own, above, below, tail, shares)
-    )
+    forces, following = call(
+        last_body, [shape(*coords.shape), shape(*cheb_cur.shape)], [VMEM] * 4, flops=200_000_000
+    )(own, above, below, tail)
+    return forces, following, call(moments_body, shape(2, 4), [VMEM])(shares)
 
 
 def solution(mesh):

time: 36.8 us -> 36.5 us (level)
  waiting for transfers between devices: 5.22 us -> 4.45 us
  Pallas kernels: 12.2 us -> 12.6 us
    all_to_all x1, waiting for transfers between devices: 2.97 us -> 2.2 us  [local(): shares = lax.all_to_all(share, ('gx', 'gy'), 0, 0)]
    pallas_call x1 -> x2, Pallas kernels: 0.76 us -> 1.39 us  [the longest x1 0.76 us: local(): call(last_body, [shape(*coords.shape), shape(*cheb_cur.shape)], [VMEM] *...]
  transfers between devices with their start and end apart: 9 -> 9, of which waited for: 6 -> 6; matrix products, arithmetic and copies ran while one was open for 0% -> 0% of each run, Pallas kernels for 5% -> 7%
where the time goes in v5:
time: 36.5 us; the launch traced here: 36.3 us
  starting transfers between devices  17.8 us (49%)
  Pallas kernels  12.6 us (35%)
  waiting for transfers between devices  4.45 us (12%)
  between operations  0.79 us (2%)
  local copies, waits for them, and re-layouts  0.64 us (2%)
    ppermute x8, starting transfers between devices, shifted(): return (lax.ppermute(x, axis, up), lax.ppermute(x, axis, down))  14.3 us
    pallas_call x1, Pallas kernels, local(): call(functools.partial(pair_body, entries, slots), [shape(3, 16, LANES),...  7.61 us
    all_to_all x1, starting transfers between devices, local(): shares = lax.all_to_all(share, ('gx', 'gy'), 0, 0)  3.44 us
    ppermute x8, waiting for transfers between devices, shifted(): return (lax.ppermute(x, axis, up), lax.ppermute(x, axis, down))  2.25 us
    all_to_all x1, waiting for transfers between devices, local(): shares = lax.all_to_all(share, ('gx', 'gy'), 0, 0)  2.2 us
    pallas_call x1, Pallas kernels, local(): call(field_body, [shape(24, LANES), tile, shape(40, LANES)], [pl.BlockSpe...  1.63 us
    pallas_call x1, Pallas kernels, local(): call(functools.partial(near_body, slots), shape(16, slots, LANES), [VMEM]...  1.13 us
    pallas_call x1, Pallas kernels, local(): call(last_body, [shape(*coords.shape), shape(*cheb_cur.shape)], [VMEM] *...  0.76 us
  transfers between devices with their start and end apart: 9, of which 6 were waited for; matrix products, arithmetic and copies ran while one was open for 0% of the time, Pallas kernels for 7%

profile of v5, /device:TPU:0, one launch (start us, length us, event | category | flops | bytes accessed | tf_op | source)
XLA Modules:
  0.0 36.3 jit_solution(11361107945568258367)
XLA Ops:
  0.6 0.0 copy-start.1
  0.6 0.0 copy-start
  0.7 0.0 copy-start.7
  0.7 0.0 copy-start.2
  0.7 0.0 copy-start.4
  0.7 1.6 %shard_map.148 = (f32[24,128]{1,0:T(8,128)}, f32[16,128]{1,0:T(8,128)}, f32[40,128]{1,0:T(8,128)}) custom-call(f32[3,1,1,128]{3,2,1,0:T(1,128)} %coords_hbm.1, s32[1,1,128]{2,1,0:T(1,128)} %types_hbm.1, f32[4,3,1,1,128]{4,3,2,1,0:T(1,128)} %cur_hbm.1, f32[4,3,1,1,128]{4,3,2,1,0:T(1,128)} %prev_hbm.1, s32[1,1,2,64]{3,2,1,0:T(2,128)} %send_x_hbm.1, ...), custom_call_target="tpu_custom_call" | custom-call | flops 2000000000 | bytes 65536 | tf_op jit(solution)/shard_map/pallas_call | solution.py:544
  2.3 0.0 copy-start.3
  2.3 0.5 %collective-permute-start.1 = (f32[16,128]{1,0:T(8,128)}, f32[16,128]{1,0:T(8,128)S(1)}, u32[]{:S(2)}, u32[]{:S(2)}) collective-permute-start(f32[16,128]{1,0:T(8,128)} %get-tuple-element.23), channel_id=1, source_target_pairs={{0,4},{4,8},{8,12},{12,16},{16,20},{20,24},{24,28},{28,0},{1,5},{5... | collective-permute-start | bytes 24584 | tf_op jit(solution)/shard_map/ppermute | solution.py:531
  2.8 2.9 %collective-permute-start = (f32[16,128]{1,0:T(8,128)}, f32[16,128]{1,0:T(8,128)S(1)}, u32[]{:S(2)}, u32[]{:S(2)}) collective-permute-start(f32[16,128]{1,0:T(8,128)} %get-tuple-element.23), channel_id=1, source_target_pairs={{4,0},{8,4},{12,8},{16,12},{20,16},{24,20},{28,24},{0,28},{5,1},{9... | collective-permute-start | bytes 24584 | tf_op jit(solution)/shard_map/ppermute | solution.py:531
  5.8 0.0 copy-done.7
  5.8 0.0 copy-start.5
  5.8 0.0 copy-done.1
  5.8 0.0 copy-done
  5.8 0.0 copy-done.2
  5.8 0.0 copy-done.4
  5.8 0.0 copy-done.3
  5.8 0.6 %copy-done.5 = f32[128]{0:T(128)S(1)} copy-done((f32[128]{0:T(128)S(1)}, f32[128]{0:T(128)}, u32[]{:S(2)}) %copy-start.5) | copy-done | bytes 536
  6.4 0.6 %shard_map.149 = (f32[24,128]{1,0:T(8,128)S(1)}, bf16[2,128,128]{2,1,0:T(8,128)(2,1)S(1)}, bf16[2,192,128]{2,1,0:T(8,128)(2,1)S(1)}, bf16[2,2,128,128]{3,2,1,0:T...) custom-call(f32[2,6,64]{2,1,0:T(8,128)S(1)} %copy.17.poly_ref, ...), custom_call_target="tpu_custom_call" | custom-call | flops 20000000 | bytes 65536 | tf_op jit(solution)/shard_map/pallas_call | solution.py:554
  7.1 0.2 collective-permute-done.1.lower_ref
  7.3 0.1 collective-permute-done.upper_ref
  7.4 0.1 shard_map.150
  7.4 2.3 %collective-permute-start.3 = (f32[16,128]{1,0:T(8,128)S(1)}, f32[16,128]{1,0:T(8,128)S(1)}, u32[]{:S(2)}, u32[]{:S(2)}) collective-permute-start(f32[16,128]{1,0:T(8,128)S(1)} %get-tuple-element.26), channel_id=1, source_target_pairs={{0,1},{1,2},{2,3},{3,0},{4,5},{5,6},{6,7},{7,4},{8,9},{9,10},{10,1... | collective-permute-start | bytes 24584 | tf_op jit(solution)/shard_map/ppermute | solution.py:531
  9.7 2.1 %collective-permute-start.2 = (f32[16,128]{1,0:T(8,128)S(1)}, f32[16,128]{1,0:T(8,128)S(1)}, u32[]{:S(2)}, u32[]{:S(2)}) collective-permute-start(f32[16,128]{1,0:T(8,128)S(1)} %get-tuple-element.26), channel_id=1, source_target_pairs={{1,0},{2,1},{3,2},{0,3},{5,4},{6,5},{7,6},{4,7},{9,8},{10,9},{11,1... | collective-permute-start | bytes 24584 | tf_op jit(solution)/shard_map/ppermute | solution.py:531
  11.8 1.1 %shard_map.151.near_ref = f32[16,128,128]{2,1,0:T(8,128)S(1)} custom-call(f32[24,128]{1,0:T(8,128)S(1)} %get-tuple-element.22.pack_ref, f32[16,128]{1,0:T(8,128)S(1)} %get-tuple-element.24.ghost_ref, s32[128,128]{1,0:T(8,128)S(1)} %get-tuple-element.25.nbt_ref), custom_call_target="tpu_custom_call" | custom-call | flops 20000000 | bytes 65536 | tf_op jit(solution)/shard_map/pallas_call | solution.py:566
  12.9 0.5 %collective-permute-done.3.lower_ref = f32[16,128]{1,0:T(8,128)S(1)} collective-permute-done((f32[16,128]{1,0:T(8,128)S(1)}, f32[16,128]{1,0:T(8,128)S(1)}, u32[]{:S(2)}, u32[]{:S(2)}) %collective-permute-start.3) | collective-permute-done | bytes 8224 | tf_op jit(solution)/shard_map/ppermute | solution.py:531
  13.4 0.1 collective-permute-done.2.upper_ref
  13.5 7.6 %shard_map.152 = (f32[3,16,128]{2,1,0:T(8,128)S(1)}, f32[32,128]{1,0:T(8,128)}) custom-call(f32[24,128]{1,0:T(8,128)S(1)} %get-tuple-element.22.pack_ref, f32[16,128,128]{2,1,0:T(8,128)S(1)} %shard_map.151.near_ref, f32[16,128]{1,0:T(8,128)S(1)} %collective-permute-done.2.upper_ref, f32[16,128]{1,0:T(8,128)S(1)} %collective-permute-done.3.lower_ref, ...), custom_call_target="tpu_custom_call" | custom-call | flops 40000000 | bytes 65536 | tf_op jit(solution)/shard_map/pallas_call | solution.py:569
  21.2 1.5 %collective-permute-start.5 = (f32[16,128]{1,0:T(8,128)S(1)}, f32[16,128]{1,0:T(8,128)S(1)}, u32[]{:S(2)}, u32[]{:S(2)}) collective-permute-start(f32[16,128]{1,0:T(8,128)S(1)} %slice_bitcast_fusion), channel_id=1, source_target_pairs={{0,1},{1,2},{2,3},{3,0},{4,5},{5,6},{6,7},{7,4},{8,9},{9,10},{10,1... | collective-permute-start | bytes 24584 | tf_op jit(solution)/shard_map/ppermute | solution.py:531
  22.7 2.4 %collective-permute-start.4 = (f32[16,128]{1,0:T(8,128)S(1)}, f32[16,128]{1,0:T(8,128)S(1)}, u32[]{:S(2)}, u32[]{:S(2)}) collective-permute-start(f32[16,128]{1,0:T(8,128)S(1)} %slice_bitcast_fusion), channel_id=1, source_target_pairs={{1,0},{2,1},{3,2},{0,3},{5,4},{6,5},{7,6},{4,7},{9,8},{10,9},{11,1... | collective-permute-start | bytes 24584 | tf_op jit(solution)/shard_map/ppermute | solution.py:531
  25.0 3.4 %all-to-all-start = ((f32[32,1,128]{2,1,0:T(1,128)}), f32[32,1,128]{2,1,0:T(1,128)S(1)}, u32[]{:S(2)}, u32[]{:S(2)}) async-start(f32[32,1,128]{2,1,0:T(1,128)} %bitcast.2), calls=%async_computation | async-start | bytes 32768 | tf_op jit(solution)/shard_map/all_to_all | solution.py:590
  28.5 0.0 copy-start.6
  28.5 0.0 collective-permute-done.5.below_ref
  28.5 0.0 collective-permute-done.4.above_ref
  28.5 0.1 shard_map.153
  28.6 0.3 collective-permute-start.7
  28.9 2.4 %collective-permute-start.6 = (f32[16,128]{1,0:T(8,128)S(1)}, f32[16,128]{1,0:T(8,128)S(1)}, u32[]{:S(2)}, u32[]{:S(2)}) collective-permute-start(f32[16,128]{1,0:T(8,128)S(1)} %get-tuple-element.34), channel_id=1, source_target_pairs={{4,0},{8,4},{12,8},{16,12},{20,16},{24,20},{28,24},{0,28},{5,1},{9... | collective-permute-start | bytes 24584 | tf_op jit(solution)/shard_map/ppermute | solution.py:531
  31.3 1.3 %collective-permute-done.7.below_ref = f32[16,128]{1,0:T(8,128)S(1)} collective-permute-done((f32[16,128]{1,0:T(8,128)S(1)}, f32[16,128]{1,0:T(8,128)S(1)}, u32[]{:S(2)}, u32[]{:S(2)}) %collective-permute-start.7) | collective-permute-done | bytes 8224 | tf_op jit(solution)/shard_map/ppermute | solution.py:531
  32.6 0.0 collective-permute-done.6.above_ref
  32.7 0.0 copy-done.6
  32.7 0.8 %shard_map.154 = (f32[3,1,1,128]{3,2,1,0:T(1,128)}, f32[4,3,1,1,128]{4,3,2,1,0:T(1,128)}) custom-call(f32[16,128]{1,0:T(8,128)S(1)} %get-tuple-element.33.own_ref, f32[16,128]{1,0:T(8,128)S(1)} %collective-permute-done.6.above_ref, f32[16,128]{1,0:T(8,128)S(1)} %collective-permute-done.7.below_ref, f32[40,128]{1,0:T(8,128)S(1)} %copy-done.6), custom_call_target="tpu_custom_call" | custom-call | flops 200000000 | bytes 65536 | tf_op jit(solution)/shard_map/pallas_call | solution.py:593
  33.4 2.2 %all-to-all-done = f32[32,1,128]{2,1,0:T(1,128)S(1)} async-done(((f32[32,1,128]{2,1,0:T(1,128)}), f32[32,1,128]{2,1,0:T(1,128)S(1)}, u32[]{:S(2)}, u32[]{:S(2)}) %all-to-all-start) | async-done | bytes 16416 | tf_op jit(solution)/shard_map/all_to_all | solution.py:590
  35.6 0.6 %shard_map.155 = f32[2,4]{1,0:T(2,128)} custom-call(f32[32,128]{1,0:T(8,128)S(1)} %bitcast.6), custom_call_target="tpu_custom_call" | custom-call | bytes 65536 | tf_op jit(solution)/shard_map/pallas_call | solution.py:596
  (2 shorter events, 0.0 us)
Async XLA Ops:
  0.6 5.2 %copy-start.1 = (f32[2,128,128]{2,1,0:T(8,128)S(1)}, f32[2,128,128]{2,1,0:T(8,128)}, u32[]{:S(2)}) copy-start(f32[2,128,128]{2,1,0:T(8,128)} %hidden_ref.1) | copy-start | bytes 393220
  0.6 5.2 %copy-start = (f32[512,128]{1,0:T(8,128)S(1)}, f32[512,128]{1,0:T(8,128)}, u32[]{:S(2)}) copy-start(f32[512,128]{1,0:T(8,128)} %fit_ref.1) | copy-start | bytes 786436
  0.7 5.1 %copy-start.7 = (f32[2,6,64]{2,0,1:T(2,128)S(1)}, f32[2,6,64]{2,0,1:T(2,128)}, u32[]{:S(2)}) copy-start(f32[2,6,64]{2,0,1:T(2,128)} %param.18) | copy-start | bytes 9220
  0.7 5.1 %copy-start.2 = (s32[1,1,128,128]{3,2,1,0:T(8,128)S(1)}, s32[1,1,128,128]{3,2,1,0:T(8,128)}, u32[]{:S(2)}) copy-start(s32[1,1,128,128]{3,2,1,0:T(8,128)} %nb_ref.1) | copy-start | bytes 196612
  0.7 5.1 %copy-start.4 = (f32[3,128]{1,0:T(4,128)S(1)}, f32[3,128]{1,0:T(4,128)}, u32[]{:S(2)}) copy-start(f32[3,128]{1,0:T(4,128)} %bias_ref.1) | copy-start | bytes 4612
  2.3 3.5 %copy-start.3 = (f32[24,128]{1,0:T(8,128)S(1)}, f32[24,128]{1,0:T(8,128)}, u32[]{:S(2)}) copy-start(f32[24,128]{1,0:T(8,128)} %get-tuple-element.21.pack_ref) | copy-start | bytes 36868
  2.3 4.9 %collective-permute-start.1 = (f32[16,128]{1,0:T(8,128)}, f32[16,128]{1,0:T(8,128)S(1)}, u32[]{:S(2)}, u32[]{:S(2)}) collective-permute-start(f32[16,128]{1,0:T(8,128)} %get-tuple-element.23), channel_id=1, source_target_pairs={{0,4},{4,8},{8,12},{12,16},{16,20},{20,24},{24,28},{28,0},{1,5},{5... | collective-permute-start | bytes 24584 | tf_op jit(solution)/shard_map/ppermute | solution.py:531
  2.8 4.5 %collective-permute-start = (f32[16,128]{1,0:T(8,128)}, f32[16,128]{1,0:T(8,128)S(1)}, u32[]{:S(2)}, u32[]{:S(2)}) collective-permute-start(f32[16,128]{1,0:T(8,128)} %get-tuple-element.23), channel_id=1, source_target_pairs={{4,0},{8,4},{12,8},{16,12},{20,16},{24,20},{28,24},{0,28},{5,1},{9... | collective-permute-start | bytes 24584 | tf_op jit(solution)/shard_map/ppermute | solution.py:531
  5.8 0.7 %copy-start.5 = (f32[128]{0:T(128)S(1)}, f32[128]{0:T(128)}, u32[]{:S(2)}) copy-start(f32[128]{0:T(128)} %out_ref.1) | copy-start | bytes 1540
  7.4 6.0 %collective-permute-start.3 = (f32[16,128]{1,0:T(8,128)S(1)}, f32[16,128]{1,0:T(8,128)S(1)}, u32[]{:S(2)}, u32[]{:S(2)}) collective-permute-start(f32[16,128]{1,0:T(8,128)S(1)} %get-tuple-element.26), channel_id=1, source_target_pairs={{0,1},{1,2},{2,3},{3,0},{4,5},{5,6},{6,7},{7,4},{8,9},{9,10},{10,1... | collective-permute-start | bytes 24584 | tf_op jit(solution)/shard_map/ppermute | solution.py:531
  9.7 3.8 %collective-permute-start.2 = (f32[16,128]{1,0:T(8,128)S(1)}, f32[16,128]{1,0:T(8,128)S(1)}, u32[]{:S(2)}, u32[]{:S(2)}) collective-permute-start(f32[16,128]{1,0:T(8,128)S(1)} %get-tuple-element.26), channel_id=1, source_target_pairs={{1,0},{2,1},{3,2},{0,3},{5,4},{6,5},{7,6},{4,7},{9,8},{10,9},{11,1... | collective-permute-start | bytes 24584 | tf_op jit(solution)/shard_map/ppermute | solution.py:531
  21.2 7.3 %collective-permute-start.5 = (f32[16,128]{1,0:T(8,128)S(1)}, f32[16,128]{1,0:T(8,128)S(1)}, u32[]{:S(2)}, u32[]{:S(2)}) collective-permute-start(f32[16,128]{1,0:T(8,128)S(1)} %slice_bitcast_fusion), channel_id=1, source_target_pairs={{0,1},{1,2},{2,3},{3,0},{4,5},{5,6},{6,7},{7,4},{8,9},{9,10},{10,1... | collective-permute-start | bytes 24584 | tf_op jit(solution)/shard_map/ppermute | solution.py:531
  22.7 5.8 %collective-permute-start.4 = (f32[16,128]{1,0:T(8,128)S(1)}, f32[16,128]{1,0:T(8,128)S(1)}, u32[]{:S(2)}, u32[]{:S(2)}) collective-permute-start(f32[16,128]{1,0:T(8,128)S(1)} %slice_bitcast_fusion), channel_id=1, source_target_pairs={{1,0},{2,1},{3,2},{0,3},{5,4},{6,5},{7,6},{4,7},{9,8},{10,9},{11,1... | collective-permute-start | bytes 24584 | tf_op jit(solution)/shard_map/ppermute | solution.py:531
  25.0 10.6 %all-to-all-start = ((f32[32,1,128]{2,1,0:T(1,128)}), f32[32,1,128]{2,1,0:T(1,128)S(1)}, u32[]{:S(2)}, u32[]{:S(2)}) async-start(f32[32,1,128]{2,1,0:T(1,128)} %bitcast.2), calls=%async_computation | async-start | bytes 32768 | tf_op jit(solution)/shard_map/all_to_all | solution.py:590
  28.5 4.2 %copy-start.6 = (f32[40,128]{1,0:T(8,128)S(1)}, f32[40,128]{1,0:T(8,128)}, u32[]{:S(2)}) copy-start(f32[40,128]{1,0:T(8,128)} %get-tuple-element.35.tail_ref) | copy-start | bytes 61444
  28.6 4.0 %collective-permute-start.7 = (f32[16,128]{1,0:T(8,128)S(1)}, f32[16,128]{1,0:T(8,128)S(1)}, u32[]{:S(2)}, u32[]{:S(2)}) collective-permute-start(f32[16,128]{1,0:T(8,128)S(1)} %get-tuple-element.34), channel_id=1, source_target_pairs={{0,4},{4,8},{8,12},{12,16},{16,20},{20,24},{24,28},{28,0},{1,5},{5... | collective-permute-start | bytes 24584 | tf_op jit(solution)/shard_map/ppermute | solution.py:531
  28.9 3.8 %collective-permute-start.6 = (f32[16,128]{1,0:T(8,128)S(1)}, f32[16,128]{1,0:T(8,128)S(1)}, u32[]{:S(2)}, u32[]{:S(2)}) collective-permute-start(f32[16,128]{1,0:T(8,128)S(1)} %get-tuple-element.34), channel_id=1, source_target_pairs={{4,0},{8,4},{12,8},{16,12},{20,16},{24,20},{28,24},{0,28},{5,1},{9... | collective-permute-start | bytes 24584 | tf_op jit(solution)/shard_map/ppermute | solution.py:531
